TPU v7x, 32 devices: a whole 2x2x4 slice. The times are simulated.
32 devices in a mesh: dp: 4 (over y, x), fsdp: 8 (over z, core).
Axes of the slice: x: 2, y: 2, z: 4, core: 2. Of those that a mesh axis runs over, the one named last changes fastest.
Arguments:
- frames: bfloat16 [8192, 1024], P(('dp', 'fsdp')), may hold values from -6 to 6
- lengths: int32 [32, 4], P(('dp', 'fsdp')), may hold values from 1 to 160, 256 in all within a row
- languages: int32 [32, 4], P(('dp', 'fsdp')), may hold values from 0 to 101
- embedding: bfloat16 [102, 1024], P(None, 'fsdp'), may hold values from -3 to 3
- gains: bfloat16 [6, 1024], P(None, 'fsdp'), may hold values from 0.25 to 1.75
- shifts: bfloat16 [6, 1024], P(None, 'fsdp'), may hold values from -2 to 2
- firstup: bfloat16 [1024, 4096], P('fsdp'), may hold values from -0.1875 to 0.1875
- firstdown: bfloat16 [1024, 4096], P('fsdp'), may hold values from -0.09375 to 0.09375
- projection: bfloat16 [1024, 3072], P('fsdp'), may hold values from -0.1875 to 0.1875
- merger: bfloat16 [1024, 1024], P('fsdp'), may hold values from -0.5 to 0.5
- gating: bfloat16 [1024, 2048], P('fsdp'), may hold values from -0.1875 to 0.1875
- kernel: bfloat16 [5, 1024], P(None, 'fsdp'), may hold values from -2.5 to 2.5
- pointwise: bfloat16 [1024, 1024], P('fsdp'), may hold values from -0.1875 to 0.1875
- secondup: bfloat16 [1024, 4096], P('fsdp'), may hold values from -0.1875 to 0.1875
- seconddown: bfloat16 [1024, 4096], P('fsdp'), may hold values from -0.09375 to 0.09375
- cotangent: bfloat16 [8192, 1024], P(('dp', 'fsdp')), may hold values from -6 to 6
Outputs:
- encoded: bfloat16 [8192, 1024], P(('dp', 'fsdp'))
- frames_grad: float32 [8192, 1024], P(('dp', 'fsdp'))
- embedding_grad: float32 [102, 1024], P(None, 'fsdp')
- gains_grad: float32 [6, 1024], P(None, 'fsdp')
- shifts_grad: float32 [6, 1024], P(None, 'fsdp')
- firstup_grad: float32 [1024, 4096], P('fsdp')
- firstdown_grad: float32 [1024, 4096], P('fsdp')
- projection_grad: float32 [1024, 3072], P('fsdp')
- merger_grad: float32 [1024, 1024], P('fsdp')
- gating_grad: float32 [1024, 2048], P('fsdp')
- kernel_grad: float32 [5, 1024], P(None, 'fsdp')
- pointwise_grad: float32 [1024, 1024], P('fsdp')
- secondup_grad: float32 [1024, 4096], P('fsdp')
- seconddown_grad: float32 [1024, 4096], P('fsdp')
Inputs may be any that keep to these rules, and one draw needn't show every extreme that they name: Each row of lengths sums to 256 and has exactly 160 as its largest entry.
All inputs are finite; a program needn't handle non-finite values.
Results may differ from a plain program's by a relative error of at most 0.019.
Values may be sent and summed in bfloat16 or wider, within the bound.
No kernel may reach another device: no remote copies, remote signals or barrier semaphores. Data moves between devices by JAX's collectives and lax.ppermute only.
A program may use at most 256 MiB of HBM per device.

v0:
```python
import jax
import jax.numpy as jnp
from jax import lax
from jax.sharding import PartitionSpec as P

HEAD_DIM = 128


norm_epsilon = 1e-05
masked_score = -1000000000.0


def norm_rows(values, gain_row, shift_row):
    centred = values - jnp.mean(values, axis=-1, keepdims=True)
    spread = jnp.mean(centred * centred, axis=-1, keepdims=True)
    return centred * lax.rsqrt(spread + norm_epsilon) * gain_row + shift_row


def rotate(values, cosine, sine):
    half_dim = values.shape[-1] // 2
    first_half = values[..., :half_dim]
    second_half = values[..., half_dim:]
    return jnp.concatenate(
        [first_half * cosine - second_half * sine, second_half * cosine + first_half * sine],
        axis=-1,
    )


def depthwise_time(values, kernel, segment):
    half_kernel = kernel.shape[0] // 2
    length = values.shape[-2]
    padded = jnp.pad(values, ((half_kernel, half_kernel), (0, 0)))
    segment_pad = jnp.pad(segment, (half_kernel, half_kernel), constant_values=-1)
    summed = jnp.zeros_like(values)
    for tap_index in range(kernel.shape[0]):
        keeping = (segment_pad[tap_index : tap_index + length] == segment)[:, None]
        summed = (
            summed
            + jnp.where(keeping, padded[tap_index : tap_index + length, :], 0.0) * kernel[tap_index]
        )
    return summed


def layout(lengths, languages, frame_count):
    finish = jnp.cumsum(lengths, axis=-1)
    begins = finish - lengths
    indices = jnp.arange(frame_count, dtype=jnp.int32)
    segment = jnp.sum((indices[None, :, None] >= finish[:, None, :]).astype(jnp.int32), axis=-1)
    owners = segment[:, :, None] == jnp.arange(lengths.shape[-1], dtype=jnp.int32)[None, None, :]
    first_row = jnp.sum(jnp.where(owners, begins[:, None, :], 0), axis=-1)
    language_row = jnp.sum(jnp.where(owners, languages[:, None, :], 0), axis=-1)
    return (segment, indices[None, :] - first_row, language_row)


def angles(position):
    half_dim = HEAD_DIM // 2
    frequency = 10000.0 ** (-jnp.arange(half_dim, dtype=jnp.float32) / half_dim)
    turned = position.astype(jnp.float32)[..., None] * frequency
    return (jnp.cos(turned)[..., None, :], jnp.sin(turned)[..., None, :])


def times_transposed(left_side, right_side):
    return lax.dot_general(
        left_side, right_side, (((1,), (1,)), ((), ())), preferred_element_type=jnp.float32
    )


def project_rows(inputs, weight):
    return jnp.dot(
        inputs,
        lax.all_gather(weight, "fsdp", axis=0, tiled=True),
        preferred_element_type=jnp.float32,
    )


def project_cols(inputs, weight):
    return times_transposed(inputs, lax.all_gather(weight, "fsdp", axis=0, tiled=True))


def weight_grad(left_side, right_side):
    pieces = lax.psum_scatter(
        lax.dot_general(
            left_side, right_side, (((0,), (0,)), ((), ())), preferred_element_type=jnp.float32
        ).astype(jnp.bfloat16),
        "fsdp",
        scatter_dimension=0,
        tiled=True,
    )
    return lax.psum(pieces, "dp").astype(jnp.float32)


def feed_forward(values, gain_row, shift_row, upward, downward):
    normed, norm_pull = jax.vjp(norm_rows, values, gain_row, shift_row)
    hidden = normed.astype(jnp.bfloat16)
    expanded = project_rows(hidden, upward)
    activated, silu_pull = jax.vjp(jax.nn.silu, expanded)
    active_low = activated.astype(jnp.bfloat16)
    return (project_cols(active_low, downward), (norm_pull, hidden, silu_pull, active_low))


def feed_backward(gradient, stored, upward, downward):
    norm_pull, hidden, silu_pull, active_low = stored
    grad_low = gradient.astype(jnp.bfloat16)
    active_grad = project_rows(grad_low, downward)
    expand_grad = silu_pull(active_grad)[0].astype(jnp.bfloat16)
    hidden_grad = project_cols(expand_grad, upward)
    values_grad, gain_grad, shift_grad = norm_pull(hidden_grad)
    return (
        values_grad,
        gain_grad,
        shift_grad,
        weight_grad(hidden, expand_grad),
        weight_grad(grad_low, active_low),
    )


def attention_forward(values, gain_row, shift_row, projection, merger, matching, cosine, sine):
    normed, norm_pull = jax.vjp(norm_rows, values, gain_row, shift_row)
    hidden = normed.astype(jnp.bfloat16)
    projected = project_rows(hidden, projection)
    frame_count = projected.shape[0]
    head_count = projected.shape[1] // (3 * HEAD_DIM)
    shaped = projected.reshape(frame_count, 3, head_count, HEAD_DIM)

    def turning(query_raw, key_raw):
        return (rotate(query_raw, cosine, sine) * HEAD_DIM ** (-0.5), rotate(key_raw, cosine, sine))

    (query_rot, key_rot), turn_pull = jax.vjp(turning, shaped[:, 0], shaped[:, 1])
    query_low = query_rot.astype(jnp.bfloat16)
    key_low = key_rot.astype(jnp.bfloat16)
    value_low = shaped[:, 2].astype(jnp.bfloat16)
    scores = jnp.where(
        matching,
        jnp.einsum("qhd,khd->hqk", query_low, key_low, preferred_element_type=jnp.float32),
        masked_score,
    )
    highest_score = jnp.max(scores, axis=-1, keepdims=True)
    log_total = highest_score + jnp.log(
        jnp.sum(jnp.exp(scores - highest_score), axis=-1, keepdims=True)
    )
    probs_low = jnp.exp(scores - log_total).astype(jnp.bfloat16)
    mixed = jnp.einsum("hqk,khd->qhd", probs_low, value_low, preferred_element_type=jnp.float32)
    mixed_low = mixed.reshape(frame_count, head_count * HEAD_DIM).astype(jnp.bfloat16)
    return (
        project_rows(mixed_low, merger),
        (norm_pull, hidden, turn_pull, query_low, key_low, value_low, log_total, mixed_low),
    )


def attention_backward(gradient, stored, projection, merger, matching):
    norm_pull, hidden, turn_pull, query_low, key_low, value_low, log_total, mixed_low = stored
    frame_count, head_count = (query_low.shape[0], query_low.shape[1])
    grad_low = gradient.astype(jnp.bfloat16)
    mixed_grad = (
        project_cols(grad_low, merger)
        .astype(jnp.bfloat16)
        .reshape(frame_count, head_count, HEAD_DIM)
    )
    scores = jnp.where(
        matching,
        jnp.einsum("qhd,khd->hqk", query_low, key_low, preferred_element_type=jnp.float32),
        masked_score,
    )
    probs = jnp.exp(scores - log_total)
    value_grad = jnp.einsum(
        "hqk,qhd->khd", probs.astype(jnp.bfloat16), mixed_grad, preferred_element_type=jnp.float32
    )
    probs_grad = jnp.einsum(
        "qhd,khd->hqk", mixed_grad, value_low, preferred_element_type=jnp.float32
    )
    score_grad = (
        probs * (probs_grad - jnp.sum(probs * probs_grad, axis=-1, keepdims=True))
    ).astype(jnp.bfloat16)
    query_grad = jnp.einsum("hqk,khd->qhd", score_grad, key_low, preferred_element_type=jnp.float32)
    key_grad = jnp.einsum("hqk,qhd->khd", score_grad, query_low, preferred_element_type=jnp.float32)
    query_raw_grad, key_raw_grad = turn_pull((query_grad, key_grad))
    stacked = jnp.stack([query_raw_grad, key_raw_grad, value_grad], axis=1)
    projected_grad = stacked.reshape(frame_count, 3 * head_count * HEAD_DIM).astype(jnp.bfloat16)
    hidden_grad = project_cols(projected_grad, projection)
    values_grad, gain_grad, shift_grad = norm_pull(hidden_grad)
    return (
        values_grad,
        gain_grad,
        shift_grad,
        weight_grad(hidden, projected_grad),
        weight_grad(mixed_low, grad_low),
    )


def conv_forward(values, gain_rows, shift_rows, gating, taps, pointwise, segment):
    normed, norm_pull = jax.vjp(norm_rows, values, gain_rows[2], shift_rows[2])
    hidden = normed.astype(jnp.bfloat16)
    doubled = project_rows(hidden, gating)

    def mixing(doubled_in, taps_in):
        half_width = doubled_in.shape[1] // 2
        gated = doubled_in[:, :half_width] * jax.nn.sigmoid(doubled_in[:, half_width:])
        return depthwise_time(gated, taps_in, segment)

    filtered, mix_pull = jax.vjp(mixing, doubled, taps)
    renormed, inner_pull = jax.vjp(norm_rows, filtered, gain_rows[3], shift_rows[3])
    activated, silu_pull = jax.vjp(jax.nn.silu, renormed)
    active_low = activated.astype(jnp.bfloat16)
    return (
        project_rows(active_low, pointwise),
        (norm_pull, hidden, mix_pull, inner_pull, silu_pull, active_low),
    )


def conv_backward(gradient, stored, gating, pointwise):
    norm_pull, hidden, mix_pull, inner_pull, silu_pull, active_low = stored
    grad_low = gradient.astype(jnp.bfloat16)
    active_grad = project_cols(grad_low, pointwise)
    renormed_grad = silu_pull(active_grad)[0]
    filtered_grad, inner_gain, inner_shift = inner_pull(renormed_grad)
    doubled_grad, taps_grad = mix_pull(filtered_grad)
    doubled_low = doubled_grad.astype(jnp.bfloat16)
    hidden_grad = project_cols(doubled_low, gating)
    values_grad, outer_gain, outer_shift = norm_pull(hidden_grad)
    return (
        values_grad,
        outer_gain,
        outer_shift,
        inner_gain,
        inner_shift,
        taps_grad,
        weight_grad(hidden, doubled_low),
        weight_grad(active_low, grad_low),
    )


def shards(
    frames,
    lengths,
    languages,
    embedding,
    gains,
    shifts,
    firstup,
    firstdown,
    projection,
    merger,
    gating,
    kernel,
    pointwise,
    secondup,
    seconddown,
    cotangent,
):
    frame_count = frames.shape[0]
    segment_all, position_all, language_all = layout(lengths, languages, frame_count)
    segment = segment_all[0]
    language_row = language_all[0]
    cosine, sine = angles(position_all[0])
    matching = (segment[:, None] == segment[None, :])[None, :, :]
    table_full, gain_full, shift_full, kernel_full = (
        lax.all_gather(embedding, "fsdp", axis=1, tiled=True),
        lax.all_gather(gains, "fsdp", axis=1, tiled=True),
        lax.all_gather(shifts, "fsdp", axis=1, tiled=True),
        lax.all_gather(kernel, "fsdp", axis=1, tiled=True),
    )
    gain_rows = gain_full.astype(jnp.float32)
    shift_rows = shift_full.astype(jnp.float32)
    taps = kernel_full.astype(jnp.float32)
    language_hot = (
        language_row[:, None] == jnp.arange(table_full.shape[0], dtype=jnp.int32)[None, :]
    ).astype(jnp.float32)
    start_sum = frames.astype(jnp.float32) + jnp.dot(
        language_hot.astype(jnp.bfloat16), table_full, preferred_element_type=jnp.float32
    )
    first_branch, first_stored = feed_forward(
        start_sum, gain_rows[0], shift_rows[0], firstup, firstdown
    )
    after_first = start_sum + 0.5 * first_branch
    attend_branch, attend_stored = attention_forward(
        after_first, gain_rows[1], shift_rows[1], projection, merger, matching, cosine, sine
    )
    after_attention = after_first + attend_branch
    conv_branch, conv_stored = conv_forward(
        after_attention, gain_rows, shift_rows, gating, taps, pointwise, segment
    )
    after_conv = after_attention + conv_branch
    second_branch, second_stored = feed_forward(
        after_conv, gain_rows[4], shift_rows[4], secondup, seconddown
    )
    after_second = after_conv + 0.5 * second_branch
    encoded, final_pull = jax.vjp(norm_rows, after_second, gain_rows[5], shift_rows[5])
    grad_second, final_gain, final_shift = final_pull(cotangent.astype(jnp.float32))
    branch_grad, second_gain, second_shift, secondup_grad, seconddown_grad = feed_backward(
        0.5 * grad_second, second_stored, secondup, seconddown
    )
    grad_conv = grad_second + branch_grad
    (
        branch_grad,
        outer_gain,
        outer_shift,
        inner_gain,
        inner_shift,
        taps_grad,
        gating_grad,
        pointwise_grad,
    ) = conv_backward(grad_conv, conv_stored, gating, pointwise)
    grad_attention = grad_conv + branch_grad
    branch_grad, attend_gain, attend_shift, projection_grad, merger_grad = attention_backward(
        grad_attention, attend_stored, projection, merger, matching
    )
    grad_first = grad_attention + branch_grad
    branch_grad, first_gain, first_shift, firstup_grad, firstdown_grad = feed_backward(
        0.5 * grad_first, first_stored, firstup, firstdown
    )
    frames_grad = grad_first + branch_grad
    table_grad = lax.dot_general(
        language_hot, frames_grad, (((0,), (0,)), ((), ())), precision=lax.Precision.HIGHEST
    )
    gain_stack = jnp.stack(
        [first_gain, attend_gain, outer_gain, inner_gain, second_gain, final_gain]
    )
    shift_stack = jnp.stack(
        [first_shift, attend_shift, outer_shift, inner_shift, second_shift, final_shift]
    )
    table_part, gain_part, shift_part, taps_part = (
        lax.psum_scatter(
            table_grad.astype(jnp.bfloat16), "fsdp", scatter_dimension=1, tiled=True
        ).astype(jnp.float32),
        lax.psum_scatter(
            gain_stack.astype(jnp.bfloat16), "fsdp", scatter_dimension=1, tiled=True
        ).astype(jnp.float32),
        lax.psum_scatter(
            shift_stack.astype(jnp.bfloat16), "fsdp", scatter_dimension=1, tiled=True
        ).astype(jnp.float32),
        lax.psum_scatter(
            taps_grad.astype(jnp.bfloat16), "fsdp", scatter_dimension=1, tiled=True
        ).astype(jnp.float32),
    )
    table_sum, gain_sum, shift_sum, taps_sum = lax.psum(
        (table_part, gain_part, shift_part, taps_part), "dp"
    )
    return (
        encoded.astype(jnp.bfloat16),
        frames_grad,
        table_sum,
        gain_sum,
        shift_sum,
        firstup_grad,
        firstdown_grad,
        projection_grad,
        merger_grad,
        gating_grad,
        taps_sum,
        pointwise_grad,
        secondup_grad,
        seconddown_grad,
    )


def solution(mesh):
    return jax.shard_map(
        shards,
        mesh=mesh,
        in_specs=(
            P(("dp", "fsdp"), None),
            P(("dp", "fsdp"), None),
            P(("dp", "fsdp"), None),
            P(None, "fsdp"),
            P(None, "fsdp"),
            P(None, "fsdp"),
            P("fsdp", None),
            P("fsdp", None),
            P("fsdp", None),
            P("fsdp", None),
            P("fsdp", None),
            P(None, "fsdp"),
            P("fsdp", None),
            P("fsdp", None),
            P("fsdp", None),
            P(("dp", "fsdp"), None),
        ),
        out_specs=(
            P(("dp", "fsdp"), None),
            P(("dp", "fsdp"), None),
            P(None, "fsdp"),
            P(None, "fsdp"),
            P(None, "fsdp"),
            P("fsdp", None),
            P("fsdp", None),
            P("fsdp", None),
            P("fsdp", None),
            P("fsdp", None),
            P(None, "fsdp"),
            P("fsdp", None),
            P("fsdp", None),
            P("fsdp", None),
        ),
        check_vma=False,
    )
```

profile of v0, /device:TPU:0, one launch (start us, length us, event | category | flops | bytes accessed | tf_op | source)
XLA Modules:
  0.0 1386.7 jit_solution(13179683566529117681)
XLA Ops:
  12.9 14.4 %all_gather.52 = bf16[5,1024]{1,0:T(8,128)(2,1)S(1)} all-gather(bf16[5,128]{1,0:T(8,128)(2,1)S(1)} %copy-done.90), channel_id=1, replica_groups=mesh['dp'=4,'fsdp'=8] {'fsdp'}, dimensions={1}, use_global_device_ids=true | all-gather | bytes 11520 | tf_op jit(solution)/shard_map/all_gather | solution.py:260
  27.4 12.8 all_gather.46
  40.2 13.1 all_gather.45
  53.3 16.6 %all_gather.44 = bf16[102,1024]{1,0:T(8,128)(2,1)S(1)} all-gather(bf16[102,128]{1,0:T(8,128)(2,1)S(1)} %copy-done.44), channel_id=1, replica_groups=mesh['dp'=4,'fsdp'=8] {'fsdp'}, dimensions={1}, use_global_device_ids=true | all-gather | bytes 235008 | tf_op jit(solution)/shard_map/all_gather | solution.py:257
  73.5 23.0 %all-gather.9.cloned.1.call-done = bf16[1024,4096]{1,0:T(8,128)(2,1)} async-done(((bf16[128,4096]{1,0:T(8,128)(2,1)}), bf16[1024,4096]{1,0:T(8,128)(2,1)}) %all-gather.9.cloned.1.call-update) | async-done | bytes 8388624 | tf_op jit(solution)/shard_map/all_gather | solution.py:71
  104.2 74.4 %all-gather.11.cloned.1.call-done = bf16[1024,4096]{1,0:T(8,128)(2,1)} async-done(((bf16[128,4096]{1,0:T(8,128)(2,1)}), bf16[1024,4096]{1,0:T(8,128)(2,1)}) %all-gather.11.cloned.1.call-update) | async-done | bytes 8388624 | tf_op jit(solution)/shard_map/all_gather | solution.py:77
  186.0 57.6 %all-gather.13.cloned.1.call-done = bf16[1024,3072]{1,0:T(8,128)(2,1)} async-done(((bf16[128,3072]{1,0:T(8,128)(2,1)}), bf16[1024,3072]{1,0:T(8,128)(2,1)}) %all-gather.13.cloned.1.call-update) | async-done | bytes 6291472 | tf_op jit(solution)/shard_map/all_gather | solution.py:71
  257.9 14.9 %all-gather.15.cloned.1.call-done = bf16[1024,1024]{1,0:T(8,128)(2,1)} async-done(((bf16[128,1024]{1,0:T(8,128)(2,1)}), bf16[1024,1024]{1,0:T(8,128)(2,1)}) %all-gather.15.cloned.1.call-update) | async-done | bytes 2097168 | tf_op jit(solution)/shard_map/all_gather | solution.py:71
  276.7 44.3 %all-gather.17.cloned.1.call-done = bf16[1024,2048]{1,0:T(8,128)(2,1)} async-done(((bf16[128,2048]{1,0:T(8,128)(2,1)}), bf16[1024,2048]{1,0:T(8,128)(2,1)}) %all-gather.17.cloned.1.call-update) | async-done | bytes 4194320 | tf_op jit(solution)/shard_map/all_gather | solution.py:71
  329.6 20.7 %all-gather.19.cloned.1.call-done = bf16[1024,1024]{1,0:T(8,128)(2,1)} async-done(((bf16[128,1024]{1,0:T(8,128)(2,1)}), bf16[1024,1024]{1,0:T(8,128)(2,1)}) %all-gather.19.cloned.1.call-update) | async-done | bytes 2097168 | tf_op jit(solution)/shard_map/all_gather | solution.py:71
  355.5 77.9 %all-gather.21.cloned.1.call-done = bf16[1024,4096]{1,0:T(8,128)(2,1)} async-done(((bf16[128,4096]{1,0:T(8,128)(2,1)}), bf16[1024,4096]{1,0:T(8,128)(2,1)}) %all-gather.21.cloned.1.call-update) | async-done | bytes 8388624 | tf_op jit(solution)/shard_map/all_gather | solution.py:71
  441.6 74.1 %all-gather.23.cloned.1.call-done = bf16[1024,4096]{1,0:T(8,128)(2,1)} async-done(((bf16[128,4096]{1,0:T(8,128)(2,1)}), bf16[1024,4096]{1,0:T(8,128)(2,1)}) %all-gather.23.cloned.1.call-update) | async-done | bytes 8388624 | tf_op jit(solution)/shard_map/all_gather | solution.py:77
  637.7 32.9 %reduce-scatter.29.cloned.1.call-done = bf16[128,2048]{1,0:T(8,128)(2,1)} async-done(((bf16[1024,2048]{1,0:T(8,128)(2,1)}), bf16[128,2048]{1,0:T(8,128)(2,1)}) %reduce-scatter.29.cloned.1.call-update) | async-done | bytes 524304 | tf_op jit(solution)/shard_map/reduce_scatter | solution.py:81
  670.6 70.1 %reduce-scatter.25.cloned.1.call-done = bf16[128,3072]{1,0:T(8,128)(2,1)} async-done(((bf16[1024,3072]{1,0:T(8,128)(2,1)}), bf16[128,3072]{1,0:T(8,128)(2,1)}) %reduce-scatter.25.cloned.1.call-update) | async-done | bytes 786448 | tf_op jit(solution)/shard_map/reduce_scatter | solution.py:81
  740.8 90.3 %reduce-scatter.21.cloned.1.call-done = bf16[128,4096]{1,0:T(8,128)(2,1)} async-done(((bf16[1024,4096]{1,0:T(8,128)(2,1)}), bf16[128,4096]{1,0:T(8,128)(2,1)}) %reduce-scatter.21.cloned.1.call-update) | async-done | bytes 1048592 | tf_op jit(solution)/shard_map/reduce_scatter | solution.py:81
  831.1 90.1 %reduce-scatter.23.cloned.1.call-done = bf16[128,4096]{1,0:T(8,128)(2,1)} async-done(((bf16[1024,4096]{1,0:T(8,128)(2,1)}), bf16[128,4096]{1,0:T(8,128)(2,1)}) %reduce-scatter.23.cloned.1.call-update) | async-done | bytes 1048592 | tf_op jit(solution)/shard_map/reduce_scatter | solution.py:81
  921.2 90.1 %reduce-scatter.33.cloned.1.call-done = bf16[128,4096]{1,0:T(8,128)(2,1)} async-done(((bf16[1024,4096]{1,0:T(8,128)(2,1)}), bf16[128,4096]{1,0:T(8,128)(2,1)}) %reduce-scatter.33.cloned.1.call-update) | async-done | bytes 1048592 | tf_op jit(solution)/shard_map/reduce_scatter | solution.py:81
  1011.3 90.1 %reduce-scatter.35.cloned.1.call-done = bf16[128,4096]{1,0:T(8,128)(2,1)} async-done(((bf16[1024,4096]{1,0:T(8,128)(2,1)}), bf16[128,4096]{1,0:T(8,128)(2,1)}) %reduce-scatter.35.cloned.1.call-update) | async-done | bytes 1048592 | tf_op jit(solution)/shard_map/reduce_scatter | solution.py:81
  1101.5 31.4 %reduce-scatter.43.cloned.1.call-done = bf16[128,5]{1,0:T(8,128)(2,1)} async-done(((bf16[1024,5]{1,0:T(8,128)(2,1)}), bf16[128,5]{1,0:T(8,128)(2,1)}) %reduce-scatter.43.cloned.1.call-update) | async-done | bytes 1296
  1133.7 30.6 %reduce-scatter.39.cloned.1.call-done = bf16[128,6]{1,0:T(8,128)(2,1)} async-done(((bf16[1024,6]{1,0:T(8,128)(2,1)}), bf16[128,6]{1,0:T(8,128)(2,1)}) %reduce-scatter.39.cloned.1.call-update) | async-done | bytes 1552
  1165.1 30.5 %reduce-scatter.41.cloned.1.call-done = bf16[128,6]{1,0:T(8,128)(2,1)} async-done(((bf16[1024,6]{1,0:T(8,128)(2,1)}), bf16[128,6]{1,0:T(8,128)(2,1)}) %reduce-scatter.41.cloned.1.call-update) | async-done | bytes 1552
  1196.5 30.6 %reduce-scatter.37.cloned.1.call-done = bf16[128,102]{1,0:T(8,128)(2,1)} async-done(((bf16[1024,102]{1,0:T(8,128)(2,1)}), bf16[128,102]{1,0:T(8,128)(2,1)}) %reduce-scatter.37.cloned.1.call-update) | async-done | bytes 26128
  1227.9 18.3 %all-reduce.18 = (f32[102,128]{1,0:T(8,128)}, f32[6,128]{1,0:T(8,128)}, f32[6,128]{1,0:T(8,128)}, f32[5,128]{1,0:T(8,128)}) all-reduce(bf16[102,128]{1,0:T(8,128)(2,1)S(1)} %copy.104, bf16[6,128]{1,0:T(8,128)(2,1)S(1)} %copy.106, bf16[6,128]{1,0:T(8,128)(2,1)S(1)} %copy.108, ...), channel_id=1, replica_groups=mesh['dp'=4,'fsdp'=8] {'dp'}, use_global_device_ids=true, to_apply=%region_32.33 | all-reduce | flops 15232 | bytes 91392 | tf_op jit(solution)/shard_map/psum | solution.py:335
  1246.2 120.5 %all-reduce.22.cloned.1.call-done = (bf16[128,4096]{1,0:T(8,128)(2,1)}, bf16[128,4096]{1,0:T(8,128)(2,1)}, bf16[128,3072]{1,0:T(8,128)(2,1)}, bf16[128,1024]{1,0...) async-done(((bf16[128,4096]{1,0:T(8,128)(2,1)}, bf16[128,4096]{1,0:T(8,128)(2,1)}, ...) | async-done | bytes 6029328 | tf_op jit(solution)/shard_map/psum | solution.py:89
  (399 shorter events, 201.2 us)
Async XLA Ops:
  7.2 62.8 %copy-start.41 = (bf16[256,1024]{1,0:T(8,128)(2,1)S(1)}, bf16[256,1024]{1,0:T(8,128)(2,1)}, u32[]{:S(2)}) copy-start(bf16[256,1024]{1,0:T(8,128)(2,1)} %param.16) | copy-start | bytes 1572868
  7.3 89.2 %all-gather.9.cloned.1.call-start = ((), (), s32[]{:S(2)}) async-start(), calls=%async_computation.12 | async-start | bytes 9437184 | tf_op jit(solution)/shard_map/all_gather | solution.py:71
  8.0 170.6 %all-gather.11.cloned.1.call-start = ((), (), s32[]{:S(2)}) async-start(), calls=%async_computation.13 | async-start | bytes 9437184 | tf_op jit(solution)/shard_map/all_gather | solution.py:77
  8.7 234.9 %all-gather.13.cloned.1.call-start = ((), (), s32[]{:S(2)}) async-start(), calls=%async_computation.14 | async-start | bytes 7077888 | tf_op jit(solution)/shard_map/all_gather | solution.py:71
  9.5 263.3 %all-gather.15.cloned.1.call-start = ((), (), s32[]{:S(2)}) async-start(), calls=%async_computation.15 | async-start | bytes 2359296 | tf_op jit(solution)/shard_map/all_gather | solution.py:71
  10.0 310.9 %all-gather.17.cloned.1.call-start = ((), (), s32[]{:S(2)}) async-start(), calls=%async_computation.16 | async-start | bytes 4718592 | tf_op jit(solution)/shard_map/all_gather | solution.py:71
  10.6 339.6 %all-gather.19.cloned.1.call-start = ((), (), s32[]{:S(2)}) async-start(), calls=%async_computation.17 | async-start | bytes 2359296 | tf_op jit(solution)/shard_map/all_gather | solution.py:71
  11.2 422.2 %all-gather.21.cloned.1.call-start = ((), (), s32[]{:S(2)}) async-start(), calls=%async_computation.18 | async-start | bytes 9437184 | tf_op jit(solution)/shard_map/all_gather | solution.py:71
  12.0 503.7 %all-gather.23.cloned.1.call-start = ((), (), s32[]{:S(2)}) async-start(), calls=%async_computation.19 | async-start | bytes 9437184 | tf_op jit(solution)/shard_map/all_gather | solution.py:77
  12.7 624.9 %reduce-scatter.27.cloned.1.call-start = ((), (), s32[]{:S(2)}) async-start(), calls=%async_computation.23 | async-start | bytes 2359296 | tf_op jit(solution)/shard_map/reduce_scatter | solution.py:81
  70.6 108.0 %copy-start.2 = (f32[256,1024]{1,0:T(8,128)}, f32[256,1024]{1,0:T(8,128)S(1)}, u32[]{:S(2)}) copy-start(f32[256,1024]{1,0:T(8,128)S(1)} %get-tuple-element.110) | copy-start | bytes 3145732
  547.9 89.7 %reduce-scatter.31.cloned.1.call-start = ((), (), s32[]{:S(2)}) async-start(), calls=%async_computation.25 | async-start | bytes 2359296 | tf_op jit(solution)/shard_map/reduce_scatter | solution.py:81
  551.9 118.7 %reduce-scatter.29.cloned.1.call-start = ((), (), s32[]{:S(2)}) async-start(), calls=%async_computation.24 | async-start | bytes 4718592 | tf_op jit(solution)/shard_map/reduce_scatter | solution.py:81
  557.0 183.8 %reduce-scatter.25.cloned.1.call-start = ((), (), s32[]{:S(2)}) async-start(), calls=%async_computation.22 | async-start | bytes 7077888 | tf_op jit(solution)/shard_map/reduce_scatter | solution.py:81
  576.7 254.3 %reduce-scatter.21.cloned.1.call-start = ((), (), s32[]{:S(2)}) async-start(), calls=%async_computation.20 | async-start | bytes 9437184 | tf_op jit(solution)/shard_map/reduce_scatter | solution.py:81
  598.5 322.7 %reduce-scatter.23.cloned.1.call-start = ((), (), s32[]{:S(2)}) async-start(), calls=%async_computation.21 | async-start | bytes 9437184 | tf_op jit(solution)/shard_map/reduce_scatter | solution.py:81
  606.5 404.8 %reduce-scatter.33.cloned.1.call-start = ((), (), s32[]{:S(2)}) async-start(), calls=%async_computation.26 | async-start | bytes 9437184 | tf_op jit(solution)/shard_map/reduce_scatter | solution.py:81
  615.1 486.4 %reduce-scatter.35.cloned.1.call-start = ((), (), s32[]{:S(2)}) async-start(), calls=%async_computation.27 | async-start | bytes 9437184 | tf_op jit(solution)/shard_map/reduce_scatter | solution.py:81
  624.3 508.5 %reduce-scatter.43.cloned.1.call-start = ((), (), s32[]{:S(2)}) async-start(), calls=%async_computation.31 | async-start | bytes 294912
  633.6 530.7 %reduce-scatter.39.cloned.1.call-start = ((), (), s32[]{:S(2)}) async-start(), calls=%async_computation.29 | async-start | bytes 294912
  634.8 560.9 %reduce-scatter.41.cloned.1.call-start = ((), (), s32[]{:S(2)}) async-start(), calls=%async_computation.30 | async-start | bytes 294912
  635.0 466.5 %copy-start.31 = (f32[256,1024]{1,0:T(8,128)}, f32[256,1024]{1,0:T(8,128)S(1)}, u32[]{:S(2)}) copy-start(f32[256,1024]{1,0:T(8,128)S(1)} %add_add_fusion.6) | copy-start | bytes 3145732
  636.1 591.0 %reduce-scatter.37.cloned.1.call-start = ((), (), s32[]{:S(2)}) async-start(), calls=%async_computation.28 | async-start | bytes 294912
  637.6 729.2 %all-reduce.22.cloned.1.call-start = ((), (), s32[]{:S(2)}) async-start(), calls=%async_computation.32 | async-start | bytes 12058624 | tf_op jit(solution)/shard_map/psum | solution.py:89
  (105 other events, 781.5 us)
Sparse Core Ops, SparseCore 0:
  9.7 86.7 all-gather.8
  98.1 80.4 all-gather.10
  180.3 63.3 all-gather.12
  245.1 27.6 all-gather.14
  274.3 46.6 all-gather.16
  322.4 27.8 all-gather.18
  351.8 81.5 all-gather.20
  435.0 80.5 all-gather.22
  548.0 34.3 reduce-scatter.26
  585.2 34.4 reduce-scatter.30
  622.0 48.6 reduce-scatter.28
  672.8 67.9 reduce-scatter.24
  743.0 87.9 reduce-scatter.20
  833.2 87.9 reduce-scatter.22
  923.3 87.9 reduce-scatter.32
  1013.5 87.9 reduce-scatter.34
  1104.1 28.7 reduce-scatter.42
  1135.7 28.5 reduce-scatter.38
  1167.1 28.4 reduce-scatter.40
  1198.4 28.5 reduce-scatter.36
  1231.6 135.0 all-reduce.21
where the time goes:
time: 1400 us; the launch traced here: 1390 us
  waiting for transfers between devices  1100 us (79%)
  matrix products  130 us (9%)
  blocking collectives  75.2 us (5%)
  local copies, waits for them, and re-layouts  32.7 us (2%)
  other arithmetic  31.2 us (2%)
  between operations  16.1 us (1%)
    reduce_scatter x8, waiting for transfers between devices, weight_grad(): lax.psum_scatter(lax.dot_general(left_side, right_side, (((0,), (0,)), ((...  464 us
    all_gather x6, waiting for transfers between devices, project_rows(): lax.all_gather(weight, 'fsdp', axis=0, tiled=True)  238 us
    all_gather x2, waiting for transfers between devices, project_cols(): lax.all_gather(weight, 'fsdp', axis=0, tiled=True)  148 us
    unnamed x25, waiting for transfers between devices  128 us
    psum x1, waiting for transfers between devices, weight_grad(): return lax.psum(pieces, 'dp').astype(jnp.float32)  121 us
    dot_general x8, matrix products, weight_grad(): lax.dot_general(left_side, right_side, (((0,), (0,)), ((), ())), preferre...  46.1 us
    dot_general x8, matrix products, project_rows(): jnp.dot(inputs, lax.all_gather(weight, 'fsdp', axis=0, tiled=True), prefe...  40.2 us
    dot_general x8, matrix products, times_transposed(): lax.dot_general(left_side, right_side, (((1,), (1,)), ((), ())), preferre...  37.5 us
  transfers between devices with their start and end apart: 21, of which 19 were waited for; matrix products, arithmetic and copies ran while one was open for 10% of the time, Pallas kernels for 0%

commit v1 on v0

v1 whole, which is shorter than its diff:
```python
import functools

import jax
import jax.numpy as jnp
import numpy as np
from jax import lax
from jax.experimental import pallas as pl
from jax.experimental.pallas import tpu as pltpu
from jax.sharding import Mesh
from jax.sharding import PartitionSpec as P

HEAD_DIM = 128


norm_epsilon = 1e-05
masked_score = -1000000000.0


def norm_rows(values, gain_row, shift_row):
    centred = values - jnp.mean(values, axis=-1, keepdims=True)
    spread = jnp.mean(centred * centred, axis=-1, keepdims=True)
    return centred * lax.rsqrt(spread + norm_epsilon) * gain_row + shift_row


def rotate(values, cosine, sine):
    half_dim = values.shape[-1] // 2
    first_half = values[..., :half_dim]
    second_half = values[..., half_dim:]
    return jnp.concatenate(
        [first_half * cosine - second_half * sine, second_half * cosine + first_half * sine],
        axis=-1,
    )


def depthwise_time(values, kernel, segment):
    half_kernel = kernel.shape[0] // 2
    length = values.shape[-2]
    padded = jnp.pad(values, ((half_kernel, half_kernel), (0, 0)))
    segment_pad = jnp.pad(segment, (half_kernel, half_kernel), constant_values=-1)
    summed = jnp.zeros_like(values)
    for tap_index in range(kernel.shape[0]):
        keeping = (segment_pad[tap_index : tap_index + length] == segment)[:, None]
        summed = (
            summed
            + jnp.where(keeping, padded[tap_index : tap_index + length, :], 0.0) * kernel[tap_index]
        )
    return summed


def layout(lengths, languages, frame_count):
    utterances = jnp.arange(lengths.shape[-1], dtype=jnp.int32)
    earlier = utterances[:, None] <= utterances[None, :]
    finish = jnp.sum(jnp.where(earlier[None], lengths[:, :, None], 0), axis=1)
    begins = finish - lengths
    indices = jnp.arange(frame_count, dtype=jnp.int32)
    segment = jnp.sum((indices[None, :, None] >= finish[:, None, :]).astype(jnp.int32), axis=-1)
    owners = segment[:, :, None] == jnp.arange(lengths.shape[-1], dtype=jnp.int32)[None, None, :]
    first_row = jnp.sum(jnp.where(owners, begins[:, None, :], 0), axis=-1)
    language_row = jnp.sum(jnp.where(owners, languages[:, None, :], 0), axis=-1)
    return (segment, indices[None, :] - first_row, language_row)


def angles(position):
    half_dim = HEAD_DIM // 2
    frequency = 10000.0 ** (-jnp.arange(half_dim, dtype=jnp.float32) / half_dim)
    turned = position.astype(jnp.float32)[..., None] * frequency
    return (jnp.cos(turned)[..., None, :], jnp.sin(turned)[..., None, :])


def tie(value, *others):
    return lax.optimization_barrier((value, *others))[0]


def rows_dot(inputs, weight):
    return jnp.dot(inputs, weight, preferred_element_type=jnp.float32)


VMEM_LIMIT = 60 * 1024 * 1024
QUARTERS = 4
BITS = (0, 1)


def swap_dp(value, bit, size):
    return lax.ppermute(value, "dp", [(i, i ^ (1 << bit)) for i in range(size)])


def swap_core(value):
    return lax.ppermute(value, "core", [(0, 1), (1, 0)])


def last_bit(index, order):
    return [bit for bit in order if index >> bit & 1][-1]


def assemble_kernel(layers, widths, place, *refs):
    count = len(widths)
    own, other = refs[:count], refs[count : 2 * count]
    gathered = refs[2 * count]
    pieces = refs[2 * count + 1 : 2 * count + QUARTERS]
    others = refs[2 * count + QUARTERS : 2 * count + 2 * QUARTERS - 1]
    outs = refs[2 * count + 2 * QUARTERS - 1 : -1]
    sems = refs[-1]
    quarter, layer, core = place[0], place[1], place[2]
    copies = []

    def move(source, target):
        copy = pltpu.make_async_copy(source, target, sems.at[len(copies)])
        copy.start()
        copies.append(copy)

    base = 0
    for i, width in enumerate(widths):
        part = width // QUARTERS
        span = pl.ds(base, part)
        mine = pl.ds(pl.multiple_of(quarter * part, part), part)
        move(gathered.at[:, :, span], outs[i].at[:, :, mine])
        for r in range(1, QUARTERS):
            column = pl.ds(pl.multiple_of((quarter ^ r) * part, part), part)
            for source, lane in ((own[i], core), (other[i], 1 - core)):
                move(source.at[:, column], outs[i].at[2 * layer + lane, :, column])
            for source, lane in ((pieces[r - 1], core), (others[r - 1], 1 - core)):
                for k in range(1, layers):
                    row = lax.rem(layer + k, layers) * 2 + lane
                    move(source.at[k - 1, :, span], outs[i].at[row, :, column])
        base += part
    for copy in copies:
        copy.wait()


def assemble(place, layers, own, other, gathered, pieces, others):
    widths = [w.shape[1] for w in own]
    rows = own[0].shape[0]
    copies = len(widths) * (1 + (QUARTERS - 1) * 2 * layers)
    operands = [*own, *other, gathered, *pieces, *others]
    outs = pl.pallas_call(
        functools.partial(assemble_kernel, layers, widths),
        out_shape=[jax.ShapeDtypeStruct((2 * layers, rows, w), jnp.bfloat16) for w in widths],
        in_specs=[pl.BlockSpec(memory_space=pltpu.SMEM)]
        + [pl.BlockSpec(memory_space=pl.ANY)] * len(operands),
        out_specs=[pl.BlockSpec(memory_space=pl.ANY)] * len(widths),
        scratch_shapes=[pltpu.SemaphoreType.DMA((copies,))],
    )(place, *operands)
    return [out.reshape(2 * layers * rows, w) for out, w in zip(outs, widths)]


def weight_terms_kernel(widths, wanted, whole, given, place, *refs):
    count = len(widths)
    lefts, rights = refs[:count], refs[count : 2 * count]
    arrived = refs[2 * count : -1]
    out = refs[-1]
    quarter, core = place[0], place[2]
    side = 1 - core if whole else core
    base = 0
    for i, width in enumerate(widths):
        part = width // QUARTERS
        layers, _, rows, tokens = lefts[i].shape
        left = lefts[i][:, pl.ds(side, 1)].reshape(layers * rows, tokens)
        tile = min(part, 256)

        def tiles(n, body):
            if n == 1:
                body(0)
            else:
                pl.loop(0, n)(body)

        if whole:

            def step(t, i=i, left=left, base=base, tile=tile):
                column = pl.multiple_of(t * tile, tile)
                product = jnp.dot(
                    left, rights[i][:, pl.ds(column, tile)], preferred_element_type=jnp.float32
                )
                out[:, pl.ds(QUARTERS * base + column, tile)] = product.astype(out.dtype)

            tiles(width // tile, step)
        else:
            for at, r in enumerate(wanted):
                start = (quarter ^ r) * part

                def step(t, i=i, left=left, base=base, part=part, tile=tile, at=at, r=r, start=start):
                    column = pl.multiple_of(t * tile, tile)
                    source = pl.multiple_of(start + column, tile)
                    product = jnp.dot(
                        left, rights[i][:, pl.ds(source, tile)], preferred_element_type=jnp.float32
                    )
                    full = pl.ds(pl.multiple_of(QUARTERS * base + source, tile), tile)
                    product += arrived[0][:, full].astype(jnp.float32)
                    narrow = pl.ds(pl.multiple_of(base + column, tile), tile)
                    for ref, holds in zip(arrived[1:], given):
                        product += ref[holds.index(r), :, narrow].astype(jnp.float32)
                    out[at, :, narrow] = product.astype(out.dtype)

                tiles(part // tile, step)
        base += part


def weight_terms(place, lefts, rights, arrived=(), wanted=None, given=()):
    widths = [right.shape[1] for right in rights]
    layers, _, rows, tokens = lefts[0].shape
    whole = wanted is None
    if whole:
        shape = (layers * rows, sum(widths))
        flops = 2 * tokens * layers * rows * sum(widths)
    else:
        shape = (len(wanted), layers * rows, sum(widths) // QUARTERS)
        flops = 2 * tokens * layers * rows * sum(widths) // QUARTERS * len(wanted)
    operands = [*lefts, *rights, *arrived]
    return pl.pallas_call(
        functools.partial(weight_terms_kernel, widths, wanted, whole, given),
        out_shape=jax.ShapeDtypeStruct(shape, jnp.bfloat16),
        in_specs=[pl.BlockSpec(memory_space=pltpu.SMEM)]
        + [pl.BlockSpec(memory_space=pltpu.VMEM)] * len(operands),
        out_specs=pl.BlockSpec(memory_space=pltpu.VMEM),
        compiler_params=pltpu.CompilerParams(vmem_limit_bytes=VMEM_LIMIT),
        cost_estimate=pl.CostEstimate(
            flops=flops,
            bytes_accessed=2 * sum(int(np.prod(x.shape)) for x in operands) + 2 * int(np.prod(shape)),
            transcendentals=0,
        ),
    )(place, *operands)


def spread_kernel(widths, place, *refs):
    pieces, outs = refs[:QUARTERS], refs[QUARTERS:]
    quarter = place[0]
    base = 0
    for i, width in enumerate(widths):
        part = width // QUARTERS
        for r in range(QUARTERS):
            column = pl.ds(pl.multiple_of((quarter ^ r) * part, part), part)
            outs[i][:, column] = pieces[r][:, pl.ds(base, part)].astype(jnp.float32)
        base += part


def spread(place, widths, pieces):
    rows = pieces[0].shape[0]
    return pl.pallas_call(
        functools.partial(spread_kernel, widths),
        out_shape=[jax.ShapeDtypeStruct((rows, w), jnp.float32) for w in widths],
        in_specs=[pl.BlockSpec(memory_space=pltpu.SMEM)]
        + [pl.BlockSpec(memory_space=pltpu.VMEM)] * QUARTERS,
        out_specs=[pl.BlockSpec(memory_space=pltpu.VMEM)] * len(widths),
        compiler_params=pltpu.CompilerParams(vmem_limit_bytes=VMEM_LIMIT),
    )(place, *pieces)


def gather_weights(place, sizes, groups):
    dp_size, layers = sizes
    quarter, layer, core = place[0], place[1], place[2]
    gathered = []
    for group in groups:
        mine = jnp.concatenate(
            [
                lax.dynamic_slice_in_dim(w, quarter * (w.shape[1] // QUARTERS), w.shape[1] // QUARTERS, 1)
                for w in group
            ],
            axis=1,
        )
        gathered.append(lax.all_gather(mine, ("z", "core"), axis=0, tiled=False))
    fulls = []
    for index, group in enumerate(groups):
        order = BITS if index % 2 == 0 else BITS[::-1]
        other = [swap_core(w) for w in group]
        rows, width = gathered[index].shape[1:]
        grid = gathered[index].reshape(layers, 2, rows, width)
        held = {
            0: jnp.stack(
                [
                    lax.dynamic_slice(
                        grid, (lax.rem(layer + k, layers), core, 0, 0), (1, 1, rows, width)
                    )[0, 0]
                    for k in range(1, layers)
                ]
            )
        }
        for r in range(1, QUARTERS):
            bit = last_bit(r, order)
            held[r] = swap_dp(held[r ^ (1 << bit)], bit, dp_size)
        pieces = [held[r] for r in range(1, QUARTERS)]
        others = [swap_core(piece) for piece in pieces]
        fulls.append(assemble(place, layers, group, other, gathered[index], pieces, others))
    return fulls


def weight_grads(place, sizes, pairs, flip):
    dp_size, layers = sizes
    first, second = BITS if not flip else BITS[::-1]
    lefts = []
    for left, _ in pairs:
        tokens, features = left.shape
        lefts.append(left.T.reshape(layers, 2, features // (2 * layers), tokens))
    rights = [right for _, right in pairs]
    widths = [right.shape[1] for right in rights]
    across = swap_core(weight_terms(place, lefts, rights))
    sent = [r for r in range(QUARTERS) if r >> first & 1]
    first_sums = swap_dp(weight_terms(place, lefts, rights, (across,), sent), first, dp_size)
    first_given = [r ^ (1 << first) for r in sent]
    second_sums = swap_dp(
        weight_terms(place, lefts, rights, (across, first_sums), [1 << second], (first_given,)),
        second,
        dp_size,
    )
    own = weight_terms(
        place, lefts, rights, (across, first_sums, second_sums), [0], (first_given, [0])
    )[0]
    summed = lax.psum_scatter(own, "z", scatter_dimension=0, tiled=True)
    bit = len(BITS)
    while 1 << bit < dp_size:
        summed = summed + swap_dp(summed, bit, dp_size)
        bit += 1
    held = {0: summed}
    for r in range(1, QUARTERS):
        bit = last_bit(r, (second, first))
        held[r] = swap_dp(held[r ^ (1 << bit)], bit, dp_size)
    return spread(place, widths, [held[r] for r in range(QUARTERS)])


def gather_small(arrays):
    rows = [a.shape[0] for a in arrays]
    packed = jnp.concatenate(arrays, axis=0)
    packed = jnp.pad(packed, ((0, -packed.shape[0] % 16), (0, 0)))
    full = lax.all_gather(packed, ("z", "core"), axis=0, tiled=False)
    full = full.transpose(1, 0, 2).reshape(packed.shape[0], -1)
    pieces, start = [], 0
    for count in rows:
        pieces.append(full[start : start + count])
        start += count
    return pieces


def sum_small(place, sizes, arrays):
    rows = [a.shape[0] for a in arrays]
    packed = jnp.concatenate(arrays, axis=0)
    width = packed.shape[1] // (2 * sizes[1])
    total = lax.psum(packed, ("dp", "z", "core"))
    mine = lax.dynamic_slice_in_dim(total, (place[1] * 2 + place[2]) * width, width, 1)
    pieces, start = [], 0
    for count in rows:
        pieces.append(mine[start : start + count])
        start += count
    return pieces


def times_transposed(left_side, right_side):
    return lax.dot_general(
        left_side, right_side, (((1,), (1,)), ((), ())), preferred_element_type=jnp.float32
    )


def feed_forward(values, gain_row, shift_row, upward, downward):
    normed, norm_pull = jax.vjp(norm_rows, values, gain_row, shift_row)
    hidden = normed.astype(jnp.bfloat16)
    expanded = rows_dot(hidden, upward)
    activated, silu_pull = jax.vjp(jax.nn.silu, expanded)
    active_low = activated.astype(jnp.bfloat16)
    return (times_transposed(active_low, downward), (norm_pull, hidden, silu_pull, active_low))


def feed_backward(gradient, stored, upward, downward):
    norm_pull, hidden, silu_pull, active_low = stored
    grad_low = gradient.astype(jnp.bfloat16)
    active_grad = rows_dot(grad_low, downward)
    expand_grad = silu_pull(active_grad)[0].astype(jnp.bfloat16)
    hidden_grad = times_transposed(expand_grad, upward)
    values_grad, gain_grad, shift_grad = norm_pull(hidden_grad)
    return (
        values_grad,
        gain_grad,
        shift_grad,
        (hidden, expand_grad),
        (grad_low, active_low),
    )


def attention_forward(values, gain_row, shift_row, projection, merger, matching, cosine, sine):
    normed, norm_pull = jax.vjp(norm_rows, values, gain_row, shift_row)
    hidden = normed.astype(jnp.bfloat16)
    projected = rows_dot(hidden, projection)
    frame_count = projected.shape[0]
    head_count = projected.shape[1] // (3 * HEAD_DIM)
    shaped = projected.reshape(frame_count, 3, head_count, HEAD_DIM)

    def turning(query_raw, key_raw):
        return (rotate(query_raw, cosine, sine) * HEAD_DIM ** (-0.5), rotate(key_raw, cosine, sine))

    (query_rot, key_rot), turn_pull = jax.vjp(turning, shaped[:, 0], shaped[:, 1])
    query_low = query_rot.astype(jnp.bfloat16)
    key_low = key_rot.astype(jnp.bfloat16)
    value_low = shaped[:, 2].astype(jnp.bfloat16)
    scores = jnp.where(
        matching,
        jnp.einsum("qhd,khd->hqk", query_low, key_low, preferred_element_type=jnp.float32),
        masked_score,
    )
    highest_score = jnp.max(scores, axis=-1, keepdims=True)
    log_total = highest_score + jnp.log(
        jnp.sum(jnp.exp(scores - highest_score), axis=-1, keepdims=True)
    )
    probs_low = jnp.exp(scores - log_total).astype(jnp.bfloat16)
    mixed = jnp.einsum("hqk,khd->qhd", probs_low, value_low, preferred_element_type=jnp.float32)
    mixed_low = mixed.reshape(frame_count, head_count * HEAD_DIM).astype(jnp.bfloat16)
    return (
        rows_dot(mixed_low, merger),
        (norm_pull, hidden, turn_pull, query_low, key_low, value_low, log_total, mixed_low),
    )


def attention_backward(gradient, stored, projection, merger, matching):
    norm_pull, hidden, turn_pull, query_low, key_low, value_low, log_total, mixed_low = stored
    frame_count, head_count = (query_low.shape[0], query_low.shape[1])
    grad_low = gradient.astype(jnp.bfloat16)
    mixed_grad = (
        times_transposed(grad_low, merger)
        .astype(jnp.bfloat16)
        .reshape(frame_count, head_count, HEAD_DIM)
    )
    scores = jnp.where(
        matching,
        jnp.einsum("qhd,khd->hqk", query_low, key_low, preferred_element_type=jnp.float32),
        masked_score,
    )
    probs = jnp.exp(scores - log_total)
    value_grad = jnp.einsum(
        "hqk,qhd->khd", probs.astype(jnp.bfloat16), mixed_grad, preferred_element_type=jnp.float32
    )
    probs_grad = jnp.einsum(
        "qhd,khd->hqk", mixed_grad, value_low, preferred_element_type=jnp.float32
    )
    score_grad = (
        probs * (probs_grad - jnp.sum(probs * probs_grad, axis=-1, keepdims=True))
    ).astype(jnp.bfloat16)
    query_grad = jnp.einsum("hqk,khd->qhd", score_grad, key_low, preferred_element_type=jnp.float32)
    key_grad = jnp.einsum("hqk,qhd->khd", score_grad, query_low, preferred_element_type=jnp.float32)
    query_raw_grad, key_raw_grad = turn_pull((query_grad, key_grad))
    stacked = jnp.stack([query_raw_grad, key_raw_grad, value_grad], axis=1)
    projected_grad = stacked.reshape(frame_count, 3 * head_count * HEAD_DIM).astype(jnp.bfloat16)
    hidden_grad = times_transposed(projected_grad, projection)
    values_grad, gain_grad, shift_grad = norm_pull(hidden_grad)
    return (
        values_grad,
        gain_grad,
        shift_grad,
        (hidden, projected_grad),
        (mixed_low, grad_low),
    )


def conv_forward(values, gain_rows, shift_rows, gating, taps, pointwise, segment):
    normed, norm_pull = jax.vjp(norm_rows, values, gain_rows[2], shift_rows[2])
    hidden = normed.astype(jnp.bfloat16)
    doubled = rows_dot(hidden, gating)

    def mixing(doubled_in, taps_in):
        half_width = doubled_in.shape[1] // 2
        gated = doubled_in[:, :half_width] * jax.nn.sigmoid(doubled_in[:, half_width:])
        return depthwise_time(gated, taps_in, segment)

    filtered, mix_pull = jax.vjp(mixing, doubled, taps)
    renormed, inner_pull = jax.vjp(norm_rows, filtered, gain_rows[3], shift_rows[3])
    activated, silu_pull = jax.vjp(jax.nn.silu, renormed)
    active_low = activated.astype(jnp.bfloat16)
    return (
        rows_dot(active_low, pointwise),
        (norm_pull, hidden, mix_pull, inner_pull, silu_pull, active_low),
    )


def conv_backward(gradient, stored, gating, pointwise):
    norm_pull, hidden, mix_pull, inner_pull, silu_pull, active_low = stored
    grad_low = gradient.astype(jnp.bfloat16)
    active_grad = times_transposed(grad_low, pointwise)
    renormed_grad = silu_pull(active_grad)[0]
    filtered_grad, inner_gain, inner_shift = inner_pull(renormed_grad)
    doubled_grad, taps_grad = mix_pull(filtered_grad)
    doubled_low = doubled_grad.astype(jnp.bfloat16)
    hidden_grad = times_transposed(doubled_low, gating)
    values_grad, outer_gain, outer_shift = norm_pull(hidden_grad)
    return (
        values_grad,
        outer_gain,
        outer_shift,
        inner_gain,
        inner_shift,
        taps_grad,
        (hidden, doubled_low),
        (active_low, grad_low),
    )


def shards(
    sizes,
    frames,
    lengths,
    languages,
    embedding,
    gains,
    shifts,
    firstup,
    firstdown,
    projection,
    merger,
    gating,
    kernel,
    pointwise,
    secondup,
    seconddown,
    cotangent,
):
    frame_count = frames.shape[0]
    segment_all, position_all, language_all = layout(lengths, languages, frame_count)
    segment = segment_all[0]
    language_row = language_all[0]
    cosine, sine = angles(position_all[0])
    matching = (segment[:, None] == segment[None, :])[None, :, :]
    dp_index = lax.axis_index("dp").astype(jnp.int32)
    place = jnp.stack(
        [
            lax.rem(dp_index, jnp.int32(QUARTERS)),
            lax.axis_index("z").astype(jnp.int32),
            lax.axis_index("core").astype(jnp.int32),
        ]
    )
    table_full, gain_full, shift_full, kernel_full = gather_small(
        [embedding, gains, shifts, kernel]
    )
    groups = gather_weights(
        place,
        sizes,
        [[firstup], [firstdown, projection], [merger, gating, pointwise, secondup], [seconddown]],
    )
    (
        firstup_full,
        firstdown_full,
        projection_full,
        merger_full,
        gating_full,
        pointwise_full,
        secondup_full,
        seconddown_full,
    ) = [w for group in groups for w in group]
    gain_rows = gain_full.astype(jnp.float32)
    shift_rows = shift_full.astype(jnp.float32)
    taps = kernel_full.astype(jnp.float32)
    language_hot = (
        language_row[:, None] == jnp.arange(table_full.shape[0], dtype=jnp.int32)[None, :]
    ).astype(jnp.float32)
    start_sum = frames.astype(jnp.float32) + jnp.dot(
        language_hot.astype(jnp.bfloat16), table_full, preferred_element_type=jnp.float32
    )
    first_branch, first_stored = feed_forward(
        start_sum, gain_rows[0], shift_rows[0], firstup_full, firstdown_full
    )
    after_first = start_sum + 0.5 * first_branch
    attend_branch, attend_stored = attention_forward(
        after_first, gain_rows[1], shift_rows[1], projection_full, merger_full, matching, cosine, sine
    )
    after_attention = after_first + attend_branch
    conv_branch, conv_stored = conv_forward(
        after_attention, gain_rows, shift_rows, gating_full, taps, pointwise_full, segment
    )
    after_conv = after_attention + conv_branch
    second_branch, second_stored = feed_forward(
        after_conv, gain_rows[4], shift_rows[4], secondup_full, seconddown_full
    )
    after_second = after_conv + 0.5 * second_branch
    encoded, final_pull = jax.vjp(norm_rows, after_second, gain_rows[5], shift_rows[5])
    grad_second, final_gain, final_shift = final_pull(cotangent.astype(jnp.float32))
    branch_grad, second_gain, second_shift, secondup_grad, seconddown_grad = feed_backward(
        0.5 * grad_second, second_stored, secondup_full, seconddown_full
    )
    grad_conv = grad_second + branch_grad
    (
        branch_grad,
        outer_gain,
        outer_shift,
        inner_gain,
        inner_shift,
        taps_grad,
        gating_grad,
        pointwise_grad,
    ) = conv_backward(grad_conv, conv_stored, gating_full, pointwise_full)
    grad_attention = grad_conv + branch_grad
    branch_grad, attend_gain, attend_shift, projection_grad, merger_grad = attention_backward(
        grad_attention, attend_stored, projection_full, merger_full, matching
    )
    grad_first = grad_attention + branch_grad
    branch_grad, first_gain, first_shift, firstup_grad, firstdown_grad = feed_backward(
        0.5 * grad_first, first_stored, firstup_full, firstdown_full
    )
    frames_grad = grad_first + branch_grad
    table_grad = lax.dot_general(
        language_hot, frames_grad, (((0,), (0,)), ((), ())), precision=lax.Precision.HIGHEST
    )
    gain_stack = jnp.stack(
        [first_gain, attend_gain, outer_gain, inner_gain, second_gain, final_gain]
    )
    shift_stack = jnp.stack(
        [first_shift, attend_shift, outer_shift, inner_shift, second_shift, final_shift]
    )
    table_sum, gain_sum, shift_sum, taps_sum = sum_small(
        place, sizes, [table_grad, gain_stack, shift_stack, taps_grad]
    )
    (seconddown_sum,) = weight_grads(place, sizes, [seconddown_grad], False)
    (secondup_sum,) = weight_grads(place, sizes, [secondup_grad], True)
    pointwise_sum, gating_sum = weight_grads(place, sizes, [pointwise_grad, gating_grad], False)
    merger_sum, projection_sum = weight_grads(place, sizes, [merger_grad, projection_grad], True)
    (firstdown_sum,) = weight_grads(place, sizes, [firstdown_grad], False)
    (firstup_sum,) = weight_grads(place, sizes, [firstup_grad], True)
    return (
        encoded.astype(jnp.bfloat16),
        frames_grad,
        table_sum,
        gain_sum,
        shift_sum,
        firstup_sum,
        firstdown_sum,
        projection_sum,
        merger_sum,
        gating_sum,
        taps_sum,
        pointwise_sum,
        secondup_sum,
        seconddown_sum,
    )


def solution(mesh):
    dp_size, fsdp_size = mesh.shape["dp"], mesh.shape["fsdp"]
    layers = fsdp_size // 2
    split = Mesh(mesh.devices.reshape(dp_size, layers, 2), ("dp", "z", "core"))
    return jax.shard_map(
        functools.partial(shards, (dp_size, layers)),
        mesh=split,
        in_specs=(
            P(("dp", "z", "core"), None),
            P(("dp", "z", "core"), None),
            P(("dp", "z", "core"), None),
            P(None, ("z", "core")),
            P(None, ("z", "core")),
            P(None, ("z", "core")),
            P(("z", "core"), None),
            P(("z", "core"), None),
            P(("z", "core"), None),
            P(("z", "core"), None),
            P(("z", "core"), None),
            P(None, ("z", "core")),
            P(("z", "core"), None),
            P(("z", "core"), None),
            P(("z", "core"), None),
            P(("dp", "z", "core"), None),
        ),
        out_specs=(
            P(("dp", "z", "core"), None),
            P(("dp", "z", "core"), None),
            P(None, ("z", "core")),
            P(None, ("z", "core")),
            P(None, ("z", "core")),
            P(("z", "core"), None),
            P(("z", "core"), None),
            P(("z", "core"), None),
            P(("z", "core"), None),
            P(("z", "core"), None),
            P(None, ("z", "core")),
            P(("z", "core"), None),
            P(("z", "core"), None),
            P(("z", "core"), None),
        ),
        check_vma=False,
    )
```

time: 1400 us -> 2520 us (1.80)
  Pallas kernels: 0 us -> 1630 us
  waiting for transfers between devices: 1100 us -> 609 us
  matrix products: 130 us -> 69.3 us
  blocking collectives: 75.2 us -> 16.7 us
  starting transfers between devices: 1.63 us -> 58.1 us
  local copies, waits for them, and re-layouts: 32.7 us -> 69.8 us
    pallas_call x0 -> x34, Pallas kernels: none -> 1630 us  [the longest x4 1470 us: assemble(): pl.pallas_call(functools.partial(assemble_kernel, layers, widths), out_sh...]
    reduce_scatter x8 -> x6, waiting for transfers between devices: 464 us -> 4.68 us  [weight_grads(): summed = lax.psum_scatter(own, 'z', scatter_dimension=0, tiled=True)]
    ppermute x0 -> x68, waiting for transfers between devices: none -> 380 us  [the longest x42 378 us: swap_dp(): return lax.ppermute(value, 'dp', [(i, i ^ 1 << bit) for i in range(size)])]
    all_gather x8 -> x4, waiting for transfers between devices: 387 us -> 116 us  [gather_weights(): gathered.append(lax.all_gather(mine, ('z', 'core'), axis=0, tiled=False))]
    unnamed x25 -> x11, waiting for transfers between devices: 128 us -> 0.18 us
    ppermute x0 -> x68, starting transfers between devices: none -> 57.6 us  [the longest x42 52.6 us: swap_dp(): return lax.ppermute(value, 'dp', [(i, i ^ 1 << bit) for i in range(size)])]
    dot_general x16 -> x8, matrix products: 86.3 us -> 36.9 us  [rows_dot(): return jnp.dot(inputs, weight, preferred_element_type=jnp.float32)]
    all_gather x4 -> x1, blocking collectives: 56.9 us -> 16.7 us  [gather_small(): full = lax.all_gather(packed, ('z', 'core'), axis=0, tiled=False)]
  transfers between devices with their start and end apart: 21 -> 79, of which waited for: 19 -> 27; matrix products, arithmetic and copies ran while one was open for 10% -> 4% of each run, Pallas kernels for 0% -> 44%
where the time goes in v1:
time: 2520 us; the launch traced here: 2510 us
  Pallas kernels  1630 us (65%)
  waiting for transfers between devices  609 us (24%)
  local copies, waits for them, and re-layouts  69.8 us (3%)
  matrix products  69.3 us (3%)
  starting transfers between devices  58.1 us (2%)
  other arithmetic  35.3 us (1%)
    pallas_call x4, Pallas kernels, assemble(): pl.pallas_call(functools.partial(assemble_kernel, layers, widths), out_sh...  1470 us
    ppermute x42, waiting for transfers between devices, swap_dp(): return lax.ppermute(value, 'dp', [(i, i ^ 1 << bit) for i in range(size)])  378 us
    pallas_call x24, Pallas kernels, weight_terms(): pl.pallas_call(functools.partial(weight_terms_kernel, widths, wanted, who...  148 us
    all_gather x4, waiting for transfers between devices, gather_weights(): gathered.append(lax.all_gather(mine, ('z', 'core'), axis=0, tiled=False))  116 us
    psum x1, waiting for transfers between devices, sum_small(): total = lax.psum(packed, ('dp', 'z', 'core'))  108 us
    ppermute x42, starting transfers between devices, swap_dp(): return lax.ppermute(value, 'dp', [(i, i ^ 1 << bit) for i in range(size)])  52.6 us
  transfers between devices with their start and end apart: 79, of which 27 were waited for; matrix products, arithmetic and copies ran while one was open for 4% of the time, Pallas kernels for 44%

profile of v1, /device:TPU:0, one launch (start us, length us, event | category | flops | bytes accessed | tf_op | source)
XLA Modules:
  0.0 2508.8 jit_solution(16477908026093409751)
XLA Ops:
  19.6 16.7 all-gather
  44.1 30.8 %all-gather.16.cloned.1.call-done = bf16[1024,1024]{1,0:T(8,128)(2,1)} async-done(((bf16[128,1024]{1,0:T(8,128)(2,1)}), bf16[1024,1024]{1,0:T(8,128)(2,1)}) %all-gather.16.cloned.1.call-update) | async-done | bytes 2097168 | tf_op jit(solution)/shard_map/all_gather | solution.py:259
  83.0 36.3 %all-gather.12.cloned.1.call-done = bf16[1024,1792]{1,0:T(8,128)(2,1)} async-done(((bf16[128,1792]{1,0:T(8,128)(2,1)}), bf16[1024,1792]{1,0:T(8,128)(2,1)}) %all-gather.12.cloned.1.call-update) | async-done | bytes 3670032 | tf_op jit(solution)/shard_map/all_gather | solution.py:259
  125.1 42.2 %all-gather.14.cloned.1.call-done = bf16[1024,2048]{1,0:T(8,128)(2,1)} async-done(((bf16[128,2048]{1,0:T(8,128)(2,1)}), bf16[1024,2048]{1,0:T(8,128)(2,1)}) %all-gather.14.cloned.1.call-update) | async-done | bytes 4194320 | tf_op jit(solution)/shard_map/all_gather | solution.py:259
  175.0 15.5 collective-permute-done.28.refs_5_
  194.3 30.0 %collective-permute-done.19.refs_9_ = bf16[3,128,2048]{2,1,0:T(8,128)(2,1)} collective-permute-done((bf16[3,128,2048]{2,1,0:T(8,128)(2,1)}, bf16[3,128,2048]{2,1,0:T(8,128)(2,1)}, u32[]{:S(2)}, u32[]{:S(2)}) %collective-permute-start.19) | collective-permute-done | bytes 1572896 | tf_op jit(solution)/shard_map/ppermute | solution.py:84
  226.7 27.1 %collective-permute-done.9.refs_5_ = bf16[3,128,1792]{2,1,0:T(8,128)(2,1)} collective-permute-done((bf16[3,128,1792]{2,1,0:T(8,128)(2,1)}, bf16[3,128,1792]{2,1,0:T(8,128)(2,1)}, u32[]{:S(2)}, u32[]{:S(2)}) %collective-permute-start.9) | collective-permute-done | bytes 1376288 | tf_op jit(solution)/shard_map/ppermute | solution.py:84
  253.8 28.8 %collective-permute-done.11.refs_7_ = bf16[3,128,1792]{2,1,0:T(8,128)(2,1)} collective-permute-done((bf16[3,128,1792]{2,1,0:T(8,128)(2,1)}, bf16[3,128,1792]{2,1,0:T(8,128)(2,1)}, u32[]{:S(2)}, u32[]{:S(2)}) %collective-permute-start.11) | collective-permute-done | bytes 1376288 | tf_op jit(solution)/shard_map/ppermute | solution.py:84
  284.2 256.1 %shard_map.266 = bf16[8,128,4096]{2,1,0:T(8,128)(2,1)} custom-call(s32[3]{0:T(128)} %pad_add_fusion.5.place, bf16[128,4096]{1,0:T(8,128)(2,1)} %refs_0_.4, bf16[128,4096]{1,0:T(8,128)(2,1)} %collective-permute-done.refs_1_, bf16[8,128,1024]{2,1,0:T(8,128)(2,1)} %bitcast.271, bf16[3,128,1024]{2,1,0:T(8,128)(2,1)} %collective-permute-done.1.refs_3_, ...), custom_call_target="tpu_custom_call" | custom-call | tf_op jit(solution)/shard_map/pallas_call | solution.py:135
  540.3 256.1 %shard_map.269 = bf16[8,128,4096]{2,1,0:T(8,128)(2,1)} custom-call(s32[3]{0:T(128)} %pad_add_fusion.5.place, bf16[128,4096]{1,0:T(8,128)(2,1)} %refs_0_.7, bf16[128,4096]{1,0:T(8,128)(2,1)} %collective-permute-done.25.refs_1_, bf16[8,128,1024]{2,1,0:T(8,128)(2,1)} %bitcast.273, bf16[3,128,1024]{2,1,0:T(8,128)(2,1)} %collective-permute-done.26.refs_3_, ...), custom_call_target="tpu_custom_call" | custom-call | tf_op jit(solution)/shard_map/pallas_call | solution.py:135
  796.5 7.8 multiply_convert_fusion.1
  805.9 446.9 %shard_map.267 = (bf16[8,128,4096]{2,1,0:T(8,128)(2,1)}, bf16[8,128,3072]{2,1,0:T(8,128)(2,1)}) custom-call(s32[3]{0:T(128)} %pad_add_fusion.5.place, bf16[128,4096]{1,0:T(8,128)(2,1)} %refs_0_.5, bf16[128,3072]{1,0:T(8,128)(2,1)} %refs_1_.2, bf16[128,4096]{1,0:T(8,128)(2,1)} %collective-permute-done.7.refs_2_, ...), custom_call_target="tpu_custom_call" | custom-call | tf_op jit(solution)/shard_map/pallas_call | solution.py:135
  1252.8 8.8 copy.100
  1276.9 510.9 %shard_map.268 = (bf16[8,128,1024]{2,1,0:T(8,128)(2,1)}, bf16[8,128,2048]{2,1,0:T(8,128)(2,1)}, bf16[8,128,1024]{2,1,0:T(8,128)(2,1)}, bf16[8,128,4096]{2,1,0:T(8,128)(2,1)}) custom-call(s32[3]{0:T(128)} %pad_add_fusion.5.place, bf16[128,1024]{1,0:T(8,128)(2,1)} %refs_0_.6, bf16[128,2048]{1,0:T(8,128)(2,1)} %refs_1_.3, bf16[128,1024]{1,0:T(8,128)(2,1)} %refs_2_.1, ...), custom_call_target="tpu_custom_call" | custom-call | tf_op jit(solution)/shard_map/pallas_call | solution.py:135
  1803.6 8.0 multiply_convert_fusion
  1911.9 8.1 fusion.5.refs_1_
  1920.1 11.3 collective-permute-done.51.refs_5_
  1944.8 10.3 collective-permute-done.52.refs_6_
  1984.4 63.2 %collective-permute-done.64.refs_4_ = bf16[1,512,1024]{2,1,0:T(8,128)(2,1)} collective-permute-done((bf16[1,512,1024]{2,1,0:T(8,128)(2,1)}, bf16[1,512,1024]{2,1,0:T(8,128)(2,1)}, u32[]{:S(2)}, u32[]{:S(2)}) %collective-permute-start.64) | collective-permute-done | bytes 1048608 | tf_op jit(solution)/shard_map/ppermute | solution.py:84
  2081.1 61.8 %collective-permute-done.58.refs_4_ = bf16[1,512,1024]{2,1,0:T(8,128)(2,1)S(1)} collective-permute-done((bf16[1,512,1024]{2,1,0:T(8,128)(2,1)}, bf16[1,512,1024]{2,1,0:T(8,128)(2,1)S(1)}, u32[]{:S(2)}, u32[]{:S(2)}) %collective-permute-start.58) | collective-permute-done | bytes 1048608 | tf_op jit(solution)/shard_map/ppermute | solution.py:84
  2163.7 62.5 %collective-permute-done.40.refs_4_ = bf16[1,512,1024]{2,1,0:T(8,128)(2,1)} collective-permute-done((bf16[1,512,1024]{2,1,0:T(8,128)(2,1)}, bf16[1,512,1024]{2,1,0:T(8,128)(2,1)}, u32[]{:S(2)}, u32[]{:S(2)}) %collective-permute-start.40) | collective-permute-done | bytes 1048608 | tf_op jit(solution)/shard_map/ppermute | solution.py:84
  2248.6 22.3 collective-permute-done.34.refs_4_
  2292.4 21.9 collective-permute-done.46.refs_6_
  2371.5 108.3 %all-reduce.21.cloned.1.call-done = f32[119,1024]{1,0:T(8,128)} async-done(((f32[119,1024]{1,0:T(8,128)}), f32[119,1024]{1,0:T(8,128)}) %all-reduce.21.cloned.1.call-update) | async-done | bytes 487440 | tf_op jit(solution)/shard_map/psum | solution.py:335
  (613 shorter events, 400.6 us)
Async XLA Ops:
  13.6 153.8 %all-gather.14.cloned.1.call-start = ((), (), s32[]{:S(2)}) async-start(), calls=%async_computation.15 | async-start | bytes 4718592 | tf_op jit(solution)/shard_map/all_gather | solution.py:259
  18.2 2303.2 %reduce-scatter.13.cloned.1.call-start = ((), (), s32[]{:S(2)}) async-start(), calls=%async_computation.10 | async-start | bytes 983040 | tf_op jit(solution)/shard_map/reduce_scatter | solution.py:306
  192.8 611.5 %collective-permute-start.20 = (bf16[3,128,2048]{2,1,0:T(8,128)(2,1)}, bf16[3,128,2048]{2,1,0:T(8,128)(2,1)}, u32[]{:S(2)}, u32[]{:S(2)}) collective-permute-start(bf16[3,128,2048]{2,1,0:T(8,128)(2,1)} %pad_maximum_fusion), channel_id=1, source_target_pairs={{0,16},{8,24},{16,0},{24,8},{1,17},{9,25},{17,1},{25,9},{2,18},{10... | collective-permute-start | bytes 4718600 | tf_op jit(solution)/shard_map/ppermute | solution.py:84
  224.3 581.0 %collective-permute-start.21 = (bf16[3,128,2048]{2,1,0:T(8,128)(2,1)}, bf16[3,128,2048]{2,1,0:T(8,128)(2,1)}, u32[]{:S(2)}, u32[]{:S(2)}) collective-permute-start(bf16[3,128,2048]{2,1,0:T(8,128)(2,1)} %collective-permute-done.19.refs_9_), channel_id=1, source_target_pairs={{0,16},{8,24},{16,0},{24,8},{1,17},{9,25},{17,1},{25,9},{2,18},{10... | collective-permute-start | bytes 4718600 | tf_op jit(solution)/shard_map/ppermute | solution.py:84
  225.8 579.0 %collective-permute-start.13 = (bf16[3,128,1792]{2,1,0:T(8,128)(2,1)}, bf16[3,128,1792]{2,1,0:T(8,128)(2,1)}, u32[]{:S(2)}, u32[]{:S(2)}) collective-permute-start(bf16[3,128,1792]{2,1,0:T(8,128)(2,1)} %collective-permute-done.10.refs_6_), channel_id=1, source_target_pairs={{0,1},{1,0},{2,3},{3,2},{4,5},{5,4},{6,7},{7,6},{8,9},{9,8},{10,11... | collective-permute-start | bytes 4128776 | tf_op jit(solution)/shard_map/ppermute | solution.py:88
  253.8 551.1 %collective-permute-start.12 = (bf16[3,128,1792]{2,1,0:T(8,128)(2,1)}, bf16[3,128,1792]{2,1,0:T(8,128)(2,1)}, u32[]{:S(2)}, u32[]{:S(2)}) collective-permute-start(bf16[3,128,1792]{2,1,0:T(8,128)(2,1)} %collective-permute-done.9.refs_5_), channel_id=1, source_target_pairs={{0,1},{1,0},{2,3},{3,2},{4,5},{5,4},{6,7},{7,6},{8,9},{9,8},{10,11... | collective-permute-start | bytes 4128776 | tf_op jit(solution)/shard_map/ppermute | solution.py:88
  282.6 522.8 %collective-permute-start.14 = (bf16[3,128,1792]{2,1,0:T(8,128)(2,1)}, bf16[3,128,1792]{2,1,0:T(8,128)(2,1)}, u32[]{:S(2)}, u32[]{:S(2)}) collective-permute-start(bf16[3,128,1792]{2,1,0:T(8,128)(2,1)} %collective-permute-done.11.refs_7_), channel_id=1, source_target_pairs={{0,1},{1,0},{2,3},{3,2},{4,5},{5,4},{6,7},{7,6},{8,9},{9,8},{10,11... | collective-permute-start | bytes 4128776 | tf_op jit(solution)/shard_map/ppermute | solution.py:88
  804.3 467.0 %collective-permute-start.15 = (bf16[128,1024]{1,0:T(8,128)(2,1)}, bf16[128,1024]{1,0:T(8,128)(2,1)}, u32[]{:S(2)}, u32[]{:S(2)}) collective-permute-start(bf16[128,1024]{1,0:T(8,128)(2,1)} %refs_0_.6), channel_id=1, source_target_pairs={{0,1},{1,0},{2,3},{3,2},{4,5},{5,4},{6,7},{7,6},{8,9},{9,8},{10,11... | collective-permute-start | bytes 786440 | tf_op jit(solution)/shard_map/ppermute | solution.py:88
  804.8 468.5 %collective-permute-start.17 = (bf16[128,1024]{1,0:T(8,128)(2,1)}, bf16[128,1024]{1,0:T(8,128)(2,1)}, u32[]{:S(2)}, u32[]{:S(2)}) collective-permute-start(bf16[128,1024]{1,0:T(8,128)(2,1)} %refs_2_.1), channel_id=1, source_target_pairs={{0,1},{1,0},{2,3},{3,2},{4,5},{5,4},{6,7},{7,6},{8,9},{9,8},{10,11... | collective-permute-start | bytes 786440 | tf_op jit(solution)/shard_map/ppermute | solution.py:88
  804.9 472.0 %collective-permute-start.22 = (bf16[3,128,2048]{2,1,0:T(8,128)(2,1)}, bf16[3,128,2048]{2,1,0:T(8,128)(2,1)}, u32[]{:S(2)}, u32[]{:S(2)}) collective-permute-start(bf16[3,128,2048]{2,1,0:T(8,128)(2,1)} %collective-permute-done.19.refs_9_), channel_id=1, source_target_pairs={{0,1},{1,0},{2,3},{3,2},{4,5},{5,4},{6,7},{7,6},{8,9},{9,8},{10,11... | collective-permute-start | bytes 4718600 | tf_op jit(solution)/shard_map/ppermute | solution.py:88
  805.4 471.4 %collective-permute-start.23 = (bf16[3,128,2048]{2,1,0:T(8,128)(2,1)}, bf16[3,128,2048]{2,1,0:T(8,128)(2,1)}, u32[]{:S(2)}, u32[]{:S(2)}) collective-permute-start(bf16[3,128,2048]{2,1,0:T(8,128)(2,1)} %collective-permute-done.20.refs_10_), channel_id=1, source_target_pairs={{0,1},{1,0},{2,3},{3,2},{4,5},{5,4},{6,7},{7,6},{8,9},{9,8},{10,11... | collective-permute-start | bytes 4718600 | tf_op jit(solution)/shard_map/ppermute | solution.py:88
  805.4 471.5 %collective-permute-start.24 = (bf16[3,128,2048]{2,1,0:T(8,128)(2,1)}, bf16[3,128,2048]{2,1,0:T(8,128)(2,1)}, u32[]{:S(2)}, u32[]{:S(2)}) collective-permute-start(bf16[3,128,2048]{2,1,0:T(8,128)(2,1)} %collective-permute-done.21.refs_11_), channel_id=1, source_target_pairs={{0,1},{1,0},{2,3},{3,2},{4,5},{5,4},{6,7},{7,6},{8,9},{9,8},{10,11... | collective-permute-start | bytes 4718600 | tf_op jit(solution)/shard_map/ppermute | solution.py:88
  1905.0 160.9 %collective-permute-start.38 = (bf16[512,4096]{1,0:T(8,128)(2,1)}, bf16[512,4096]{1,0:T(8,128)(2,1)}, u32[]{:S(2)}, u32[]{:S(2)}) collective-permute-start(bf16[512,4096]{1,0:T(8,128)(2,1)} %shard_map.275), channel_id=1, source_target_pairs={{0,1},{1,0},{2,3},{3,2},{4,5},{5,4},{6,7},{7,6},{8,9},{9,8},{10,11... | collective-permute-start | bytes 12582920 | tf_op jit(solution)/shard_map/ppermute | solution.py:88
  1960.2 369.3 %reduce-scatter.17.cloned.1.call-start = ((), (), s32[]{:S(2)}) async-start(), calls=%async_computation.12 | async-start | bytes 1310720 | tf_op jit(solution)/shard_map/reduce_scatter | solution.py:306
  1970.5 179.4 %collective-permute-start.32 = (bf16[512,4096]{1,0:T(8,128)(2,1)}, bf16[512,4096]{1,0:T(8,128)(2,1)}, u32[]{:S(2)}, u32[]{:S(2)}) collective-permute-start(bf16[512,4096]{1,0:T(8,128)(2,1)} %shard_map.270), channel_id=1, source_target_pairs={{0,1},{1,0},{2,3},{3,2},{4,5},{5,4},{6,7},{7,6},{8,9},{9,8},{10,11... | collective-permute-start | bytes 12582920 | tf_op jit(solution)/shard_map/ppermute | solution.py:88
  2053.6 278.3 %reduce-scatter.15.cloned.1.call-start = ((), (), s32[]{:S(2)}) async-start(), calls=%async_computation.11 | async-start | bytes 1310720 | tf_op jit(solution)/shard_map/reduce_scatter | solution.py:306
  2065.9 166.4 %collective-permute-start.44 = (bf16[512,4096]{1,0:T(8,128)(2,1)}, bf16[512,4096]{1,0:T(8,128)(2,1)}, u32[]{:S(2)}, u32[]{:S(2)}) collective-permute-start(bf16[512,4096]{1,0:T(8,128)(2,1)} %shard_map.280), channel_id=1, source_target_pairs={{0,1},{1,0},{2,3},{3,2},{4,5},{5,4},{6,7},{7,6},{8,9},{9,8},{10,11... | collective-permute-start | bytes 12582920 | tf_op jit(solution)/shard_map/ppermute | solution.py:88
  2149.8 185.5 %reduce-scatter.9.cloned.1.call-start = ((), (), s32[]{:S(2)}) async-start(), calls=%async_computation.8 | async-start | bytes 1310720 | tf_op jit(solution)/shard_map/reduce_scatter | solution.py:306
  2321.4 158.4 %all-reduce.21.cloned.1.call-start = ((), (), s32[]{:S(2)}) async-start(), calls=%async_computation.6 | async-start | bytes 983040 | tf_op jit(solution)/shard_map/psum | solution.py:335
  2354.9 139.5 %collective-permute-start.36 = (bf16[128,1024]{1,0:T(8,128)(2,1)}, bf16[128,1024]{1,0:T(8,128)(2,1)S(1)}, u32[]{:S(2)}, u32[]{:S(2)}) collective-permute-start(bf16[128,1024]{1,0:T(8,128)(2,1)} %reduce-scatter.7.cloned.1.call-done.refs_0_), channel_id=1, source_target_pairs={{0,16},{8,24},{16,0},{24,8},{1,17},{9,25},{17,1},{25,9},{2,18},{10... | collective-permute-start | bytes 786440 | tf_op jit(solution)/shard_map/ppermute | solution.py:84
  2358.1 133.7 %collective-permute-start.43 = (bf16[128,1024]{1,0:T(8,128)(2,1)}, bf16[128,1024]{1,0:T(8,128)(2,1)}, u32[]{:S(2)}, u32[]{:S(2)}) collective-permute-start(bf16[128,1024]{1,0:T(8,128)(2,1)} %collective-permute-done.42.refs_2_), channel_id=1, source_target_pairs={{0,8},{8,0},{16,24},{24,16},{1,9},{9,1},{17,25},{25,17},{2,10},{10... | collective-permute-start | bytes 786440 | tf_op jit(solution)/shard_map/ppermute | solution.py:84
  2364.1 130.4 %collective-permute-start.37 = (bf16[128,1024]{1,0:T(8,128)(2,1)S(1)}, bf16[128,1024]{1,0:T(8,128)(2,1)}, u32[]{:S(2)}, u32[]{:S(2)}) collective-permute-start(bf16[128,1024]{1,0:T(8,128)(2,1)S(1)} %collective-permute-done.35.refs_1_), channel_id=1, source_target_pairs={{0,16},{8,24},{16,0},{24,8},{1,17},{9,25},{17,1},{25,9},{2,18},{10... | collective-permute-start | bytes 786440 | tf_op jit(solution)/shard_map/ppermute | solution.py:84
  2369.5 128.3 %collective-permute-start.48 = (bf16[128,1024]{1,0:T(8,128)(2,1)}, bf16[128,1024]{1,0:T(8,128)(2,1)S(1)}, u32[]{:S(2)}, u32[]{:S(2)}) collective-permute-start(bf16[128,1024]{1,0:T(8,128)(2,1)} %reduce-scatter.11.cloned.1.call-done.refs_0_), channel_id=1, source_target_pairs={{0,16},{8,24},{16,0},{24,8},{1,17},{9,25},{17,1},{25,9},{2,18},{10... | collective-permute-start | bytes 786440 | tf_op jit(solution)/shard_map/ppermute | solution.py:84
  2370.9 126.9 %collective-permute-start.49 = (bf16[128,1024]{1,0:T(8,128)(2,1)S(1)}, bf16[128,1024]{1,0:T(8,128)(2,1)S(1)}, u32[]{:S(2)}, u32[]{:S(2)}) collective-permute-start(bf16[128,1024]{1,0:T(8,128)(2,1)S(1)} %collective-permute-done.47.refs_1_), channel_id=1, source_target_pairs={{0,16},{8,24},{16,0},{24,8},{1,17},{9,25},{17,1},{25,9},{2,18},{10... | collective-permute-start | bytes 786440 | tf_op jit(solution)/shard_map/ppermute | solution.py:84
  (204 other events, 10947.9 us)
Sparse Core Ops, SparseCore 0:
  10.2 33.8 all-gather.9
  46.3 28.5 all-gather.15
  77.1 42.0 all-gather.11
  121.3 46.0 all-gather.13
  1960.3 22.0 reduce-scatter.12
  2053.7 25.8 reduce-scatter.16
  2150.0 26.0 reduce-scatter.14
  2232.4 25.9 reduce-scatter.8
  2277.9 25.1 reduce-scatter.6
  2321.5 26.1 reduce-scatter.10
  2355.0 124.7 all-reduce.20

commit v2 on v0

v2 whole, which is shorter than its diff:
```python
import functools

import jax
import jax.numpy as jnp
import numpy as np
from jax import lax
from jax.experimental import pallas as pl
from jax.experimental.pallas import tpu as pltpu
from jax.sharding import Mesh
from jax.sharding import PartitionSpec as P

HEAD_DIM = 128


def layout(lengths, languages, frame_count):
    utterances = jnp.arange(lengths.shape[-1], dtype=jnp.int32)
    earlier = utterances[:, None] <= utterances[None, :]
    finish = jnp.sum(jnp.where(earlier[None], lengths[:, :, None], 0), axis=1)
    begins = finish - lengths
    indices = jnp.arange(frame_count, dtype=jnp.int32)
    segment = jnp.sum((indices[None, :, None] >= finish[:, None, :]).astype(jnp.int32), axis=-1)
    owners = segment[:, :, None] == jnp.arange(lengths.shape[-1], dtype=jnp.int32)[None, None, :]
    first_row = jnp.sum(jnp.where(owners, begins[:, None, :], 0), axis=-1)
    language_row = jnp.sum(jnp.where(owners, languages[:, None, :], 0), axis=-1)
    return (segment, indices[None, :] - first_row, language_row)


def angles(position):
    half_dim = HEAD_DIM // 2
    frequency = 10000.0 ** (-jnp.arange(half_dim, dtype=jnp.float32) / half_dim)
    turned = position.astype(jnp.float32)[..., None] * frequency
    return (jnp.cos(turned)[..., None, :], jnp.sin(turned)[..., None, :])


VMEM_SPACE = pl.BlockSpec(memory_space=pltpu.VMEM)
SMEM_SPACE = pl.BlockSpec(memory_space=pltpu.SMEM)
ANY_SPACE = pl.BlockSpec(memory_space=pl.ANY)


class Order:
    def __init__(self, value):
        self.value = value

    def call(self, kernel, out_shape, in_specs, out_specs, scratch_shapes, operands, after=(), micros=8.0):
        count, outs, extra = len(operands), len(out_shape), len(after)
        held_in = [i for i in range(count) if in_specs[i] is VMEM_SPACE]
        held_out = [i for i in range(outs) if out_specs[i] is VMEM_SPACE]
        buffers = [pltpu.VMEM(operands[i].shape, operands[i].dtype) for i in held_in]
        buffers += [pltpu.VMEM(out_shape[i].shape, out_shape[i].dtype) for i in held_out]
        copies = max(1, len(held_in), len(held_out))
        needed = sum(
            int(np.prod(b.shape)) * np.dtype(b.dtype).itemsize
            for b in [*buffers, *scratch_shapes]
            if b.memory_space == pltpu.VMEM
        )

        def body(*refs):
            ins, rest = list(refs[:count]), refs[count + extra + 1 :]
            results, rest = list(rest[:outs]), rest[outs + 1 :]
            held, scratch, sems = rest[: len(buffers)], rest[len(buffers) : -1], rest[-1]
            moves = []
            for at, i in enumerate(held_in):
                moves.append(pltpu.make_async_copy(ins[i], held[at], sems.at[at]))
                moves[-1].start()
                ins[i] = held[at]
            targets = []
            for at, i in enumerate(held_out):
                targets.append(results[i])
                results[i] = held[len(held_in) + at]
            for move in moves:
                move.wait()
            kernel(*ins, *results, *scratch)
            moves = []
            for at, i in enumerate(held_out):
                moves.append(pltpu.make_async_copy(results[i], targets[at], sems.at[at]))
                moves[-1].start()
            for move in moves:
                move.wait()

        result = pl.pallas_call(
            body,
            out_shape=[*out_shape, jax.ShapeDtypeStruct(self.value.shape, self.value.dtype)],
            in_specs=[ANY_SPACE if s is VMEM_SPACE else s for s in in_specs]
            + [ANY_SPACE] * (extra + 1),
            out_specs=[ANY_SPACE] * (outs + 1),
            scratch_shapes=[*buffers, *scratch_shapes, pltpu.SemaphoreType.DMA((copies,))],
            input_output_aliases={count + extra: outs},
            compiler_params=pltpu.CompilerParams(vmem_limit_bytes=min(VMEM_LIMIT, needed + VMEM_SPARE)),
            cost_estimate=pl.CostEstimate(
                flops=1, bytes_accessed=int(micros * COST_SCALE), transcendentals=0
            ),
        )(*operands, *after, self.value)
        self.value = result[-1]
        return result[:-1]


COST_SCALE = 3.0e5
VMEM_LIMIT = 60 * 1024 * 1024
VMEM_SPARE = 16 * 1024 * 1024
QUARTERS = 4
LANES = 128
BITS = (0, 1)


def swap_dp(value, bit, size):
    return lax.ppermute(value, "dp", [(i, i ^ (1 << bit)) for i in range(size)])


def swap_core(value):
    return lax.ppermute(value, "core", [(0, 1), (1, 0)])


def last_bit(index, order):
    return [bit for bit in order if index >> bit & 1][-1]


def pick_kernel(layers, place, gathered, out, sems):
    layer, core = place[1], place[2]
    copies = []
    for k in range(1, layers):
        row = lax.rem(layer + k, layers) * 2 + core
        copies.append(pltpu.make_async_copy(gathered.at[row], out.at[k - 1], sems.at[k - 1]))
        copies[-1].start()
    for copy in copies:
        copy.wait()


def pick(order, place, layers, gathered, after):
    _, rows, width = gathered.shape
    return order.call(
        functools.partial(pick_kernel, layers),
        [jax.ShapeDtypeStruct((layers - 1, rows, width), gathered.dtype)],
        [SMEM_SPACE, ANY_SPACE],
        [VMEM_SPACE],
        [pltpu.SemaphoreType.DMA((layers - 1,))],
        [place, gathered],
        after,
        3.0,
    )[0]


class Factors:
    def __init__(self, left, right):
        self.rights = list(right) if isinstance(right, (list, tuple)) else [right]
        self.split = len(self.rights) > 1
        self.width = sum(r.shape[1] for r in self.rights)
        self.tokens = left.shape[0]
        self.operands = [left, swap_core(left)]
        self.rest = [*self.rights, *[swap_core(r) for r in self.rights]]

    def columns(self, refs, quarter, r, start, tile):
        part = self.width // QUARTERS
        count = len(self.rights)
        if self.split:
            column = pl.ds(start, tile)
            return [refs[r].at[:, column], refs[count + r].at[:, column]]
        column = pl.ds(pl.multiple_of((quarter ^ r) * part + start, tile), tile)
        return [refs[0].at[:, column], refs[1].at[:, column]]


def own_rows(ref, layers, core):
    tokens, features = ref.shape
    rows = features // (2 * layers)
    if rows % LANES == 0:
        blocks = [
            ref[:, pl.ds(pl.multiple_of((2 * k + core) * rows, rows), rows)] for k in range(layers)
        ]
        return jnp.concatenate(blocks, axis=1).T
    turned = ref[...].T.reshape(layers, 2, rows, tokens)
    return jnp.where(core == 0, turned[:, 0], turned[:, 1]).reshape(layers * rows, tokens)


def weight_terms_kernel(layers, factors, tile, wanted, given, place, *refs):
    lefts, at = [], 0
    for f in factors:
        lefts.append(refs[at : at + 2])
        at += 2
    rights = []
    for f in factors:
        rights.append(refs[at : at + len(f.rest)])
        at += len(f.rest)
    sums = []
    for holds in given:
        sums.append(dict(zip(holds, refs[at : at + len(holds)])))
        at += len(holds)
    outs, buffers = refs[at : at + len(wanted)], refs[at + len(wanted) :]
    right_buffer, add_buffer, out_buffer, in_sems, out_sems = buffers
    quarter, core = place[0], place[2]
    jobs, base = [], 0
    for i, f in enumerate(factors):
        part = f.width // QUARTERS
        for number, r in enumerate(wanted):
            for start in range(0, part, tile):
                narrow = pl.ds(base + start, tile)
                jobs.append(
                    (
                        i,
                        f.columns(rights[i], quarter, r, start, tile),
                        [held[r].at[:, narrow] for held in sums if r in held],
                        outs[number].at[:, narrow],
                    )
                )
        base += part
    loads = []
    for number, (i, columns, adds, _) in enumerate(jobs):
        tokens = factors[i].tokens
        moves = [
            (column, right_buffer.at[number, k * tokens : (k + 1) * tokens])
            for k, column in enumerate(columns)
        ]
        moves += [(ref, add_buffer.at[number, k]) for k, ref in enumerate(adds)]
        started = []
        for k, (source, target) in enumerate(moves):
            started.append(pltpu.make_async_copy(source, target, in_sems.at[number, k]))
            started[-1].start()
        loads.append(started)
    stores = []
    for number, (i, _, adds, target) in enumerate(jobs):
        tokens = factors[i].tokens
        if number == 0 or jobs[number - 1][0] != i:
            left = jnp.concatenate([own_rows(ref, layers, core) for ref in lefts[i]], axis=1)
        for copy in loads[number]:
            copy.wait()
        product = jnp.dot(
            left, right_buffer[number, : 2 * tokens], preferred_element_type=jnp.float32
        )
        for k in range(len(adds)):
            product += add_buffer[number, k].astype(jnp.float32)
        out_buffer[number] = product.astype(jnp.bfloat16)
        copy = pltpu.make_async_copy(out_buffer.at[number], target, out_sems.at[number])
        copy.start()
        stores.append(copy)
    for copy in stores:
        copy.wait()


def weight_terms(order, place, layers, factors, wanted, sums, given):
    height = factors[0].operands[0].shape[1] // 2
    tokens = 2 * max(f.tokens for f in factors)
    tile = int(np.gcd.reduce([512] + [f.width // QUARTERS for f in factors]))
    width = sum(f.width for f in factors) // QUARTERS
    count = len(wanted) * width // tile
    depth = max(1, len(sums))
    lefts = [o for f in factors for o in f.operands]
    rest = [o for f in factors for o in f.rest] + [a for each in sums for a in each]
    return order.call(
        functools.partial(weight_terms_kernel, layers, factors, tile, wanted, given),
        [jax.ShapeDtypeStruct((height, width), jnp.bfloat16)] * len(wanted),
        [SMEM_SPACE] + [VMEM_SPACE] * len(lefts) + [ANY_SPACE] * len(rest),
        [ANY_SPACE] * len(wanted),
        [
            pltpu.VMEM((count, tokens, tile), jnp.bfloat16),
            pltpu.VMEM((count if sums else 1, depth, height, tile), jnp.bfloat16),
            pltpu.VMEM((count, height, tile), jnp.bfloat16),
            pltpu.SemaphoreType.DMA((count, depth + 2)),
            pltpu.SemaphoreType.DMA((count,)),
        ],
        [place, *lefts, *rest],
        (),
        5.0,
    )


def spread_kernel(widths, place, *refs):
    pieces, outs = refs[:QUARTERS], refs[QUARTERS:]
    quarter = place[0]
    base = 0
    for i, width in enumerate(widths):
        part = width // QUARTERS
        for r in range(QUARTERS):
            column = pl.ds(pl.multiple_of((quarter ^ r) * part, part), part)
            outs[i][:, column] = pieces[r][:, pl.ds(base, part)].astype(jnp.float32)
        base += part


def spread(order, place, widths, pieces):
    rows = pieces[0].shape[0]
    return order.call(
        functools.partial(spread_kernel, widths),
        [jax.ShapeDtypeStruct((rows, w), jnp.float32) for w in widths],
        [SMEM_SPACE] + [VMEM_SPACE] * QUARTERS,
        [VMEM_SPACE] * len(widths),
        [],
        [place, *pieces],
        (),
        3.0,
    )


class Gather:
    def __init__(self, place, sizes, order, group):
        self.place, self.order, self.group = place, order, group
        self.dp_size, self.layers = sizes
        self.other = [swap_core(w) for w in group]

    def begin(self):
        quarter = self.place[0]
        mine = jnp.concatenate(
            [
                lax.dynamic_slice_in_dim(w, quarter * (w.shape[1] // QUARTERS), w.shape[1] // QUARTERS, 1)
                for w in self.group
            ],
            axis=1,
        )
        self.gathered = lax.all_gather(mine, ("z", "core"), axis=0, tiled=False)

    def exchange(self, flip, after=()):
        held = {0: pick(self.order, self.place, self.layers, self.gathered, after)}
        order = BITS[::-1] if flip else BITS
        for r in range(1, QUARTERS):
            bit = last_bit(r, order)
            held[r] = swap_dp(held[r ^ (1 << bit)], bit, self.dp_size)
        self.pieces = [held[r] for r in range(1, QUARTERS)]
        self.others = [swap_core(piece) for piece in self.pieces]


class Scatter:
    def __init__(self, place, sizes, order, flip):
        self.place, self.order = place, order
        self.dp_size, self.layers = sizes
        self.first, self.second = BITS[::-1] if flip else BITS

    def terms(self, wanted, sums, given):
        return weight_terms(self.order, self.place, self.layers, self.factors, wanted, sums, given)

    def halves(self, *factors):
        self.factors = factors
        self.widths = [f.width for f in factors]
        sent = [r for r in range(QUARTERS) if r >> self.first & 1]
        self.held = [r ^ (1 << self.first) for r in sent]
        away = self.terms(sent, (), ())
        self.sums = [swap_dp(part, self.first, self.dp_size) for part in away]

    def quarters(self):
        (part,) = self.terms([1 << self.second], (self.sums,), (self.held,))
        self.last = swap_dp(part, self.second, self.dp_size)

    def rows(self):
        (own,) = self.terms([0], (self.sums, [self.last]), (self.held, [0]))
        self.mine = lax.psum_scatter(own, "z", scatter_dimension=0, tiled=True)

    def share(self):
        summed = self.mine
        bit = len(BITS)
        while 1 << bit < self.dp_size:
            summed = summed + swap_dp(summed, bit, self.dp_size)
            bit += 1
        held = {0: summed}
        for r in range(1, QUARTERS):
            bit = last_bit(r, (self.first, self.second))
            held[r] = swap_dp(held[r ^ (1 << bit)], bit, self.dp_size)
        self.pieces = [held[r] for r in range(QUARTERS)]

    def spread(self):
        return spread(self.order, self.place, self.widths, self.pieces)


def gather_small(arrays):
    rows = [a.shape[0] for a in arrays]
    packed = jnp.concatenate(arrays, axis=0)
    packed = jnp.pad(packed, ((0, -packed.shape[0] % 16), (0, 0)))
    full = lax.all_gather(packed, ("z", "core"), axis=0, tiled=False)
    full = full.transpose(1, 0, 2).reshape(packed.shape[0], -1)
    pieces, start = [], 0
    for count in rows:
        pieces.append(full[start : start + count])
        start += count
    return pieces


def pack_small(table_hot, frames_grad, vectors):
    count = table_hot.shape[1]
    extra = -(frames_grad.shape[0] + vectors.shape[0]) % 16
    left = jnp.concatenate([frames_grad, vectors, jnp.zeros((extra, vectors.shape[1]), vectors.dtype)])
    used = count + vectors.shape[0]
    share = -(-used // QUARTERS)
    unit = jnp.eye(vectors.shape[0], dtype=table_hot.dtype)
    right = jnp.block(
        [
            [table_hot, jnp.zeros((table_hot.shape[0], vectors.shape[0]), table_hot.dtype)],
            [jnp.zeros((vectors.shape[0], count), table_hot.dtype), unit],
        ]
    )
    right = jnp.pad(right, ((0, extra), (0, share * QUARTERS - used)))
    right = right.reshape(right.shape[0], QUARTERS, share)
    right = jnp.pad(right, ((0, 0), (0, 0), (0, LANES - share)))
    return (
        left.astype(jnp.bfloat16),
        right.reshape(right.shape[0], QUARTERS * LANES).astype(jnp.bfloat16),
    )


def unpack_small(summed, counts):
    used = sum(counts)
    share = -(-used // QUARTERS)
    rows = summed.reshape(summed.shape[0], QUARTERS, LANES)[:, :, :share]
    rows = rows.reshape(summed.shape[0], QUARTERS * share).T
    pieces, start = [], 0
    for count in counts:
        pieces.append(rows[start : start + count])
        start += count
    return pieces

EPSILON = 1e-05
MASKED = -1000000000.0


def dot_rows(left, right):
    return jnp.dot(left, right, preferred_element_type=jnp.float32)


def dot_cols(left, right):
    return lax.dot_general(
        left, right, (((1,), (1,)), ((), ())), preferred_element_type=jnp.float32
    )


def dot_down(left, right):
    return jnp.dot(left.T, right, preferred_element_type=jnp.float32)


def standard(values):
    centred = values - jnp.mean(values, axis=-1, keepdims=True)
    spread = lax.rsqrt(jnp.mean(centred * centred, axis=-1, keepdims=True) + EPSILON)
    return centred * spread, spread


def norm_back(values, gradient, gain):
    shape, spread = standard(values)
    inner = gradient * gain
    back = spread * (
        inner
        - jnp.mean(inner, axis=-1, keepdims=True)
        - shape * jnp.mean(inner * shape, axis=-1, keepdims=True)
    )
    return (
        back,
        jnp.sum(gradient * shape, axis=0, keepdims=True),
        jnp.sum(gradient, axis=0, keepdims=True),
    )


def sigmoid(values):
    return 1.0 / (1.0 + jnp.exp(-values))


def silu_back(values, gradient):
    gate = sigmoid(values)
    return gradient * gate * (1.0 + values * (1.0 - gate))


class Pieces:
    def __init__(self, gather, index):
        group = gather.group
        self.layers = gather.layers
        self.base = sum(w.shape[1] for w in group[:index]) // QUARTERS
        self.rows, self.width = group[index].shape
        self.operands = [
            group[index],
            gather.other[index],
            gather.gathered,
            *gather.pieces,
            *gather.others,
        ]

    @property
    def part(self):
        return self.width // QUARTERS

    def quarters(self, tokens):
        return [jax.ShapeDtypeStruct((tokens, self.part), jnp.bfloat16)] * QUARTERS

    @property
    def scratch(self):
        copies = 1 + (QUARTERS - 1) * 2 * self.layers
        return [
            pltpu.VMEM((QUARTERS, 2 * self.layers, self.rows, self.part), jnp.bfloat16),
            pltpu.SemaphoreType.DMA((copies,)),
        ]

    def load(self, place, refs, buffer, sems):
        own, other, gathered = refs[:3]
        pieces, others = refs[3 : 2 + QUARTERS], refs[2 + QUARTERS :]
        quarter, layer, core = place[0], place[1], place[2]
        span = pl.ds(self.base, self.part)
        number, steps = 0, []
        for r in range(QUARTERS):
            index = quarter ^ r
            column = pl.ds(pl.multiple_of(index * self.part, self.part), self.part)
            moves = []
            if r == 0:
                moves.append((gathered.at[:, :, span], buffer.at[index]))
            else:
                for source, lane in ((own, core), (other, 1 - core)):
                    moves.append((source.at[:, column], buffer.at[index, 2 * layer + lane]))
                for source, lane in ((pieces[r - 1], core), (others[r - 1], 1 - core)):
                    for k in range(1, self.layers):
                        row = lax.rem(layer + k, self.layers) * 2 + lane
                        moves.append((source.at[k - 1, :, span], buffer.at[index, row]))
            copies = []
            for source, target in moves:
                copies.append(pltpu.make_async_copy(source, target, sems.at[number]))
                copies[-1].start()
                number += 1
            steps.append((index, copies))
        return steps

    def block(self, buffer, index):
        return buffer[index].reshape(2 * self.layers * self.rows, self.part)


def wait_all(steps):
    for _, copies in steps:
        for copy in copies:
            copy.wait()


def up_kernel(pieces, row, place, values, gains, shifts, *refs):
    weight, outs, (buffer, sems) = refs[: -4 - QUARTERS], refs[-4 - QUARTERS : -2], refs[-2:]
    hidden_out, expanded_out, active_outs = outs[0], outs[1], outs[2:]
    steps = pieces.load(place, weight, buffer, sems)
    shape, _ = standard(values[...])
    hidden = (shape * gains[row : row + 1] + shifts[row : row + 1]).astype(jnp.bfloat16)
    hidden_out[...] = hidden
    for r, (index, copies) in enumerate(steps):
        for copy in copies:
            copy.wait()
        expanded = dot_rows(hidden, pieces.block(buffer, index))
        expanded_out[r] = expanded
        active_outs[r][...] = (expanded * sigmoid(expanded)).astype(jnp.bfloat16)


def up_step(order, place, gather, index, row, values, gains, shifts):
    pieces = Pieces(gather, index)
    tokens, width = values.shape
    return order.call(
        functools.partial(up_kernel, pieces, row),
        [
            jax.ShapeDtypeStruct((tokens, width), jnp.bfloat16),
            jax.ShapeDtypeStruct((QUARTERS, tokens, pieces.part), jnp.float32),
            *pieces.quarters(tokens),
        ],
        [SMEM_SPACE] + [VMEM_SPACE] * 3 + [ANY_SPACE] * len(pieces.operands),
        [VMEM_SPACE] * (2 + QUARTERS),
        pieces.scratch,
        [place, values, gains, shifts, *pieces.operands],
    )


def down_sum(pieces, place, quarters, weight, buffer, sems):
    total = None
    for r, (index, copies) in enumerate(pieces.load(place, weight, buffer, sems)):
        for copy in copies:
            copy.wait()
        term = dot_cols(quarters[r][...], pieces.block(buffer, index))
        total = term if total is None else total + term
    return total


def down_kernel(pieces, place, values, *refs):
    active, weight, (out, buffer, sems) = refs[:QUARTERS], refs[QUARTERS:-3], refs[-3:]
    out[...] = values[...] + 0.5 * down_sum(pieces, place, active, weight, buffer, sems)


def down_step(order, place, gather, index, values, active):
    pieces = Pieces(gather, index)
    return order.call(
        functools.partial(down_kernel, pieces),
        [jax.ShapeDtypeStruct(values.shape, jnp.float32)],
        [SMEM_SPACE] + [VMEM_SPACE] * (1 + QUARTERS) + [ANY_SPACE] * len(pieces.operands),
        [VMEM_SPACE],
        pieces.scratch,
        [place, values, *active, *pieces.operands],
    )[0]


def last_kernel(pieces, row, place, values, cotangent, gains, shifts, *refs):
    active, weight, outs = refs[:QUARTERS], refs[QUARTERS:-7], refs[-7:]
    encoded, grad_out, low_out, gain_out, shift_out, buffer, sems = outs
    total = values[...] + 0.5 * down_sum(pieces, place, active, weight, buffer, sems)
    gain = gains[row : row + 1]
    shape, _ = standard(total)
    encoded[...] = (shape * gain + shifts[row : row + 1]).astype(jnp.bfloat16)
    back, gain_grad, shift_grad = norm_back(total, cotangent[...].astype(jnp.float32), gain)
    grad_out[...] = back
    low_out[...] = (0.5 * back).astype(jnp.bfloat16)
    gain_out[...] = gain_grad
    shift_out[...] = shift_grad


def vector_shapes(width, count=2):
    return [jax.ShapeDtypeStruct((1, width), jnp.float32)] * count


def last_step(order, place, gather, index, row, values, active, cotangent, gains, shifts):
    pieces = Pieces(gather, index)
    return order.call(
        functools.partial(last_kernel, pieces, row),
        [
            jax.ShapeDtypeStruct(values.shape, jnp.bfloat16),
            jax.ShapeDtypeStruct(values.shape, jnp.float32),
            jax.ShapeDtypeStruct(values.shape, jnp.bfloat16),
            *vector_shapes(values.shape[1]),
        ],
        [SMEM_SPACE] + [VMEM_SPACE] * (4 + QUARTERS) + [ANY_SPACE] * len(pieces.operands),
        [VMEM_SPACE] * 5,
        pieces.scratch,
        [place, values, cotangent, gains, shifts, *active, *pieces.operands],
    )


def down_back_kernel(pieces, place, gradient, expanded, *refs):
    weight, outs, (buffer, sems) = refs[: -2 - QUARTERS], refs[-2 - QUARTERS : -2], refs[-2:]
    for r, (index, copies) in enumerate(pieces.load(place, weight, buffer, sems)):
        for copy in copies:
            copy.wait()
        active_grad = dot_rows(gradient[...], pieces.block(buffer, index))
        outs[r][...] = silu_back(expanded[r], active_grad).astype(jnp.bfloat16)


def down_back_step(order, place, gather, index, gradient, expanded):
    pieces = Pieces(gather, index)
    return order.call(
        functools.partial(down_back_kernel, pieces),
        pieces.quarters(gradient.shape[0]),
        [SMEM_SPACE] + [VMEM_SPACE] * 2 + [ANY_SPACE] * len(pieces.operands),
        [VMEM_SPACE] * QUARTERS,
        pieces.scratch,
        [place, gradient, expanded, *pieces.operands],
    )


def into_norm_kernel(pieces, row, scale, place, values, residual, gains, *refs):
    gradient, refs = refs[:QUARTERS], refs[QUARTERS:]
    weight, (grad_out, low_out, gain_out, shift_out, buffer, sems) = refs[:-6], refs[-6:]
    hidden_grad = down_sum(pieces, place, gradient, weight, buffer, sems)
    back, gain_grad, shift_grad = norm_back(values[...], hidden_grad, gains[row : row + 1])
    total = residual[...] + back
    grad_out[...] = total
    low_out[...] = (scale * total).astype(jnp.bfloat16)
    gain_out[...] = gain_grad
    shift_out[...] = shift_grad


def into_norm_step(order, place, gather, index, row, scale, gradient, values, residual, gains):
    pieces = Pieces(gather, index)
    return order.call(
        functools.partial(into_norm_kernel, pieces, row, scale),
        [
            jax.ShapeDtypeStruct(values.shape, jnp.float32),
            jax.ShapeDtypeStruct(values.shape, jnp.bfloat16),
            *vector_shapes(values.shape[1]),
        ],
        [SMEM_SPACE] + [VMEM_SPACE] * (3 + QUARTERS) + [ANY_SPACE] * len(pieces.operands),
        [VMEM_SPACE] * 4,
        pieces.scratch,
        [place, values, residual, gains, *gradient, *pieces.operands],
    )


def whole_weight(pieces, place, weight, buffer, sems):
    wait_all(pieces.load(place, weight, buffer, sems))


def turn(values, cosine, sine):
    return values * cosine + pltpu.roll(values, HEAD_DIM // 2, 1) * sine


def masked_scores(query, key, matching):
    return jnp.where(matching, dot_cols(query, key), MASKED)


def head(index):
    return slice(index * HEAD_DIM, (index + 1) * HEAD_DIM)


def attend_kernel(pieces, row, place, values, gains, shifts, cosine, sine, down, across, *refs):
    weight, outs = refs[:-7], refs[-7:]
    hidden_out, turned_out, totals_out, mixed_out, projected, buffer, sems = outs
    steps = pieces.load(place, weight, buffer, sems)
    shape, _ = standard(values[...])
    hidden = (shape * gains[row : row + 1] + shifts[row : row + 1]).astype(jnp.bfloat16)
    hidden_out[...] = hidden
    for index, copies in steps:
        for copy in copies:
            copy.wait()
        column = pl.ds(pl.multiple_of(index * pieces.part, pieces.part), pieces.part)
        projected[:, column] = dot_rows(hidden, pieces.block(buffer, index))
    heads = pieces.width // (3 * HEAD_DIM)
    matching = down[...] == across[...]
    for h in range(heads):
        query = turn(projected[:, head(h)], cosine[...], sine[...]) * HEAD_DIM ** (-0.5)
        key = turn(projected[:, head(heads + h)], cosine[...], sine[...])
        query, key = query.astype(jnp.bfloat16), key.astype(jnp.bfloat16)
        value = projected[:, head(2 * heads + h)].astype(jnp.bfloat16)
        turned_out[:, head(h)] = query
        turned_out[:, head(heads + h)] = key
        turned_out[:, head(2 * heads + h)] = value
        scores = masked_scores(query, key, matching)
        highest = jnp.max(scores, axis=-1, keepdims=True)
        powers = jnp.exp(scores - highest)
        total = jnp.sum(powers, axis=-1, keepdims=True)
        totals_out[:, h : h + 1] = highest + jnp.log(total)
        probs = (powers / total).astype(jnp.bfloat16)
        mixed_out[:, head(h)] = dot_rows(probs, value).astype(jnp.bfloat16)


def attend_step(order, place, gather, index, row, values, gains, shifts, cosine, sine, down, across):
    pieces = Pieces(gather, index)
    tokens, width = values.shape
    heads = pieces.width // (3 * HEAD_DIM)
    return order.call(
        functools.partial(attend_kernel, pieces, row),
        [
            jax.ShapeDtypeStruct((tokens, width), jnp.bfloat16),
            jax.ShapeDtypeStruct((tokens, pieces.width), jnp.bfloat16),
            jax.ShapeDtypeStruct((tokens, heads), jnp.float32),
            jax.ShapeDtypeStruct((tokens, heads * HEAD_DIM), jnp.bfloat16),
        ],
        [SMEM_SPACE] + [VMEM_SPACE] * 7 + [ANY_SPACE] * len(pieces.operands),
        [VMEM_SPACE] * 4,
        [pltpu.VMEM((tokens, pieces.width), jnp.float32), *pieces.scratch],
        [place, values, gains, shifts, cosine, sine, down, across, *pieces.operands],
    )


def quarter_shapes(shape):
    return [jax.ShapeDtypeStruct((shape[0], shape[1] // QUARTERS), jnp.bfloat16)] * QUARTERS


def to_quarters(place, values, outs):
    part = values.shape[1] // QUARTERS
    for r, out in enumerate(outs):
        out[...] = values[:, pl.ds(pl.multiple_of((place[0] ^ r) * part, part), part)]


def attend_back_kernel(pieces, place, gradient, turned, totals, cosine, sine, down, across, *refs):
    weight, rest = refs[: -4 - QUARTERS], refs[-4 - QUARTERS :]
    outs, (out, mixed_grad, buffer, sems) = rest[:QUARTERS], rest[QUARTERS:]
    heads = turned.shape[1] // (3 * HEAD_DIM)
    whole_weight(pieces, place, weight, buffer, sems)
    total = None
    for index in range(QUARTERS):
        column = slice(index * pieces.part, (index + 1) * pieces.part)
        term = dot_cols(gradient[:, column], pieces.block(buffer, index))
        total = term if total is None else total + term
    mixed_grad[...] = total.astype(jnp.bfloat16)
    matching = down[...] == across[...]
    for h in range(heads):
        query = turned[:, head(h)]
        key = turned[:, head(heads + h)]
        value = turned[:, head(2 * heads + h)]
        gradient_h = mixed_grad[:, head(h)]
        probs = jnp.exp(masked_scores(query, key, matching) - totals[:, h : h + 1])
        value_grad = dot_down(probs.astype(jnp.bfloat16), gradient_h)
        probs_grad = dot_cols(gradient_h, value)
        inner = jnp.sum(probs * probs_grad, axis=-1, keepdims=True)
        score_grad = (probs * (probs_grad - inner)).astype(jnp.bfloat16)
        query_grad = dot_rows(score_grad, key) * HEAD_DIM ** (-0.5)
        key_grad = dot_down(score_grad, query)
        out[:, head(h)] = turn(query_grad, cosine[...], -sine[...]).astype(jnp.bfloat16)
        out[:, head(heads + h)] = turn(key_grad, cosine[...], -sine[...]).astype(jnp.bfloat16)
        out[:, head(2 * heads + h)] = value_grad.astype(jnp.bfloat16)
    to_quarters(place, out, outs)


def attend_back_step(order, place, gather, index, gradient, turned, totals, cosine, sine, down, across):
    pieces = Pieces(gather, index)
    return order.call(
        functools.partial(attend_back_kernel, pieces),
        quarter_shapes(turned.shape),
        [SMEM_SPACE] + [VMEM_SPACE] * 7 + [ANY_SPACE] * len(pieces.operands),
        [VMEM_SPACE] * QUARTERS,
        [
            pltpu.VMEM(turned.shape, jnp.bfloat16),
            pltpu.VMEM(gradient.shape, jnp.bfloat16),
            *pieces.scratch,
        ],
        [place, gradient, turned, totals, cosine, sine, down, across, *pieces.operands],
    )


def rows_sum(pieces, buffer, left, out):
    for index in range(QUARTERS):
        column = slice(index * pieces.part, (index + 1) * pieces.part)
        out[:, column] = dot_rows(left, pieces.block(buffer, index))


def shifted(values, amount):
    return values if amount == 0 else pltpu.roll(values, amount % values.shape[0], 0)


def merge_kernel(pieces, place, values, mixed, *refs):
    weight, (out, buffer, sems) = refs[:-3], refs[-3:]
    whole_weight(pieces, place, weight, buffer, sems)
    for index in range(QUARTERS):
        column = slice(index * pieces.part, (index + 1) * pieces.part)
        out[:, column] = values[:, column] + dot_rows(mixed[...], pieces.block(buffer, index))


def merge_step(order, place, gather, index, values, mixed):
    pieces = Pieces(gather, index)
    return order.call(
        functools.partial(merge_kernel, pieces),
        [jax.ShapeDtypeStruct(values.shape, jnp.float32)],
        [SMEM_SPACE] + [VMEM_SPACE] * 2 + [ANY_SPACE] * len(pieces.operands),
        [VMEM_SPACE],
        pieces.scratch,
        [place, values, mixed, *pieces.operands],
    )[0]


def conv_kernel(weights, row, place, values, gains, shifts, taps, keep, *refs):
    count = len(weights[0].operands)
    operands = [refs[i * count : (i + 1) * count] for i in range(len(weights))]
    rest = refs[len(weights) * count :]
    done_out, hidden_out, doubled_out, filtered_out, active_out = rest[:5]
    scratch = rest[5:]
    buffers = [scratch[2 * i : 2 * i + 2] for i in range(len(weights))]
    steps = [w.load(place, o, *b) for w, o, b in zip(weights, operands, buffers)]
    gating, pointwise = weights
    shape, _ = standard(values[...])
    hidden = (shape * gains[row : row + 1] + shifts[row : row + 1]).astype(jnp.bfloat16)
    hidden_out[...] = hidden
    wait_all(steps[0])
    rows_sum(gating, buffers[0][0], hidden, doubled_out)
    half = gating.width // 2
    gated = doubled_out[:, :half] * sigmoid(doubled_out[:, half:])
    reach = taps.shape[0] // 2
    filtered = None
    for k in range(taps.shape[0]):
        term = shifted(gated, reach - k) * keep[:, k : k + 1] * taps[k : k + 1]
        filtered = term if filtered is None else filtered + term
    filtered_out[...] = filtered
    shape, _ = standard(filtered)
    renormed = shape * gains[row + 1 : row + 2] + shifts[row + 1 : row + 2]
    active = (renormed * sigmoid(renormed)).astype(jnp.bfloat16)
    active_out[...] = active
    wait_all(steps[1])
    for index in range(QUARTERS):
        column = slice(index * pointwise.part, (index + 1) * pointwise.part)
        term = dot_rows(active, pointwise.block(buffers[1][0], index))
        done_out[:, column] = values[:, column] + term


def conv_step(order, place, gather, row, values, gains, shifts, taps, keep):
    weights = [Pieces(gather, i) for i in range(2)]
    tokens, width = values.shape
    operands = [o for w in weights for o in w.operands]
    return order.call(
        functools.partial(conv_kernel, weights, row),
        [
            jax.ShapeDtypeStruct((tokens, width), jnp.float32),
            jax.ShapeDtypeStruct((tokens, width), jnp.bfloat16),
            jax.ShapeDtypeStruct((tokens, weights[0].width), jnp.float32),
            jax.ShapeDtypeStruct((tokens, weights[0].width // 2), jnp.float32),
            jax.ShapeDtypeStruct((tokens, width), jnp.bfloat16),
        ],
        [SMEM_SPACE] + [VMEM_SPACE] * 5 + [ANY_SPACE] * len(operands),
        [VMEM_SPACE] * 5,
        [s for w in weights for s in w.scratch],
        [place, values, gains, shifts, taps, keep, *operands],
    )


def conv_back_kernel(pieces, row, place, gradient, filtered, doubled, gains, shifts, taps, keep, *refs):
    weight, rest = refs[: -6 - QUARTERS], refs[-6 - QUARTERS :]
    outs = rest[:QUARTERS]
    gain_out, shift_out, taps_out, doubled_grad, buffer, sems = rest[QUARTERS:]
    whole_weight(pieces, place, weight, buffer, sems)
    total = None
    for index in range(QUARTERS):
        column = slice(index * pieces.part, (index + 1) * pieces.part)
        term = dot_cols(gradient[:, column], pieces.block(buffer, index))
        total = term if total is None else total + term
    gain = gains[row : row + 1]
    shape, _ = standard(filtered[...])
    renormed = shape * gain + shifts[row : row + 1]
    back, gain_grad, shift_grad = norm_back(filtered[...], silu_back(renormed, total), gain)
    gain_out[...] = gain_grad
    shift_out[...] = shift_grad
    half = doubled.shape[1] // 2
    gate = sigmoid(doubled[:, half:])
    gated = doubled[:, :half] * gate
    reach = taps.shape[0] // 2
    gated_grad = None
    for k in range(taps.shape[0]):
        kept = back * keep[:, k : k + 1]
        taps_out[k : k + 1] = jnp.sum(kept * shifted(gated, reach - k), axis=0, keepdims=True)
        term = shifted(kept, k - reach) * taps[k : k + 1]
        gated_grad = term if gated_grad is None else gated_grad + term
    doubled_grad[:, :half] = (gated_grad * gate).astype(jnp.bfloat16)
    doubled_grad[:, half:] = (gated_grad * gated * (1.0 - gate)).astype(jnp.bfloat16)
    to_quarters(place, doubled_grad, outs)


def conv_back_step(order, place, gather, index, row, gradient, filtered, doubled, gains, shifts, taps, keep):
    pieces = Pieces(gather, index)
    width = filtered.shape[1]
    return order.call(
        functools.partial(conv_back_kernel, pieces, row),
        [
            *quarter_shapes(doubled.shape),
            *vector_shapes(width),
            jax.ShapeDtypeStruct(taps.shape, jnp.float32),
        ],
        [SMEM_SPACE] + [VMEM_SPACE] * 7 + [ANY_SPACE] * len(pieces.operands),
        [VMEM_SPACE] * (3 + QUARTERS),
        [pltpu.VMEM(doubled.shape, jnp.bfloat16), *pieces.scratch],
        [place, gradient, filtered, doubled, gains, shifts, taps, keep, *pieces.operands],
    )


def shards(
    sizes,
    frames,
    lengths,
    languages,
    embedding,
    gains,
    shifts,
    firstup,
    firstdown,
    projection,
    merger,
    gating,
    kernel,
    pointwise,
    secondup,
    seconddown,
    cotangent,
):
    frame_count = frames.shape[0]
    dp_index = lax.axis_index("dp").astype(jnp.int32)
    place = jnp.stack(
        [
            lax.rem(dp_index, jnp.int32(QUARTERS)),
            lax.axis_index("z").astype(jnp.int32),
            lax.axis_index("core").astype(jnp.int32),
        ]
    )
    order = Order(frames)
    gathers = [
        Gather(place, sizes, order, group)
        for group in (
            [firstup],
            [firstdown],
            [projection, merger],
            [gating, pointwise],
            [secondup],
            [seconddown],
        )
    ]
    for gather in gathers:
        gather.begin()
    table_full, gain_full, shift_full, kernel_full = gather_small(
        [embedding, gains, shifts, kernel]
    )
    segment_all, position_all, language_all = layout(lengths, languages, frame_count)
    segment = segment_all[0]
    language_row = language_all[0]
    cosine, sine = angles(position_all[0])
    cosine = jnp.concatenate([cosine, cosine], axis=-1)[:, 0]
    sine = jnp.concatenate([-sine, sine], axis=-1)[:, 0]
    down, across = segment[:, None], segment[None, :]
    gain_rows = gain_full.astype(jnp.float32)
    shift_rows = shift_full.astype(jnp.float32)
    taps = kernel_full.astype(jnp.float32)
    reach = taps.shape[0] // 2
    segment_pad = jnp.pad(segment, (reach, reach), constant_values=-1)
    keep = jnp.stack(
        [segment_pad[k : k + frame_count] == segment for k in range(taps.shape[0])], axis=1
    ).astype(jnp.float32)
    language_hot = (
        language_row[:, None] == jnp.arange(table_full.shape[0], dtype=jnp.int32)[None, :]
    ).astype(jnp.float32)
    start_sum = frames.astype(jnp.float32) + jnp.dot(
        language_hot.astype(jnp.bfloat16), table_full, preferred_element_type=jnp.float32
    )

    for number, gather in enumerate(gathers[:2]):
        gather.exchange(number % 2 == 1)
    first_hidden, first_expanded, *first_active = up_step(
        order, place, gathers[0], 0, 0, start_sum, gain_rows, shift_rows
    )
    gathers[2].exchange(False)
    after_first = down_step(order, place, gathers[1], 0, start_sum, first_active)
    gathers[3].exchange(True)
    attend_hidden, turned, totals, mixed = attend_step(
        order, place, gathers[2], 0, 1, after_first, gain_rows, shift_rows, cosine, sine, down, across
    )
    after_attention = merge_step(order, place, gathers[2], 1, after_first, mixed)
    gathers[4].exchange(False)
    after_conv, conv_hidden, doubled, filtered, conv_active = conv_step(
        order, place, gathers[3], 2, after_attention, gain_rows, shift_rows, taps, keep
    )
    gathers[5].exchange(True)
    second_hidden, second_expanded, *second_active = up_step(
        order, place, gathers[4], 0, 4, after_conv, gain_rows, shift_rows
    )
    encoded, grad_second, low_second, final_gain, final_shift = last_step(
        order, place, gathers[5], 0, 5, after_conv, second_active, cotangent, gain_rows, shift_rows
    )

    def scatter(flip):
        return Scatter(place, sizes, order, flip)

    down_two, up_two, conv, attend, down_one, up_one = (
        scatter(False),
        scatter(True),
        scatter(False),
        scatter(True),
        scatter(False),
        scatter(True),
    )
    down_factors = Factors(low_second, second_active)
    second_grad = down_back_step(order, place, gathers[5], 0, low_second, second_expanded)
    up_factors = Factors(second_hidden, second_grad)
    down_two.halves(down_factors)
    grad_conv, low_conv, second_gain, second_shift = into_norm_step(
        order, place, gathers[4], 0, 4, 1.0, second_grad, after_conv, grad_second, gain_rows
    )
    up_two.halves(up_factors)
    pointwise_factors = Factors(conv_active, low_conv)
    *doubled_grad, inner_gain, inner_shift, taps_grad = conv_back_step(
        order, place, gathers[3], 1, 3, low_conv, filtered, doubled, gain_rows, shift_rows, taps, keep
    )
    gating_factors = Factors(conv_hidden, doubled_grad)
    grad_attention, low_attention, outer_gain, outer_shift = into_norm_step(
        order, place, gathers[3], 0, 2, 1.0, doubled_grad, after_attention, grad_conv, gain_rows
    )
    down_two.quarters()
    conv.halves(gating_factors, pointwise_factors)
    merger_factors = Factors(mixed, low_attention)
    projected_grad = attend_back_step(
        order, place, gathers[2], 1, low_attention, turned, totals, cosine, sine, down, across
    )
    projection_factors = Factors(attend_hidden, projected_grad)
    up_two.quarters()
    grad_first, low_first, attend_gain, attend_shift = into_norm_step(
        order, place, gathers[2], 0, 1, 0.5, projected_grad, after_first, grad_attention, gain_rows
    )
    attend.halves(projection_factors, merger_factors)
    down_factors = Factors(low_first, first_active)
    down_two.rows()
    first_grad = down_back_step(order, place, gathers[1], 0, low_first, first_expanded)
    up_factors = Factors(first_hidden, first_grad)
    conv.quarters()
    down_one.halves(down_factors)
    frames_grad, low_start, first_gain, first_shift = into_norm_step(
        order, place, gathers[0], 0, 0, 1.0, first_grad, start_sum, grad_first, gain_rows
    )
    up_two.rows()
    attend.quarters()
    vectors = jnp.concatenate(
        [
            first_gain,
            attend_gain,
            outer_gain,
            inner_gain,
            second_gain,
            final_gain,
            first_shift,
            attend_shift,
            outer_shift,
            inner_shift,
            second_shift,
            final_shift,
            taps_grad,
        ]
    )
    small_factors = Factors(*pack_small(language_hot, low_start, vectors))
    up_one.halves(up_factors, small_factors)
    conv.rows()
    down_two.share()
    down_one.quarters()
    attend.rows()
    up_two.share()
    up_one.quarters()
    (seconddown_grad,) = down_two.spread()
    conv.share()
    down_one.rows()
    (secondup_grad,) = up_two.spread()
    attend.share()
    up_one.rows()
    gating_grad, pointwise_grad = conv.spread()
    down_one.share()
    projection_grad, merger_grad = attend.spread()
    (firstdown_grad,) = down_one.spread()
    up_one.share()
    firstup_grad, small = up_one.spread()
    counts = [embedding.shape[0], gains.shape[0], shifts.shape[0], kernel.shape[0]]
    table_sum, gain_sum, shift_sum, taps_sum = unpack_small(small, counts)
    return (
        encoded,
        frames_grad,
        table_sum,
        gain_sum,
        shift_sum,
        firstup_grad,
        firstdown_grad,
        projection_grad,
        merger_grad,
        gating_grad,
        taps_sum,
        pointwise_grad,
        secondup_grad,
        seconddown_grad,
    )


def solution(mesh):
    dp_size, fsdp_size = mesh.shape["dp"], mesh.shape["fsdp"]
    layers = fsdp_size // 2
    split = Mesh(mesh.devices.reshape(dp_size, layers, 2), ("dp", "z", "core"))
    return jax.shard_map(
        functools.partial(shards, (dp_size, layers)),
        mesh=split,
        in_specs=(
            P(("dp", "z", "core"), None),
            P(("dp", "z", "core"), None),
            P(("dp", "z", "core"), None),
            P(None, ("z", "core")),
            P(None, ("z", "core")),
            P(None, ("z", "core")),
            P(("z", "core"), None),
            P(("z", "core"), None),
            P(("z", "core"), None),
            P(("z", "core"), None),
            P(("z", "core"), None),
            P(None, ("z", "core")),
            P(("z", "core"), None),
            P(("z", "core"), None),
            P(("z", "core"), None),
            P(("dp", "z", "core"), None),
        ),
        out_specs=(
            P(("dp", "z", "core"), None),
            P(("dp", "z", "core"), None),
            P(None, ("z", "core")),
            P(None, ("z", "core")),
            P(None, ("z", "core")),
            P(("z", "core"), None),
            P(("z", "core"), None),
            P(("z", "core"), None),
            P(("z", "core"), None),
            P(("z", "core"), None),
            P(None, ("z", "core")),
            P(("z", "core"), None),
            P(("z", "core"), None),
            P(("z", "core"), None),
        ),
        check_vma=False,
    )
```

time: 1400 us -> 832 us (0.59)
  waiting for transfers between devices: 1100 us -> 398 us
  Pallas kernels: 0 us -> 194 us
  matrix products: 130 us -> 1.29 us
  local copies, waits for them, and re-layouts: 32.7 us -> 115 us
  starting transfers between devices: 1.63 us -> 71.8 us
  blocking collectives: 75.2 us -> 16.6 us
  other arithmetic: 31.2 us -> 10.7 us
    reduce_scatter x8 -> x6, waiting for transfers between devices: 464 us -> 77.6 us  [rows(): self.mine = lax.psum_scatter(own, 'z', scatter_dimension=0, tiled=True)]
    all_gather x8 -> x6, waiting for transfers between devices: 387 us -> 12.8 us  [begin(): self.gathered = lax.all_gather(mine, ('z', 'core'), axis=0, tiled=False)]
    ppermute x0 -> x116, waiting for transfers between devices: none -> 306 us  [the longest x54 301 us: swap_dp(): return lax.ppermute(value, 'dp', [(i, i ^ 1 << bit) for i in range(size)])]
    pallas_call x0 -> x45, Pallas kernels: none -> 194 us  [call(): pl.pallas_call(body, out_shape=[*out_shape, jax.ShapeDtypeStruct(self.val...]
    dot_general x31 -> x0, matrix products: 130 us -> none  [the longest x8 46.1 us: weight_grad(): lax.dot_general(left_side, right_side, (((0,), (0,)), ((), ())), preferre...]
    unnamed x25 -> x12, waiting for transfers between devices: 128 us -> 1.37 us
    psum x1 -> x0, waiting for transfers between devices: 121 us -> none  [weight_grad(): return lax.psum(pieces, 'dp').astype(jnp.float32)]
    ppermute x0 -> x116, starting transfers between devices: none -> 71.1 us  [the longest x54 57.5 us: swap_dp(): return lax.ppermute(value, 'dp', [(i, i ^ 1 << bit) for i in range(size)])]
  transfers between devices with their start and end apart: 21 -> 128, of which waited for: 19 -> 32; matrix products, arithmetic and copies ran while one was open for 10% -> 3% of each run, Pallas kernels for 0% -> 22%
where the time goes in v2:
time: 832 us; the launch traced here: 826 us
  waiting for transfers between devices  398 us (48%)
  Pallas kernels  194 us (23%)
  local copies, waits for them, and re-layouts  115 us (14%)
  starting transfers between devices  71.8 us (9%)
  between operations  18.6 us (2%)
  blocking collectives  16.6 us (2%)
  other arithmetic  10.7 us (1%)
    ppermute x54, waiting for transfers between devices, swap_dp(): return lax.ppermute(value, 'dp', [(i, i ^ 1 << bit) for i in range(size)])  301 us
    pallas_call x45, Pallas kernels, call(): pl.pallas_call(body, out_shape=[*out_shape, jax.ShapeDtypeStruct(self.val...  194 us
    unnamed x628, local copies, waits for them, and re-layouts  95.3 us
    reduce_scatter x6, waiting for transfers between devices, rows(): self.mine = lax.psum_scatter(own, 'z', scatter_dimension=0, tiled=True)  77.6 us
    ppermute x54, starting transfers between devices, swap_dp(): return lax.ppermute(value, 'dp', [(i, i ^ 1 << bit) for i in range(size)])  57.5 us
    all_gather x1, blocking collectives, gather_small(): full = lax.all_gather(packed, ('z', 'core'), axis=0, tiled=False)  16.6 us
  transfers between devices with their start and end apart: 128, of which 32 were waited for; matrix products, arithmetic and copies ran while one was open for 3% of the time, Pallas kernels for 22%

profile of v2, /device:TPU:0, one launch (start us, length us, event | category | flops | bytes accessed | tf_op | source)
XLA Modules:
  0.0 826.4 jit_solution(2235404266468121651)
XLA Ops:
  18.7 16.6 %all-gather = bf16[1024,128]{1,0:T(8,128)(2,1)S(1)} all-gather(bf16[128,128]{1,0:T(8,128)(2,1)S(1)} %fusion.9), channel_id=2, replica_groups=mesh['dp'=4,'z'=4,'core'=2] {'z','core'}, dimensions={0}, use_global_device_ids=true | all-gather | bytes 294912 | tf_op jit(solution)/shard_map/all_gather | solution.py:362
  50.3 16.9 %collective-permute-done.1.refs_7_.refs_11_ = bf16[3,128,1024]{2,1,0:T(8,128)(2,1)S(1)} collective-permute-done((bf16[3,128,1024]{2,1,0:T(8,128)(2,1)}, bf16[3,128,1024]{2,1,0:T(8,128)(2,1)S(1)}, u32[]{:S(2)}, u32[]{:S(2)}) %collective-permute-start.1) | collective-permute-done | bytes 786464 | tf_op jit(solution)/shard_map/ppermute | solution.py:106
  87.8 15.3 %collective-permute-done.9.refs_10_.refs_7_ = bf16[3,128,1024]{2,1,0:T(8,128)(2,1)} collective-permute-done((bf16[3,128,1024]{2,1,0:T(8,128)(2,1)}, bf16[3,128,1024]{2,1,0:T(8,128)(2,1)}, u32[]{:S(2)}, u32[]{:S(2)}) %collective-permute-start.9) | collective-permute-done | bytes 786464 | tf_op jit(solution)/shard_map/ppermute | solution.py:106
  132.2 17.4 %collective-permute-done.15.refs_11_.refs_6_ = bf16[3,128,1024]{2,1,0:T(8,128)(2,1)S(1)} collective-permute-done((bf16[3,128,1024]{2,1,0:T(8,128)(2,1)}, bf16[3,128,1024]{2,1,0:T(8,128)(2,1)S(1)}, u32[]{:S(2)}, u32[]{:S(2)}) %collective-permute-start.15) | collective-permute-done | bytes 786464 | tf_op jit(solution)/shard_map/ppermute | solution.py:106
  166.6 14.8 %collective-permute-done.24.refs_10_.refs_19_.refs_12_ = bf16[3,128,768]{2,1,0:T(8,128)(2,1)} collective-permute-done((bf16[3,128,768]{2,1,0:T(8,128)(2,1)S(1)}, bf16[3,128,768]{2,1,0:T(8,128)(2,1)}, u32[]{:S(2)}, u32[]{:S(2)}) %collective-permute-start.24) | collective-permute-done | bytes 589856 | tf_op jit(solution)/shard_map/ppermute | solution.py:106
  183.2 12.5 %collective-permute-done.25.refs_11_.refs_20_.refs_13_ = bf16[3,128,768]{2,1,0:T(8,128)(2,1)} collective-permute-done((bf16[3,128,768]{2,1,0:T(8,128)(2,1)}, bf16[3,128,768]{2,1,0:T(8,128)(2,1)}, u32[]{:S(2)}, u32[]{:S(2)}) %collective-permute-start.25) | collective-permute-done | bytes 589856 | tf_op jit(solution)/shard_map/ppermute | solution.py:106
  204.7 8.6 %shard_map.272 = (bf16[256,1024]{1,0:T(8,128)(2,1)S(1)}, bf16[256,3072]{1,0:T(8,128)(2,1)S(1)}, f32[256,8]{1,0:T(8,128)S(1)}, bf16[256,1024]{1,0:T(8,128)(2,1)S(1)}, bf16[256,1024]{1,0:T(8,128)(2,1)S(1)}) custom-call(s32[3]{0:T(128)S(1)} %pad_add_fusion.refs_0_, f32[256,1024]{1,0:T(8,128)S(1)} %copy-done.22, ...), custom_call_target="tpu_custom_call", output_to_operand_aliasing={{4}: (17, {})} | custom-call | flops 1 | bytes 2400000 | tf_op jit(solution)/shard_map/pallas_call | solution.py:80
  248.4 16.4 %collective-permute-done.39.refs_13_.refs_7_ = bf16[3,128,1024]{2,1,0:T(8,128)(2,1)S(1)} collective-permute-done((bf16[3,128,1024]{2,1,0:T(8,128)(2,1)S(1)}, bf16[3,128,1024]{2,1,0:T(8,128)(2,1)S(1)}, u32[]{:S(2)}, u32[]{:S(2)}) %collective-permute-start.39) | collective-permute-done | bytes 786464 | tf_op jit(solution)/shard_map/ppermute | solution.py:106
  266.3 13.8 %collective-permute-done.33.refs_9_.refs_13_ = bf16[3,128,1024]{2,1,0:T(8,128)(2,1)S(1)} collective-permute-done((bf16[3,128,1024]{2,1,0:T(8,128)(2,1)}, bf16[3,128,1024]{2,1,0:T(8,128)(2,1)S(1)}, u32[]{:S(2)}, u32[]{:S(2)}) %collective-permute-start.33) | collective-permute-done | bytes 786464 | tf_op jit(solution)/shard_map/ppermute | solution.py:106
  337.3 20.6 %collective-permute-done.62.refs_12_ = bf16[512,1024]{1,0:T(8,128)(2,1)S(1)} collective-permute-done((bf16[512,1024]{1,0:T(8,128)(2,1)S(1)}, bf16[512,1024]{1,0:T(8,128)(2,1)S(1)}, u32[]{:S(2)}, u32[]{:S(2)}) %collective-permute-start.62) | collective-permute-done | bytes 1048608 | tf_op jit(solution)/shard_map/ppermute | solution.py:106
  371.3 8.6 %shard_map.287 = (bf16[256,768]{1,0:T(8,128)(2,1)S(1)}, bf16[256,768]{1,0:T(8,128)(2,1)S(1)}, bf16[256,768]{1,0:T(8,128)(2,1)S(1)}, bf16[256,768]{1,0:T(8,128)(2,1)S(1)}, bf16[256,1024]{1,0:T(8,128)(2,1)S(1)}) custom-call(s32[3]{0:T(128)S(1)} %pad_add_fusion.refs_0_, ...), custom_call_target="tpu_custom_call", output_to_operand_aliasing={{4}: (17, {})} | custom-call | flops 1 | bytes 2400000 | tf_op jit(solution)/shard_map/pallas_call | solution.py:80
  397.5 8.3 %collective-permute-done.65.refs_13_ = bf16[512,1024]{1,0:T(8,128)(2,1)S(1)} collective-permute-done((bf16[512,1024]{1,0:T(8,128)(2,1)S(1)}, bf16[512,1024]{1,0:T(8,128)(2,1)S(1)}, u32[]{:S(2)}, u32[]{:S(2)}) %collective-permute-start.65) | collective-permute-done | bytes 1048608 | tf_op jit(solution)/shard_map/ppermute | solution.py:106
  414.0 38.9 %collective-permute-done.78.refs_15_ = bf16[512,768]{1,0:T(8,128)(2,1)S(1)} collective-permute-done((bf16[512,768]{1,0:T(8,128)(2,1)}, bf16[512,768]{1,0:T(8,128)(2,1)S(1)}, u32[]{:S(2)}, u32[]{:S(2)}) %collective-permute-start.78) | collective-permute-done | bytes 786464 | tf_op jit(solution)/shard_map/ppermute | solution.py:106
  453.5 15.9 %collective-permute-done.79.refs_16_ = bf16[512,768]{1,0:T(8,128)(2,1)S(1)} collective-permute-done((bf16[512,768]{1,0:T(8,128)(2,1)}, bf16[512,768]{1,0:T(8,128)(2,1)S(1)}, u32[]{:S(2)}, u32[]{:S(2)}) %collective-permute-start.79) | collective-permute-done | bytes 786464 | tf_op jit(solution)/shard_map/ppermute | solution.py:106
  535.2 12.5 %shard_map.298 = (bf16[512,1152]{1,0:T(8,128)(2,1)}, bf16[512,1152]{1,0:T(8,128)(2,1)}, bf16[256,1024]{1,0:T(8,128)(2,1)S(1)}) custom-call(s32[3]{0:T(128)S(1)} %pad_add_fusion.refs_0_, bf16[256,1024]{1,0:T(8,128)(2,1)} %get-tuple-element.250.refs_1_, bf16[256,1024]{1,0:T(8,128)(2,1)} %collective-permute-done.80.refs_2_, ...), custom_call_target="tpu_custom_call", output_to_operand_aliasing={{2}: (15, {})} | custom-call | flops 1 | bytes 1500000 | tf_op jit(solution)/shard_map/pallas_call | solution.py:80
  557.8 18.5 %collective-permute-done.93.refs_11_ = bf16[512,1024]{1,0:T(8,128)(2,1)} collective-permute-done((bf16[512,1024]{1,0:T(8,128)(2,1)}, bf16[512,1024]{1,0:T(8,128)(2,1)}, u32[]{:S(2)}, u32[]{:S(2)}) %collective-permute-start.93) | collective-permute-done | bytes 1048608 | tf_op jit(solution)/shard_map/ppermute | solution.py:106
  576.2 22.5 %collective-permute-done.94.refs_12_ = bf16[512,1024]{1,0:T(8,128)(2,1)} collective-permute-done((bf16[512,1024]{1,0:T(8,128)(2,1)}, bf16[512,1024]{1,0:T(8,128)(2,1)}, u32[]{:S(2)}, u32[]{:S(2)}) %collective-permute-start.94) | collective-permute-done | bytes 1048608 | tf_op jit(solution)/shard_map/ppermute | solution.py:106
  609.3 10.4 %collective-permute-done.92.refs_17_ = bf16[512,1024]{1,0:T(8,128)(2,1)} collective-permute-done((bf16[512,1024]{1,0:T(8,128)(2,1)}, bf16[512,1024]{1,0:T(8,128)(2,1)}, u32[]{:S(2)}, u32[]{:S(2)}) %collective-permute-start.92) | collective-permute-done | bytes 1048608 | tf_op jit(solution)/shard_map/ppermute | solution.py:106
  624.8 7.5 shard_map.302
  636.9 27.8 %collective-permute-done.101.refs_2_ = bf16[128,1024]{1,0:T(8,128)(2,1)} collective-permute-done((bf16[128,1024]{1,0:T(8,128)(2,1)}, bf16[128,1024]{1,0:T(8,128)(2,1)}, u32[]{:S(2)}, u32[]{:S(2)}) %collective-permute-start.101) | collective-permute-done | bytes 262176 | tf_op jit(solution)/shard_map/ppermute | solution.py:106
  700.4 24.6 %reduce-scatter.11.cloned.1.call-done.refs_1_ = bf16[128,1152]{1,0:T(8,128)(2,1)} async-done(((bf16[512,1152]{1,0:T(8,128)(2,1)}), bf16[128,1152]{1,0:T(8,128)(2,1)}) %reduce-scatter.11.cloned.1.call-update) | async-done | bytes 294928 | tf_op jit(solution)/shard_map/reduce_scatter | solution.py:340
  726.4 27.3 %reduce-scatter.15.cloned.1.call-done.refs_1_ = bf16[128,1024]{1,0:T(8,128)(2,1)} async-done(((bf16[512,1024]{1,0:T(8,128)(2,1)}), bf16[128,1024]{1,0:T(8,128)(2,1)}) %reduce-scatter.15.cloned.1.call-update) | async-done | bytes 262160 | tf_op jit(solution)/shard_map/reduce_scatter | solution.py:340
  756.7 25.7 %reduce-scatter.13.cloned.1.call-done.refs_1_ = bf16[128,1024]{1,0:T(8,128)(2,1)} async-done(((bf16[512,1024]{1,0:T(8,128)(2,1)}), bf16[128,1024]{1,0:T(8,128)(2,1)}) %reduce-scatter.13.cloned.1.call-update) | async-done | bytes 262160 | tf_op jit(solution)/shard_map/reduce_scatter | solution.py:340
  798.4 11.2 %collective-permute-done.112.refs_4_ = bf16[128,1024]{1,0:T(8,128)(2,1)S(1)} collective-permute-done((bf16[128,1024]{1,0:T(8,128)(2,1)S(1)}, bf16[128,1024]{1,0:T(8,128)(2,1)S(1)}, u32[]{:S(2)}, u32[]{:S(2)}) %collective-permute-start.112) | collective-permute-done | bytes 262176 | tf_op jit(solution)/shard_map/ppermute | solution.py:106
  (983 shorter events, 395.2 us)
Async XLA Ops:
  10.0 65.0 %all-gather.16.cloned.1.call-start = ((), (), s32[]{:S(2)}) async-start(), calls=%async_computation.13 | async-start | bytes 2359296 | tf_op jit(solution)/shard_map/all_gather | solution.py:305
  11.7 114.5 %all-gather.18.cloned.1.call-start = ((), (), s32[]{:S(2)}) async-start(), calls=%async_computation.14 | async-start | bytes 2359296 | tf_op jit(solution)/shard_map/all_gather | solution.py:305
  14.3 145.0 %all-gather.20.cloned.1.call-start = ((), (), s32[]{:S(2)}) async-start(), calls=%async_computation.15 | async-start | bytes 1769472 | tf_op jit(solution)/shard_map/all_gather | solution.py:305
  16.9 203.9 %all-gather.22.cloned.1.call-start = ((), (), s32[]{:S(2)}) async-start(), calls=%async_computation.16 | async-start | bytes 2359296 | tf_op jit(solution)/shard_map/all_gather | solution.py:305
  18.6 223.3 %all-gather.24.cloned.1.call-start = ((), (), s32[]{:S(2)}) async-start(), calls=%async_computation.17 | async-start | bytes 2359296 | tf_op jit(solution)/shard_map/all_gather | solution.py:305
  84.2 550.1 %reduce-scatter.9.cloned.1.call-start = ((), (), s32[]{:S(2)}) async-start(), calls=%async_computation.7 | async-start | bytes 1310720 | tf_op jit(solution)/shard_map/reduce_scatter | solution.py:340
  199.0 48.9 %collective-permute-start.30 = (bf16[128,4096]{1,0:T(8,128)(2,1)}, bf16[128,4096]{1,0:T(8,128)(2,1)}, u32[]{:S(2)}, u32[]{:S(2)}) collective-permute-start(bf16[128,4096]{1,0:T(8,128)(2,1)} %refs_8_.8), channel_id=1, source_target_pairs={{0,1},{1,0},{2,3},{3,2},{4,5},{5,4},{6,7},{7,6},{8,9},{9,8},{10,11... | collective-permute-start | bytes 3145736 | tf_op jit(solution)/shard_map/ppermute | solution.py:110
  409.2 227.2 %reduce-scatter.7.cloned.1.call-start = ((), (), s32[]{:S(2)}) async-start(), calls=%async_computation.6 | async-start | bytes 1310720 | tf_op jit(solution)/shard_map/reduce_scatter | solution.py:340
  409.9 84.6 %collective-permute-start.89 = (bf16[512,1024]{1,0:T(8,128)(2,1)}, bf16[512,1024]{1,0:T(8,128)(2,1)S(1)}, u32[]{:S(2)}, u32[]{:S(2)}) collective-permute-start(bf16[512,1024]{1,0:T(8,128)(2,1)} %copy-done.299), channel_id=1, source_target_pairs={{0,8},{8,0},{16,24},{24,16},{1,9},{9,1},{17,25},{25,17},{2,10},{10... | collective-permute-start | bytes 3145736 | tf_op jit(solution)/shard_map/ppermute | solution.py:106
  411.9 57.4 %collective-permute-start.79 = (bf16[512,768]{1,0:T(8,128)(2,1)}, bf16[512,768]{1,0:T(8,128)(2,1)S(1)}, u32[]{:S(2)}, u32[]{:S(2)}) collective-permute-start(bf16[512,768]{1,0:T(8,128)(2,1)} %copy-done.301), channel_id=1, source_target_pairs={{0,8},{8,0},{16,24},{24,16},{1,9},{9,1},{17,25},{25,17},{2,10},{10... | collective-permute-start | bytes 2359304 | tf_op jit(solution)/shard_map/ppermute | solution.py:106
  413.5 69.6 %collective-permute-start.77 = (bf16[256,1024]{1,0:T(8,128)(2,1)}, bf16[256,1024]{1,0:T(8,128)(2,1)S(1)}, u32[]{:S(2)}, u32[]{:S(2)}) collective-permute-start(bf16[256,1024]{1,0:T(8,128)(2,1)} %copy-done.37), channel_id=1, source_target_pairs={{0,1},{1,0},{2,3},{3,2},{4,5},{5,4},{6,7},{7,6},{8,9},{9,8},{10,11... | collective-permute-start | bytes 1572872 | tf_op jit(solution)/shard_map/ppermute | solution.py:110
  413.5 69.6 %collective-permute-start.73 = (bf16[256,1024]{1,0:T(8,128)(2,1)}, bf16[256,1024]{1,0:T(8,128)(2,1)S(1)}, u32[]{:S(2)}, u32[]{:S(2)}) collective-permute-start(bf16[256,1024]{1,0:T(8,128)(2,1)} %copy-done.40), channel_id=1, source_target_pairs={{0,1},{1,0},{2,3},{3,2},{4,5},{5,4},{6,7},{7,6},{8,9},{9,8},{10,11... | collective-permute-start | bytes 1572872 | tf_op jit(solution)/shard_map/ppermute | solution.py:110
  452.9 62.5 %collective-permute-start.87 = (bf16[512,1024]{1,0:T(8,128)(2,1)}, bf16[512,1024]{1,0:T(8,128)(2,1)}, u32[]{:S(2)}, u32[]{:S(2)}) collective-permute-start(bf16[512,1024]{1,0:T(8,128)(2,1)} %copy-done.298), channel_id=1, source_target_pairs={{0,16},{8,24},{16,0},{24,8},{1,17},{9,25},{17,1},{25,9},{2,18},{10... | collective-permute-start | bytes 3145736 | tf_op jit(solution)/shard_map/ppermute | solution.py:106
  498.0 201.2 %reduce-scatter.17.cloned.1.call-start = ((), (), s32[]{:S(2)}) async-start(), calls=%async_computation.11 | async-start | bytes 983040 | tf_op jit(solution)/shard_map/reduce_scatter | solution.py:340
  547.7 76.9 %collective-permute-start.90 = (bf16[512,1152]{1,0:T(8,128)(2,1)}, bf16[512,1152]{1,0:T(8,128)(2,1)}, u32[]{:S(2)}, u32[]{:S(2)}) collective-permute-start(bf16[512,1152]{1,0:T(8,128)(2,1)} %get-tuple-element.271), channel_id=1, source_target_pairs={{0,16},{8,24},{16,0},{24,8},{1,17},{9,25},{17,1},{25,9},{2,18},{10... | collective-permute-start | bytes 3538952 | tf_op jit(solution)/shard_map/ppermute | solution.py:106
  548.3 76.3 %collective-permute-start.91 = (bf16[512,1152]{1,0:T(8,128)(2,1)}, bf16[512,1152]{1,0:T(8,128)(2,1)}, u32[]{:S(2)}, u32[]{:S(2)}) collective-permute-start(bf16[512,1152]{1,0:T(8,128)(2,1)} %get-tuple-element.272), channel_id=1, source_target_pairs={{0,16},{8,24},{16,0},{24,8},{1,17},{9,25},{17,1},{25,9},{2,18},{10... | collective-permute-start | bytes 3538952 | tf_op jit(solution)/shard_map/ppermute | solution.py:106
  551.9 67.8 %collective-permute-start.92 = (bf16[512,1024]{1,0:T(8,128)(2,1)}, bf16[512,1024]{1,0:T(8,128)(2,1)}, u32[]{:S(2)}, u32[]{:S(2)}) collective-permute-start(bf16[512,1024]{1,0:T(8,128)(2,1)} %get-tuple-element.273), channel_id=1, source_target_pairs={{0,8},{8,0},{16,24},{24,16},{1,9},{9,1},{17,25},{25,17},{2,10},{10... | collective-permute-start | bytes 3145736 | tf_op jit(solution)/shard_map/ppermute | solution.py:106
  557.7 167.3 %reduce-scatter.11.cloned.1.call-start = ((), (), s32[]{:S(2)}) async-start(), calls=%async_computation.8 | async-start | bytes 1474560 | tf_op jit(solution)/shard_map/reduce_scatter | solution.py:340
  632.2 58.6 %collective-permute-start.96 = (bf16[512,1152]{1,0:T(8,128)(2,1)}, bf16[512,1152]{1,0:T(8,128)(2,1)}, u32[]{:S(2)}, u32[]{:S(2)}) collective-permute-start(bf16[512,1152]{1,0:T(8,128)(2,1)} %get-tuple-element.281), channel_id=1, source_target_pairs={{0,8},{8,0},{16,24},{24,16},{1,9},{9,1},{17,25},{25,17},{2,10},{10... | collective-permute-start | bytes 3538952 | tf_op jit(solution)/shard_map/ppermute | solution.py:106
  697.9 55.8 %reduce-scatter.15.cloned.1.call-start = ((), (), s32[]{:S(2)}) async-start(), calls=%async_computation.10 | async-start | bytes 1310720 | tf_op jit(solution)/shard_map/reduce_scatter | solution.py:340
  698.7 83.7 %reduce-scatter.13.cloned.1.call-start = ((), (), s32[]{:S(2)}) async-start(), calls=%async_computation.9 | async-start | bytes 1310720 | tf_op jit(solution)/shard_map/reduce_scatter | solution.py:340
  699.3 57.4 %collective-permute-start.113 = (bf16[128,768]{1,0:T(8,128)(2,1)}, bf16[128,768]{1,0:T(8,128)(2,1)S(1)}, u32[]{:S(2)}, u32[]{:S(2)}) collective-permute-start(bf16[128,768]{1,0:T(8,128)(2,1)} %reduce-scatter.17.cloned.1.call-done.refs_1_), channel_id=1, source_target_pairs={{0,8},{8,0},{16,24},{24,16},{1,9},{9,1},{17,25},{25,17},{2,10},{10... | collective-permute-start | bytes 589832 | tf_op jit(solution)/shard_map/ppermute | solution.py:106
  699.8 84.0 %collective-permute-start.114 = (bf16[128,768]{1,0:T(8,128)(2,1)}, bf16[128,768]{1,0:T(8,128)(2,1)S(1)}, u32[]{:S(2)}, u32[]{:S(2)}) collective-permute-start(bf16[128,768]{1,0:T(8,128)(2,1)} %reduce-scatter.17.cloned.1.call-done.refs_1_), channel_id=1, source_target_pairs={{0,16},{8,24},{16,0},{24,8},{1,17},{9,25},{17,1},{25,9},{2,18},{10... | collective-permute-start | bytes 589832 | tf_op jit(solution)/shard_map/ppermute | solution.py:106
  725.0 65.6 %collective-permute-start.105 = (bf16[128,1152]{1,0:T(8,128)(2,1)}, bf16[128,1152]{1,0:T(8,128)(2,1)S(1)}, u32[]{:S(2)}, u32[]{:S(2)}) collective-permute-start(bf16[128,1152]{1,0:T(8,128)(2,1)} %reduce-scatter.11.cloned.1.call-done.refs_1_), channel_id=1, source_target_pairs={{0,16},{8,24},{16,0},{24,8},{1,17},{9,25},{17,1},{25,9},{2,18},{10... | collective-permute-start | bytes 884744 | tf_op jit(solution)/shard_map/ppermute | solution.py:106
  (416 other events, 5754.7 us)
Sparse Core Ops, SparseCore 0:
  10.2 33.8 all-gather.13
  46.3 28.5 all-gather.15
  77.1 28.7 all-gather.17
  107.9 26.0 all-gather.19
  136.1 28.4 all-gather.21
  166.0 28.4 all-gather.23
  409.3 25.7 reduce-scatter.8
  498.1 26.6 reduce-scatter.6
  557.9 20.9 reduce-scatter.16
  698.0 26.9 reduce-scatter.10
  727.9 25.8 reduce-scatter.14
  756.6 25.7 reduce-scatter.12

commit v3 on v2

v3 whole, which is shorter than its diff:
```python
import functools

import jax
import jax.numpy as jnp
import numpy as np
from jax import lax
from jax.experimental import pallas as pl
from jax.experimental.pallas import tpu as pltpu
from jax.sharding import Mesh
from jax.sharding import PartitionSpec as P

HEAD_DIM = 128


def layout(lengths, languages, frame_count):
    utterances = jnp.arange(lengths.shape[-1], dtype=jnp.int32)
    earlier = utterances[:, None] <= utterances[None, :]
    finish = jnp.sum(jnp.where(earlier[None], lengths[:, :, None], 0), axis=1)
    begins = finish - lengths
    indices = jnp.arange(frame_count, dtype=jnp.int32)
    segment = jnp.sum((indices[None, :, None] >= finish[:, None, :]).astype(jnp.int32), axis=-1)
    owners = segment[:, :, None] == jnp.arange(lengths.shape[-1], dtype=jnp.int32)[None, None, :]
    first_row = jnp.sum(jnp.where(owners, begins[:, None, :], 0), axis=-1)
    language_row = jnp.sum(jnp.where(owners, languages[:, None, :], 0), axis=-1)
    return (segment, indices[None, :] - first_row, language_row)


def angles(position):
    half_dim = HEAD_DIM // 2
    frequency = 10000.0 ** (-jnp.arange(half_dim, dtype=jnp.float32) / half_dim)
    turned = position.astype(jnp.float32)[..., None] * frequency
    return (jnp.cos(turned)[..., None, :], jnp.sin(turned)[..., None, :])


VMEM_SPACE = pl.BlockSpec(memory_space=pltpu.VMEM)
SMEM_SPACE = pl.BlockSpec(memory_space=pltpu.SMEM)
ANY_SPACE = pl.BlockSpec(memory_space=pl.ANY)


class Order:
    def __init__(self, value):
        self.value, self.waits = value, []

    def wait(self, *arrays):
        self.waits += arrays

    def call(self, kernel, out_shape, in_specs, out_specs, scratch_shapes, operands, through=(), lazy=False):
        after, self.waits = self.waits, []
        carried = [*through, self.value]
        count, outs, extra = len(operands), len(out_shape), len(after)
        held_in = [i for i in range(count) if in_specs[i] is VMEM_SPACE]
        held_out = [i for i in range(outs) if out_specs[i] is VMEM_SPACE]
        buffers = [pltpu.VMEM(operands[i].shape, operands[i].dtype) for i in held_in]
        buffers += [pltpu.VMEM(out_shape[i].shape, out_shape[i].dtype) for i in held_out]
        copies = max(1, len(held_in), len(held_out))

        def body(*refs):
            ins, rest = list(refs[:count]), refs[count + extra + len(carried) :]
            results, rest = list(rest[:outs]), rest[outs + len(carried) :]
            held, scratch, sems = rest[: len(buffers)], rest[len(buffers) : -1], rest[-1]
            moves = []
            for at, i in enumerate(held_in):
                moves.append(pltpu.make_async_copy(ins[i], held[at], sems.at[at]))
                moves[-1].start()
                ins[i] = held[at]
            targets = []
            for at, i in enumerate(held_out):
                targets.append(results[i])
                results[i] = held[len(held_in) + at]
            def ready():
                for move in arriving:
                    move.wait()

            arriving = moves
            if lazy:
                kernel(ready, *ins, *results, *scratch)
            else:
                ready()
                kernel(*ins, *results, *scratch)
            moves = []
            for at, i in enumerate(held_out):
                moves.append(pltpu.make_async_copy(results[i], targets[at], sems.at[at]))
                moves[-1].start()
            for move in moves:
                move.wait()

        result = pl.pallas_call(
            body,
            out_shape=[*out_shape, *[jax.ShapeDtypeStruct(x.shape, x.dtype) for x in carried]],
            in_specs=[ANY_SPACE if s is VMEM_SPACE else s for s in in_specs]
            + [ANY_SPACE] * (extra + len(carried)),
            out_specs=[ANY_SPACE] * (outs + len(carried)),
            scratch_shapes=[*buffers, *scratch_shapes, pltpu.SemaphoreType.DMA((copies,))],
            input_output_aliases={count + extra + i: outs + i for i in range(len(carried))},
            compiler_params=pltpu.CompilerParams(vmem_limit_bytes=VMEM_LIMIT),
        )(*operands, *after, *carried)
        self.value = result[-1]
        return result[:-1]


VMEM_LIMIT = 60 * 1024 * 1024
QUARTERS = 4
LANES = 128
BITS = (0, 1)


def swap_dp(value, bit, size):
    return lax.ppermute(value, "dp", [(i, i ^ (1 << bit)) for i in range(size)])


def swap_core(value):
    return lax.ppermute(value, "core", [(0, 1), (1, 0)])


def swap_pairs(value, flip, size):
    pairs = []
    for i in range(size):
        for core in range(2):
            far = i ^ (1 << BITS[core ^ flip])
            pairs.append((2 * i + core, 2 * far + core))
    return lax.ppermute(value, ("dp", "core"), pairs)


def pick_kernel(layers, base, place, gathered, out, sems):
    layer = place[1]
    rows, copies = gathered.shape[1], []
    for k in range(1, layers):
        for lane in range(2):
            at = 2 * (k - 1) + lane
            row = lax.rem(layer + k, layers) * 2 + lane
            source = gathered.at[row, :, pl.ds(base, out.shape[1])]
            target = out.at[pl.ds(at * rows, rows)]
            copies.append(pltpu.make_async_copy(source, target, sems.at[at]))
            copies[-1].start()
    for copy in copies:
        copy.wait()


def pick(order, place, layers, gathered, base, width):
    blocks = 2 * (layers - 1)
    return order.call(
        functools.partial(pick_kernel, layers, base),
        [jax.ShapeDtypeStruct((blocks * gathered.shape[1], width), gathered.dtype)],
        [SMEM_SPACE, ANY_SPACE],
        [VMEM_SPACE],
        [pltpu.SemaphoreType.DMA((blocks,))],
        [place, gathered],
    )[0]


def half_kernel(place, piece, out, sems):
    rows = out.shape[0]
    start = pl.multiple_of(place[2] * rows, rows)
    copy = pltpu.make_async_copy(piece.at[pl.ds(start, rows)], out, sems.at[0])
    copy.start()
    copy.wait()


def half(order, place, piece):
    return order.call(
        half_kernel,
        [jax.ShapeDtypeStruct((piece.shape[0] // 2, piece.shape[1]), piece.dtype)],
        [SMEM_SPACE, ANY_SPACE],
        [VMEM_SPACE],
        [pltpu.SemaphoreType.DMA((1,))],
        [place, piece],
    )[0]


def join_kernel(*refs):
    ins, out, sems = refs[:-2], refs[-2], refs[-1]
    at, copies = 0, []
    for k, ref in enumerate(ins):
        target = out.at[:, pl.ds(at, ref.shape[1])]
        copies.append(pltpu.make_async_copy(ref, target, sems.at[k]))
        copies[-1].start()
        at += ref.shape[1]
    for copy in copies:
        copy.wait()


def join(order, arrays):
    width = sum(a.shape[1] for a in arrays)
    return order.call(
        join_kernel,
        [jax.ShapeDtypeStruct((arrays[0].shape[0], width), arrays[0].dtype)],
        [ANY_SPACE] * len(arrays),
        [VMEM_SPACE],
        [pltpu.SemaphoreType.DMA((len(arrays),))],
        arrays,
    )[0]


class Packed:
    def __init__(self, arrays):
        self.own = list(arrays)
        self.all = [*self.own, *[swap_core(a) for a in self.own]]
        self.tokens = sum(a.shape[1] for a in self.all)

    def part(self, index):
        return [(a, index, a.shape[1]) for a in self.all]


class Factor:
    def __init__(self, left, left_index, right, right_index, base, width, relative=True):
        self.left = left.part(left_index)
        self.right, self.right_index, self.base, self.relative = right, right_index, base, relative
        self.width, self.part, self.tokens = width, width // QUARTERS, left.tokens
        self.arrays = [*left.all, *right.all]

    def columns(self, quarter, r, start, width):
        if self.relative:
            index, column = self.right_index + r, pl.ds(self.base + start, width)
        else:
            index = self.right_index
            column = pl.ds(pl.multiple_of((quarter ^ r) * self.part + start, LANES), width)
        return [(a, index, column, count) for a, _, count in self.right.part(0)]


class Sums:
    def __init__(self, *factors):
        self.factors = factors
        self.width = sum(f.part for f in factors)

    def spans(self):
        base = 0
        for i, f in enumerate(self.factors):
            for start in range(0, f.part, TILE):
                yield i, start, min(TILE, f.part - start), base + start
            base += f.part


TILE = 512


def own_rows(ref, layers, core):
    tokens, features = ref.shape
    rows = features // (2 * layers)
    if rows % LANES == 0:
        blocks = [
            ref[:, pl.ds(pl.multiple_of((2 * k + core) * rows, rows), rows)] for k in range(layers)
        ]
        return jnp.concatenate(blocks, axis=1).T
    turned = ref[...].T.reshape(layers, 2, rows, tokens)
    return jnp.where(core == 0, turned[:, 0], turned[:, 1]).reshape(layers * rows, tokens)


def round_kernel(layers, plan, tables, place, *refs):
    jobs, lefts, count_in, count_out = plan
    ins, outs = refs[:count_in], refs[count_in : count_in + count_out]
    left_buffer, turned, right_buffer, add_buffer, out_buffer, left_sems, in_sems, out_sems = refs[
        count_in + count_out :
    ]
    quarter, core = place[0], place[2]

    quarters = {"both": 3, "near": 1 + core, "far": 2 - core, "own": 0}

    def start(source, target, sem):
        copy = pltpu.make_async_copy(source, target, sem)
        copy.start()
        return copy

    left_copies = []
    for i, factor in enumerate(lefts):
        at, copies = 0, []
        for k, (array, index, rows) in enumerate(factor.left):
            target = left_buffer.at[i, at : at + rows]
            copies.append(start(ins[tables[id(array)]].at[index], target, left_sems.at[i, k]))
            at += rows
        left_copies.append(copies)
    loads = []
    for number, (i, r, first, width, adds, _) in enumerate(jobs):
        at, copies = 0, []
        for array, index, column, rows in lefts[i].columns(quarter, quarters[r], first, width):
            source = ins[tables[id(array)]].at[index, :, column]
            target = right_buffer.at[number, at : at + rows, pl.ds(0, width)]
            copies.append(start(source, target, in_sems.at[number, len(copies)]))
            at += rows
        for k, (array, column) in enumerate(adds):
            height = add_buffer.shape[2]
            source = ins[tables[id(array)]].at[pl.ds(0, height), pl.ds(column, width)]
            target = add_buffer.at[number, k, :, pl.ds(0, width)]
            copies.append(start(source, target, in_sems.at[number, len(copies)]))
        loads.append(copies)
    for i, factor in enumerate(lefts):
        for copy in left_copies[i]:
            copy.wait()
        turned[i, :, : factor.tokens] = own_rows(
            left_buffer.at[i, pl.ds(0, factor.tokens)], layers, core
        )
    stores = []
    for number, (i, _, _, width, adds, (out, column)) in enumerate(jobs):
        tokens = lefts[i].tokens
        for copy in loads[number]:
            copy.wait()
        product = jnp.dot(
            turned[i, :, :tokens],
            right_buffer[number, :tokens, :width],
            preferred_element_type=jnp.float32,
        )
        for k in range(len(adds)):
            product += add_buffer[number, k, :, :width].astype(jnp.float32)
        out_buffer[number, :, :width] = product.astype(jnp.bfloat16)
        source = out_buffer.at[number, :, pl.ds(0, width)]
        target = outs[out].at[pl.ds(0, out_buffer.shape[1]), pl.ds(column, width)]
        stores.append(start(source, target, out_sems.at[number]))
    for copy in stores:
        copy.wait()


class Rounds:
    def __init__(self, place, sizes, order):
        self.place, self.order = place, order
        self.dp_size, self.layers = sizes

    def step(self, halves=(), quarters=(), rows=(), margin=0):
        lefts, jobs, widths = [], [], [0, 0, 0]

        def left(factor):
            if factor not in lefts:
                lefts.append(factor)
            return lefts.index(factor)

        def add(sums, r, out, adds):
            base = widths[out]
            for i, first, width, at in sums.spans():
                mine = [(array, offset + at) for array, offset in adds]
                jobs.append((left(sums.factors[i]), r, first, width, mine, (out, base + at)))
            widths[out] += sums.width
            return base

        sent = []
        for sums in halves:
            sums.near_at = add(sums, "both", 0, [])
            sums.own_at = add(sums, "near", 0, [])
        for sums in quarters:
            sums.far_at = add(sums, "far", 1, [(sums.halves, sums.near_at)])
        for sums in rows:
            add(sums, "own", 2, [(sums.halves, sums.own_at), (sums.quarters, sums.far_at)])
        slots = [k for k in range(3) if widths[k]]
        jobs = [job[:5] + ((slots.index(job[5][0]), job[5][1]),) for job in jobs]
        arrays, tables = [], {}
        used = [a for factor in lefts for a in factor.arrays] + [a for job in jobs for a, _ in job[4]]
        for array in used:
            if id(array) not in tables:
                tables[id(array)] = len(arrays)
                arrays.append(array)
        height = lefts[0].left[0][0].shape[2] // 2
        features = lefts[0].left[0][0].shape[2]
        tokens = max(factor.tokens for factor in lefts)
        widest = max(job[3] for job in jobs)
        depth = max(1, max(len(job[4]) for job in jobs))
        pieces = max(len(factor.left) for factor in lefts)
        rights = max(len(factor.right.all) for factor in lefts)
        outs = self.order.call(
            functools.partial(
                round_kernel, self.layers, (jobs, lefts, len(arrays), len(slots)), tables
            ),
            [
                jax.ShapeDtypeStruct((height + (margin if k == 0 else 0), widths[k]), jnp.bfloat16)
                for k in slots
            ],
            [SMEM_SPACE] + [ANY_SPACE] * len(arrays),
            [ANY_SPACE] * len(slots),
            [
                pltpu.VMEM((len(lefts), tokens, features), jnp.bfloat16),
                pltpu.VMEM((len(lefts), height, tokens), jnp.bfloat16),
                pltpu.VMEM((len(jobs), tokens, widest), jnp.bfloat16),
                pltpu.VMEM((len(jobs), depth, height, widest), jnp.bfloat16),
                pltpu.VMEM((len(jobs), height, widest), jnp.bfloat16),
                pltpu.SemaphoreType.DMA((len(lefts), pieces)),
                pltpu.SemaphoreType.DMA((len(jobs), rights + depth)),
                pltpu.SemaphoreType.DMA((len(jobs),)),
            ],
            [self.place, *arrays],
        )
        moved = {k: swap_pairs(outs[slots.index(k)], k, self.dp_size) for k in slots if k < 2}
        for sums in halves:
            sums.halves = moved[0]
        for sums in quarters:
            sums.quarters = moved[1]
        if 2 in slots:
            return lax.psum_scatter(outs[slots.index(2)], "z", scatter_dimension=0, tiled=True)

    def share(self, mine):
        summed = join(self.order, mine)
        bit = len(BITS)
        while 1 << bit < self.dp_size:
            summed = summed + swap_dp(summed, bit, self.dp_size)
            bit += 1
        near = swap_pairs(summed, 0, self.dp_size)
        far = swap_pairs(summed, 1, self.dp_size)
        return [summed, near, far, swap_pairs(near, 1, self.dp_size)]


def spread_kernel(widths, place, *refs):
    pieces, outs = refs[:QUARTERS], refs[QUARTERS:]
    quarter, core = place[0], place[2]
    base = 0
    for i, width in enumerate(widths):
        part = width // QUARTERS
        for r, place_of in enumerate((0, 1 + core, 2 - core, 3)):
            column = pl.ds(pl.multiple_of((quarter ^ place_of) * part, part), part)
            outs[i][:, column] = pieces[r][:, pl.ds(base, part)].astype(jnp.float32)
        base += part


def spread(order, place, widths, pieces):
    rows = pieces[0].shape[0]
    return order.call(
        functools.partial(spread_kernel, widths),
        [jax.ShapeDtypeStruct((rows, w), jnp.float32) for w in widths],
        [SMEM_SPACE] + [VMEM_SPACE] * QUARTERS,
        [VMEM_SPACE] * len(widths),
        [],
        [place, *pieces],
    )


class GatherSet:
    def __init__(self, place, groups):
        quarter = place[0]
        mine = [
            lax.dynamic_slice_in_dim(w, quarter * (w.shape[1] // QUARTERS), w.shape[1] // QUARTERS, 1)
            for group in groups
            for w in group
        ]
        mine = jnp.concatenate(mine, axis=1) if len(mine) > 1 else mine[0]
        self.gathered = lax.all_gather(mine, ("z", "core"), axis=0, tiled=False)


class Gather:
    def __init__(self, place, sizes, order, group, source, base, other, other_base):
        self.place, self.order, self.group = place, order, group
        self.dp_size, self.layers = sizes
        self.source, self.base, self.other, self.other_base = source, base, other, other_base
        self.width = sum(w.shape[1] for w in group) // QUARTERS

    def near(self):
        piece = pick(
            self.order, self.place, self.layers, self.source.gathered, self.base, self.width
        )
        self.piece = swap_pairs(piece, 0, self.dp_size)
        self.other_piece = swap_core(self.piece)

    def arrived(self):
        return [self.other_piece, self.rest, self.other_rest]

    def far(self):
        self.rest = swap_pairs(half(self.order, self.place, self.piece), 1, self.dp_size)
        self.other_rest = swap_core(self.rest)


def gather_small(arrays):
    rows = [a.shape[0] for a in arrays]
    packed = jnp.concatenate(arrays, axis=0)
    packed = jnp.pad(packed, ((0, -packed.shape[0] % 16), (0, 0)))
    full = lax.all_gather(packed, ("z", "core"), axis=0, tiled=False)
    full = full.transpose(1, 0, 2).reshape(packed.shape[0], -1)
    pieces, start = [], 0
    for count in rows:
        pieces.append(full[start : start + count])
        start += count
    return pieces


def pack_small(table_hot, frames_grad, vectors):
    count = table_hot.shape[1]
    extra = -(frames_grad.shape[0] + vectors.shape[0]) % 16
    left = jnp.concatenate([frames_grad, vectors, jnp.zeros((extra, vectors.shape[1]), vectors.dtype)])
    used = count + vectors.shape[0]
    share = -(-used // QUARTERS)
    unit = jnp.eye(vectors.shape[0], dtype=table_hot.dtype)
    right = jnp.block(
        [
            [table_hot, jnp.zeros((table_hot.shape[0], vectors.shape[0]), table_hot.dtype)],
            [jnp.zeros((vectors.shape[0], count), table_hot.dtype), unit],
        ]
    )
    right = jnp.pad(right, ((0, extra), (0, share * QUARTERS - used)))
    right = right.reshape(right.shape[0], QUARTERS, share)
    right = jnp.pad(right, ((0, 0), (0, 0), (0, LANES - share)))
    right = right.reshape(right.shape[0], QUARTERS * LANES)
    right = jnp.pad(right, ((0, 0), (0, left.shape[1] - right.shape[1])))
    return jnp.stack([left.astype(jnp.bfloat16), right.astype(jnp.bfloat16)])


def unpack_small(summed, counts):
    used = sum(counts)
    share = -(-used // QUARTERS)
    rows = summed.reshape(summed.shape[0], QUARTERS, LANES)[:, :, :share]
    rows = rows.reshape(summed.shape[0], QUARTERS * share).T
    pieces, start = [], 0
    for count in counts:
        pieces.append(rows[start : start + count])
        start += count
    return pieces

EPSILON = 1e-05
MASKED = -1000000000.0


def dot_rows(left, right):
    return jnp.dot(left, right, preferred_element_type=jnp.float32)


def dot_cols(left, right):
    return lax.dot_general(
        left, right, (((1,), (1,)), ((), ())), preferred_element_type=jnp.float32
    )


def dot_down(left, right):
    return jnp.dot(left.T, right, preferred_element_type=jnp.float32)


def standard(values):
    centred = values - jnp.mean(values, axis=-1, keepdims=True)
    spread = lax.rsqrt(jnp.mean(centred * centred, axis=-1, keepdims=True) + EPSILON)
    return centred * spread, spread


def norm_back(values, gradient, gain):
    shape, spread = standard(values)
    inner = gradient * gain
    back = spread * (
        inner
        - jnp.mean(inner, axis=-1, keepdims=True)
        - shape * jnp.mean(inner * shape, axis=-1, keepdims=True)
    )
    return (
        back,
        jnp.sum(gradient * shape, axis=0, keepdims=True),
        jnp.sum(gradient, axis=0, keepdims=True),
    )


def sigmoid(values):
    return 1.0 / (1.0 + jnp.exp(-values))


def silu_back(values, gradient):
    gate = sigmoid(values)
    return gradient * gate * (1.0 + values * (1.0 - gate))


CUTS = 2


def packed_shapes(parts, tokens, width):
    return [jax.ShapeDtypeStruct((parts, tokens // CUTS, width), jnp.bfloat16)] * CUTS


def store_part(outs, index, values, column=slice(None)):
    at = 0
    for out in outs:
        out[index, :, column] = values[at : at + out.shape[1]]
        at += out.shape[1]


def load_part(refs, index, width):
    return jnp.concatenate([ref[index, :, :width] for ref in refs], axis=0)


class Pieces:
    def __init__(self, gather, index):
        group = gather.group
        self.layers = gather.layers
        before = sum(w.shape[1] for w in group[:index])
        self.base = before // QUARTERS
        self.set_base = gather.base + self.base
        self.other_base = gather.other_base + before
        self.rows, self.width = group[index].shape
        self.operands = [
            group[index],
            gather.other,
            gather.source.gathered,
            gather.piece,
            gather.other_piece,
            gather.rest,
            gather.other_rest,
        ]

    @property
    def part(self):
        return self.width // QUARTERS

    @property
    def scratch(self):
        copies = 1 + (QUARTERS - 1) * 2 * self.layers
        return [
            pltpu.VMEM((QUARTERS, 2 * self.layers, self.rows, self.part), jnp.bfloat16),
            pltpu.SemaphoreType.DMA((copies,)),
        ]

    def load(self, place, refs, buffer, sems):
        own, other, gathered, piece, other_piece, rest, other_rest = refs
        quarter, layer, core = place[0], place[1], place[2]
        span = pl.ds(self.base, self.part)
        copies = []

        def move(source, target):
            copies.append(pltpu.make_async_copy(source, target, sems.at[len(copies)]))
            copies[-1].start()

        def blocks(source, index, first, count):
            for number in range(count):
                at = first + number
                row = lax.rem(layer + 1 + at // 2, self.layers) * 2 + lax.rem(at, 2)
                move(source.at[pl.ds(number * self.rows, self.rows), span], buffer.at[index, row])

        move(gathered.at[:, :, pl.ds(self.set_base, self.part)], buffer.at[quarter])
        for r in range(1, QUARTERS):
            index = quarter ^ r
            near = pl.multiple_of(index * self.part, LANES)
            far = pl.multiple_of(self.other_base + index * self.part, LANES)
            move(own.at[:, pl.ds(near, self.part)], buffer.at[index, 2 * layer + core])
            move(other.at[:, pl.ds(far, self.part)], buffer.at[index, 2 * layer + 1 - core])
        count = 2 * (self.layers - 1)
        blocks(piece, quarter ^ (1 + core), jnp.int32(0), count)
        blocks(other_piece, quarter ^ (2 - core), jnp.int32(0), count)
        blocks(rest, quarter ^ 3, core * (count // 2), count // 2)
        blocks(other_rest, quarter ^ 3, (1 - core) * (count // 2), count // 2)
        return [(quarter, copies[:1]), (quarter ^ 1, copies[1:]), (quarter ^ 2, []), (quarter ^ 3, [])]

    def block(self, buffer, index):
        return buffer[index].reshape(2 * self.layers * self.rows, self.part)


def wait_all(steps):
    for _, copies in steps:
        for copy in copies:
            copy.wait()


def up_kernel(pieces, row, ready, place, values, gains, shifts, *refs):
    weight, outs, (buffer, sems) = refs[: -3 - CUTS], refs[-3 - CUTS : -2], refs[-2:]
    expanded_out, packed = outs[0], outs[1:]
    steps = pieces.load(place, weight, buffer, sems)
    ready()
    shape, _ = standard(values[...])
    hidden = (shape * gains[row : row + 1] + shifts[row : row + 1]).astype(jnp.bfloat16)
    store_part(packed, 0, hidden)
    for r, (index, copies) in enumerate(steps):
        for copy in copies:
            copy.wait()
        expanded = dot_rows(hidden, pieces.block(buffer, index))
        expanded_out[r] = expanded.astype(jnp.bfloat16)
        store_part(packed, 1 + r, (expanded * sigmoid(expanded)).astype(jnp.bfloat16))


def up_step(order, place, gather, index, row, values, gains, shifts):
    pieces = Pieces(gather, index)
    tokens, width = values.shape
    expanded, *packed = order.call(
        functools.partial(up_kernel, pieces, row),
        [
            jax.ShapeDtypeStruct((QUARTERS, tokens, pieces.part), jnp.bfloat16),
            *packed_shapes(1 + QUARTERS, tokens, width),
        ],
        [SMEM_SPACE] + [VMEM_SPACE] * 3 + [ANY_SPACE] * len(pieces.operands),
        [VMEM_SPACE] * (1 + CUTS),
        pieces.scratch,
        [place, values, gains, shifts, *pieces.operands],
        lazy=True,
    )
    return expanded, packed


def down_sum(pieces, ready, place, packed, first, weight, buffer, sems):
    total, steps = None, pieces.load(place, weight, buffer, sems)
    ready()
    for r, (index, copies) in enumerate(steps):
        for copy in copies:
            copy.wait()
        term = dot_cols(
            load_part(packed, first + r, pieces.part), pieces.block(buffer, index)
        )
        total = term if total is None else total + term
    return total


def down_kernel(pieces, ready, place, values, *refs):
    active, weight, (out, buffer, sems) = refs[:CUTS], refs[CUTS:-3], refs[-3:]
    branch = down_sum(pieces, ready, place, active, 1, weight, buffer, sems)
    out[...] = values[...] + 0.5 * branch


def down_step(order, place, gather, index, values, active):
    pieces = Pieces(gather, index)
    return order.call(
        functools.partial(down_kernel, pieces),
        [jax.ShapeDtypeStruct(values.shape, jnp.float32)],
        [SMEM_SPACE] + [VMEM_SPACE] * (1 + CUTS) + [ANY_SPACE] * len(pieces.operands),
        [VMEM_SPACE],
        pieces.scratch,
        [place, values, *active, *pieces.operands],
        lazy=True,
    )[0]


def last_kernel(pieces, row, ready, place, values, cotangent, gains, shifts, *refs):
    active, weight, outs = refs[:CUTS], refs[CUTS:-7], refs[-7:]
    encoded, grad_out, low_out, gain_out, shift_out, buffer, sems = outs
    branch = down_sum(pieces, ready, place, active, 1, weight, buffer, sems)
    total = values[...] + 0.5 * branch
    gain = gains[row : row + 1]
    shape, _ = standard(total)
    encoded[...] = (shape * gain + shifts[row : row + 1]).astype(jnp.bfloat16)
    back, gain_grad, shift_grad = norm_back(total, cotangent[...].astype(jnp.float32), gain)
    grad_out[...] = back
    low_out[...] = (0.5 * back).astype(jnp.bfloat16)
    gain_out[...] = gain_grad
    shift_out[...] = shift_grad


def vector_shapes(width, count=2):
    return [jax.ShapeDtypeStruct((1, width), jnp.float32)] * count


def last_step(order, place, gather, index, row, values, active, cotangent, gains, shifts, through):
    pieces = Pieces(gather, index)
    return order.call(
        functools.partial(last_kernel, pieces, row),
        [
            jax.ShapeDtypeStruct(values.shape, jnp.bfloat16),
            jax.ShapeDtypeStruct(values.shape, jnp.float32),
            jax.ShapeDtypeStruct(values.shape, jnp.bfloat16),
            *vector_shapes(values.shape[1]),
        ],
        [SMEM_SPACE] + [VMEM_SPACE] * (4 + CUTS) + [ANY_SPACE] * len(pieces.operands),
        [VMEM_SPACE] * 5,
        pieces.scratch,
        [place, values, cotangent, gains, shifts, *active, *pieces.operands],
        through,
        lazy=True,
    )


def down_back_kernel(pieces, ready, place, gradient, expanded, *refs):
    weight, outs, (buffer, sems) = refs[: -2 - CUTS], refs[-2 - CUTS : -2], refs[-2:]
    steps = pieces.load(place, weight, buffer, sems)
    ready()
    store_part(outs, 0, gradient[...])
    for r, (index, copies) in enumerate(steps):
        for copy in copies:
            copy.wait()
        active_grad = dot_rows(gradient[...], pieces.block(buffer, index))
        store_part(outs, 1 + r, silu_back(expanded[r].astype(jnp.float32), active_grad).astype(jnp.bfloat16))


def down_back_step(order, place, gather, index, gradient, expanded):
    pieces = Pieces(gather, index)
    return order.call(
        functools.partial(down_back_kernel, pieces),
        packed_shapes(1 + QUARTERS, *gradient.shape),
        [SMEM_SPACE] + [VMEM_SPACE] * 2 + [ANY_SPACE] * len(pieces.operands),
        [VMEM_SPACE] * CUTS,
        pieces.scratch,
        [place, gradient, expanded, *pieces.operands],
        lazy=True,
    )


def into_norm_kernel(pieces, first, row, scale, ready, place, values, residual, gains, *refs):
    gradient, refs = refs[:CUTS], refs[CUTS:]
    weight, (grad_out, low_out, gain_out, shift_out, buffer, sems) = refs[:-6], refs[-6:]
    hidden_grad = down_sum(pieces, ready, place, gradient, first, weight, buffer, sems)
    back, gain_grad, shift_grad = norm_back(values[...], hidden_grad, gains[row : row + 1])
    total = residual[...] + back
    grad_out[...] = total
    low_out[...] = (scale * total).astype(jnp.bfloat16)
    gain_out[...] = gain_grad
    shift_out[...] = shift_grad


def into_norm_step(
    order, place, gather, index, first, row, scale, gradient, values, residual, gains, through=()
):
    pieces = Pieces(gather, index)
    return order.call(
        functools.partial(into_norm_kernel, pieces, first, row, scale),
        [
            jax.ShapeDtypeStruct(values.shape, jnp.float32),
            jax.ShapeDtypeStruct(values.shape, jnp.bfloat16),
            *vector_shapes(values.shape[1]),
        ],
        [SMEM_SPACE] + [VMEM_SPACE] * (3 + CUTS) + [ANY_SPACE] * len(pieces.operands),
        [VMEM_SPACE] * 4,
        pieces.scratch,
        [place, values, residual, gains, *gradient, *pieces.operands],
        through,
        lazy=True,
    )


def whole_weight(pieces, ready, place, weight, buffer, sems):
    steps = pieces.load(place, weight, buffer, sems)
    ready()
    wait_all(steps)


def turn(values, cosine, sine):
    return values * cosine + pltpu.roll(values, HEAD_DIM // 2, 1) * sine


def masked_scores(query, key, matching):
    return jnp.where(matching, dot_cols(query, key), MASKED)


def head(index):
    return slice(index * HEAD_DIM, (index + 1) * HEAD_DIM)


def attend_kernel(pieces, row, ready, place, values, gains, shifts, cosine, sine, down, across, *refs):
    weight, outs = refs[:-6], refs[-6:]
    turned_out, totals_out, packed, projected, buffer, sems = outs
    steps = pieces.load(place, weight, buffer, sems)
    ready()
    shape, _ = standard(values[...])
    hidden = (shape * gains[row : row + 1] + shifts[row : row + 1]).astype(jnp.bfloat16)
    packed[0] = hidden
    for index, copies in steps:
        for copy in copies:
            copy.wait()
        column = pl.ds(pl.multiple_of(index * pieces.part, pieces.part), pieces.part)
        projected[:, column] = dot_rows(hidden, pieces.block(buffer, index))
    heads = pieces.width // (3 * HEAD_DIM)
    matching = down[...] == across[...]
    for h in range(heads):
        query = turn(projected[:, head(h)], cosine[...], sine[...]) * HEAD_DIM ** (-0.5)
        key = turn(projected[:, head(heads + h)], cosine[...], sine[...])
        query, key = query.astype(jnp.bfloat16), key.astype(jnp.bfloat16)
        value = projected[:, head(2 * heads + h)].astype(jnp.bfloat16)
        turned_out[:, head(h)] = query
        turned_out[:, head(heads + h)] = key
        turned_out[:, head(2 * heads + h)] = value
        scores = masked_scores(query, key, matching)
        highest = jnp.max(scores, axis=-1, keepdims=True)
        powers = jnp.exp(scores - highest)
        total = jnp.sum(powers, axis=-1, keepdims=True)
        totals_out[:, h : h + 1] = highest + jnp.log(total)
        probs = (powers / total).astype(jnp.bfloat16)
        packed[1, :, head(h)] = dot_rows(probs, value).astype(jnp.bfloat16)


def attend_step(order, place, gather, index, row, values, gains, shifts, cosine, sine, down, across):
    pieces = Pieces(gather, index)
    tokens, width = values.shape
    heads = pieces.width // (3 * HEAD_DIM)
    return order.call(
        functools.partial(attend_kernel, pieces, row),
        [
            jax.ShapeDtypeStruct((tokens, pieces.width), jnp.bfloat16),
            jax.ShapeDtypeStruct((tokens, heads), jnp.float32),
            jax.ShapeDtypeStruct((2, tokens, width), jnp.bfloat16),
        ],
        [SMEM_SPACE] + [VMEM_SPACE] * 7 + [ANY_SPACE] * len(pieces.operands),
        [VMEM_SPACE] * 3,
        [pltpu.VMEM((tokens, pieces.width), jnp.float32), *pieces.scratch],
        [place, values, gains, shifts, cosine, sine, down, across, *pieces.operands],
        lazy=True,
    )


def to_quarters(place, outs, column, values):
    part = values.shape[1] // QUARTERS
    for r in range(QUARTERS):
        block = values[:, pl.ds(pl.multiple_of((place[0] ^ r) * part, part), part)]
        store_part(outs, r, block, slice(column, column + part))


def attend_back_kernel(pieces, ready, place, gradient, turned, totals, cosine, sine, down, across, *refs):
    weight, rest = refs[: -4 - CUTS], refs[-4 - CUTS :]
    outs, (out, mixed_grad, buffer, sems) = rest[:CUTS], rest[CUTS:]
    heads = turned.shape[1] // (3 * HEAD_DIM)
    whole_weight(pieces, ready, place, weight, buffer, sems)
    total = None
    for index in range(QUARTERS):
        column = slice(index * pieces.part, (index + 1) * pieces.part)
        term = dot_cols(gradient[:, column], pieces.block(buffer, index))
        total = term if total is None else total + term
    mixed_grad[...] = total.astype(jnp.bfloat16)
    matching = down[...] == across[...]
    for h in range(heads):
        query = turned[:, head(h)]
        key = turned[:, head(heads + h)]
        value = turned[:, head(2 * heads + h)]
        gradient_h = mixed_grad[:, head(h)]
        probs = jnp.exp(masked_scores(query, key, matching) - totals[:, h : h + 1])
        value_grad = dot_down(probs.astype(jnp.bfloat16), gradient_h)
        probs_grad = dot_cols(gradient_h, value)
        inner = jnp.sum(probs * probs_grad, axis=-1, keepdims=True)
        score_grad = (probs * (probs_grad - inner)).astype(jnp.bfloat16)
        query_grad = dot_rows(score_grad, key) * HEAD_DIM ** (-0.5)
        key_grad = dot_down(score_grad, query)
        out[:, head(h)] = turn(query_grad, cosine[...], -sine[...]).astype(jnp.bfloat16)
        out[:, head(heads + h)] = turn(key_grad, cosine[...], -sine[...]).astype(jnp.bfloat16)
        out[:, head(2 * heads + h)] = value_grad.astype(jnp.bfloat16)
    to_quarters(place, outs, 0, out)
    to_quarters(place, outs, out.shape[1] // QUARTERS, gradient)


def attend_back_step(order, place, gather, index, gradient, turned, totals, cosine, sine, down, across):
    pieces = Pieces(gather, index)
    return order.call(
        functools.partial(attend_back_kernel, pieces),
        packed_shapes(
            QUARTERS, turned.shape[0], (turned.shape[1] + gradient.shape[1]) // QUARTERS
        ),
        [SMEM_SPACE] + [VMEM_SPACE] * 7 + [ANY_SPACE] * len(pieces.operands),
        [VMEM_SPACE] * CUTS,
        [
            pltpu.VMEM(turned.shape, jnp.bfloat16),
            pltpu.VMEM(gradient.shape, jnp.bfloat16),
            *pieces.scratch,
        ],
        [place, gradient, turned, totals, cosine, sine, down, across, *pieces.operands],
        lazy=True,
    )


def rows_sum(pieces, buffer, left):
    return jnp.concatenate(
        [dot_rows(left, pieces.block(buffer, index)) for index in range(QUARTERS)], axis=1
    )


def shifted(values, amount):
    return values if amount == 0 else pltpu.roll(values, amount % values.shape[0], 0)


def merge_kernel(pieces, ready, place, values, mixed, *refs):
    weight, (out, buffer, sems) = refs[:-3], refs[-3:]
    whole_weight(pieces, ready, place, weight, buffer, sems)
    for index in range(QUARTERS):
        column = slice(index * pieces.part, (index + 1) * pieces.part)
        out[:, column] = values[:, column] + dot_rows(mixed[1], pieces.block(buffer, index))


def merge_step(order, place, gather, index, values, mixed):
    pieces = Pieces(gather, index)
    return order.call(
        functools.partial(merge_kernel, pieces),
        [jax.ShapeDtypeStruct(values.shape, jnp.float32)],
        [SMEM_SPACE] + [VMEM_SPACE] * 2 + [ANY_SPACE] * len(pieces.operands),
        [VMEM_SPACE],
        pieces.scratch,
        [place, values, mixed, *pieces.operands],
        lazy=True,
    )[0]


def conv_kernel(weights, row, ready, place, values, gains, shifts, taps, keep, *refs):
    count = len(weights[0].operands)
    operands = [refs[i * count : (i + 1) * count] for i in range(len(weights))]
    rest = refs[len(weights) * count :]
    done_out, doubled_out, filtered_out, packed = rest[:4]
    scratch = rest[4:]
    buffers = [scratch[2 * i : 2 * i + 2] for i in range(len(weights))]
    steps = [w.load(place, o, *b) for w, o, b in zip(weights, operands, buffers)]
    gating, pointwise = weights
    ready()
    shape, _ = standard(values[...])
    hidden = (shape * gains[row : row + 1] + shifts[row : row + 1]).astype(jnp.bfloat16)
    packed[0] = hidden
    wait_all(steps[0])
    doubled = rows_sum(gating, buffers[0][0], hidden)
    doubled_out[...] = doubled.astype(jnp.bfloat16)
    half = gating.width // 2
    gated = doubled[:, :half] * sigmoid(doubled[:, half:])
    reach = taps.shape[0] // 2
    filtered = None
    for k in range(taps.shape[0]):
        term = shifted(gated, reach - k) * keep[:, k : k + 1] * taps[k : k + 1]
        filtered = term if filtered is None else filtered + term
    filtered_out[...] = filtered
    shape, _ = standard(filtered)
    renormed = shape * gains[row + 1 : row + 2] + shifts[row + 1 : row + 2]
    active = (renormed * sigmoid(renormed)).astype(jnp.bfloat16)
    packed[1] = active
    wait_all(steps[1])
    for index in range(QUARTERS):
        column = slice(index * pointwise.part, (index + 1) * pointwise.part)
        term = dot_rows(active, pointwise.block(buffers[1][0], index))
        done_out[:, column] = values[:, column] + term


def conv_step(order, place, gather, row, values, gains, shifts, taps, keep):
    weights = [Pieces(gather, i) for i in range(2)]
    tokens, width = values.shape
    operands = [o for w in weights for o in w.operands]
    return order.call(
        functools.partial(conv_kernel, weights, row),
        [
            jax.ShapeDtypeStruct((tokens, width), jnp.float32),
            jax.ShapeDtypeStruct((tokens, weights[0].width), jnp.bfloat16),
            jax.ShapeDtypeStruct((tokens, weights[0].width // 2), jnp.float32),
            jax.ShapeDtypeStruct((2, tokens, width), jnp.bfloat16),
        ],
        [SMEM_SPACE] + [VMEM_SPACE] * 5 + [ANY_SPACE] * len(operands),
        [VMEM_SPACE] * 4,
        [s for w in weights for s in w.scratch],
        [place, values, gains, shifts, taps, keep, *operands],
        lazy=True,
    )


def conv_back_kernel(pieces, row, ready, place, gradient, filtered, doubled, gains, shifts, taps, keep, *refs):
    weight, rest = refs[: -6 - CUTS], refs[-6 - CUTS :]
    outs = rest[:CUTS]
    gain_out, shift_out, taps_out, doubled_grad, buffer, sems = rest[CUTS:]
    whole_weight(pieces, ready, place, weight, buffer, sems)
    total = None
    for index in range(QUARTERS):
        column = slice(index * pieces.part, (index + 1) * pieces.part)
        term = dot_cols(gradient[:, column], pieces.block(buffer, index))
        total = term if total is None else total + term
    gain = gains[row : row + 1]
    shape, _ = standard(filtered[...])
    renormed = shape * gain + shifts[row : row + 1]
    back, gain_grad, shift_grad = norm_back(filtered[...], silu_back(renormed, total), gain)
    gain_out[...] = gain_grad
    shift_out[...] = shift_grad
    half = doubled.shape[1] // 2
    gate = sigmoid(doubled[:, half:].astype(jnp.float32))
    gated = doubled[:, :half].astype(jnp.float32) * gate
    reach = taps.shape[0] // 2
    gated_grad = None
    for k in range(taps.shape[0]):
        kept = back * keep[:, k : k + 1]
        taps_out[k : k + 1] = jnp.sum(kept * shifted(gated, reach - k), axis=0, keepdims=True)
        term = shifted(kept, k - reach) * taps[k : k + 1]
        gated_grad = term if gated_grad is None else gated_grad + term
    doubled_grad[:, :half] = (gated_grad * gate).astype(jnp.bfloat16)
    doubled_grad[:, half:] = (gated_grad * gated * (1.0 - gate)).astype(jnp.bfloat16)
    to_quarters(place, outs, 0, doubled_grad)
    to_quarters(place, outs, doubled_grad.shape[1] // QUARTERS, gradient)


def conv_back_step(order, place, gather, index, row, gradient, filtered, doubled, gains, shifts, taps, keep):
    pieces = Pieces(gather, index)
    width = filtered.shape[1]
    return order.call(
        functools.partial(conv_back_kernel, pieces, row),
        [
            *packed_shapes(
                QUARTERS, doubled.shape[0], (doubled.shape[1] + gradient.shape[1]) // QUARTERS
            ),
            *vector_shapes(width),
            jax.ShapeDtypeStruct(taps.shape, jnp.float32),
        ],
        [SMEM_SPACE] + [VMEM_SPACE] * 7 + [ANY_SPACE] * len(pieces.operands),
        [VMEM_SPACE] * (3 + CUTS),
        [pltpu.VMEM(doubled.shape, jnp.bfloat16), *pieces.scratch],
        [place, gradient, filtered, doubled, gains, shifts, taps, keep, *pieces.operands],
        lazy=True,
    )


def shards(
    sizes,
    frames,
    lengths,
    languages,
    embedding,
    gains,
    shifts,
    firstup,
    firstdown,
    projection,
    merger,
    gating,
    kernel,
    pointwise,
    secondup,
    seconddown,
    cotangent,
):
    frame_count = frames.shape[0]
    dp_index = lax.axis_index("dp").astype(jnp.int32)
    place = jnp.stack(
        [
            lax.rem(dp_index, jnp.int32(QUARTERS)),
            lax.axis_index("z").astype(jnp.int32),
            lax.axis_index("core").astype(jnp.int32),
        ]
    )
    order = Order(frames)
    order_of_groups = (
        ([firstup], [firstdown]),
        ([projection, merger], [gating, pointwise]),
        ([secondup],),
        ([seconddown],),
    )
    sources = [GatherSet(place, groups) for groups in order_of_groups]
    everything = jnp.concatenate([w for s in order_of_groups for g in s for w in g], axis=1)
    everything_other = swap_core(everything)
    gathers, other_base = [], 0
    for source, groups in zip(sources, order_of_groups):
        base = 0
        for group in groups:
            gathers.append(
                Gather(place, sizes, order, group, source, base, everything_other, other_base)
            )
            base += gathers[-1].width
            other_base += QUARTERS * gathers[-1].width
    table_full, gain_full, shift_full, kernel_full = gather_small(
        [embedding, gains, shifts, kernel]
    )
    segment_all, position_all, language_all = layout(lengths, languages, frame_count)
    segment = segment_all[0]
    language_row = language_all[0]
    cosine, sine = angles(position_all[0])
    cosine = jnp.concatenate([cosine, cosine], axis=-1)[:, 0]
    sine = jnp.concatenate([-sine, sine], axis=-1)[:, 0]
    down, across = segment[:, None], segment[None, :]
    gain_rows = gain_full.astype(jnp.float32)
    shift_rows = shift_full.astype(jnp.float32)
    taps = kernel_full.astype(jnp.float32)
    reach = taps.shape[0] // 2
    segment_pad = jnp.pad(segment, (reach, reach), constant_values=-1)
    keep = jnp.stack(
        [segment_pad[k : k + frame_count] == segment for k in range(taps.shape[0])], axis=1
    ).astype(jnp.float32)
    language_hot = (
        language_row[:, None] == jnp.arange(table_full.shape[0], dtype=jnp.int32)[None, :]
    ).astype(jnp.float32)
    start_sum = frames.astype(jnp.float32) + jnp.dot(
        language_hot.astype(jnp.bfloat16), table_full, preferred_element_type=jnp.float32
    )

    gathers[0].near()
    order.wait(everything_other)
    gathers[0].far()
    gathers[1].near()
    order.wait(*gathers[0].arrived())
    gathers[1].far()
    gathers[2].near()
    first_expanded, first_packed = up_step(
        order, place, gathers[0], 0, 0, start_sum, gain_rows, shift_rows
    )
    order.wait(*gathers[1].arrived())
    gathers[2].far()
    gathers[3].near()
    after_first = down_step(order, place, gathers[1], 0, start_sum, first_packed)
    order.wait(*gathers[2].arrived())
    gathers[3].far()
    gathers[4].near()
    turned, totals, attend_packed = attend_step(
        order, place, gathers[2], 0, 1, after_first, gain_rows, shift_rows, cosine, sine, down, across
    )
    after_attention = merge_step(order, place, gathers[2], 1, after_first, attend_packed)
    order.wait(*gathers[3].arrived())
    gathers[4].far()
    gathers[5].near()
    after_conv, doubled, filtered, conv_packed = conv_step(
        order, place, gathers[3], 2, after_attention, gain_rows, shift_rows, taps, keep
    )
    order.wait(*gathers[4].arrived())
    gathers[5].far()
    second_expanded, second_packed = up_step(
        order, place, gathers[4], 0, 4, after_conv, gain_rows, shift_rows
    )
    encoded, grad_second, low_second, final_gain, final_shift, *held = last_step(
        order,
        place,
        gathers[5],
        0,
        5,
        after_conv,
        second_packed,
        cotangent,
        gain_rows,
        shift_rows,
        [*second_packed, conv_packed, attend_packed],
    )
    *second_packed, conv_packed, attend_packed = held
    forward, conv_forward, attend_forward = (
        Packed(second_packed),
        Packed([conv_packed]),
        Packed([attend_packed]),
    )
    rounds = Rounds(place, sizes, order)
    width = frames.shape[1]

    packed = down_back_step(order, place, gathers[5], 0, low_second, second_expanded)
    backward = Packed(packed)
    grad_conv, low_conv, second_gain, second_shift, *first_packed = into_norm_step(
        order,
        place,
        gathers[4],
        0,
        1,
        4,
        1.0,
        packed,
        after_conv,
        grad_second,
        gain_rows,
        first_packed,
    )
    first_forward = Packed(first_packed)
    down_two = Sums(Factor(backward, 0, forward, 1, 0, seconddown.shape[1]))
    up_two = Sums(Factor(forward, 0, backward, 1, 0, secondup.shape[1]))
    order.wait(*conv_forward.all, *attend_forward.all)
    rounds.step([down_two], margin=80)
    order.wait(*first_forward.all)
    rounds.step([up_two], margin=64)
    *packed, inner_gain, inner_shift, taps_grad = conv_back_step(
        order, place, gathers[3], 1, 3, low_conv, filtered, doubled, gain_rows, shift_rows, taps, keep
    )
    backward = Packed(packed)
    grad_attention, low_attention, outer_gain, outer_shift = into_norm_step(
        order,
        place,
        gathers[3],
        0,
        0,
        2,
        1.0,
        packed,
        after_attention,
        grad_conv,
        gain_rows,
    )
    conv = Sums(
        Factor(conv_forward, 0, backward, 0, 0, gating.shape[1]),
        Factor(conv_forward, 1, backward, 0, gating.shape[1] // QUARTERS, pointwise.shape[1]),
    )
    order.wait(*backward.all)
    packed = attend_back_step(
        order, place, gathers[2], 1, low_attention, turned, totals, cosine, sine, down, across
    )
    backward = Packed(packed)
    rounds.step([conv], [down_two], margin=48)
    grad_first, low_first, attend_gain, attend_shift = into_norm_step(
        order,
        place,
        gathers[2],
        0,
        0,
        1,
        0.5,
        packed,
        after_first,
        grad_attention,
        gain_rows,
    )
    attend = Sums(
        Factor(attend_forward, 0, backward, 0, 0, projection.shape[1]),
        Factor(attend_forward, 1, backward, 0, projection.shape[1] // QUARTERS, merger.shape[1]),
    )
    order.wait(*backward.all)
    packed = down_back_step(order, place, gathers[1], 0, low_first, first_expanded)
    backward = Packed(packed)
    down_two_mine = rounds.step([attend], [up_two], [down_two], margin=32)
    frames_grad, low_start, first_gain, first_shift = into_norm_step(
        order, place, gathers[0], 0, 1, 0, 1.0, packed, start_sum, grad_first, gain_rows
    )
    down_one = Sums(Factor(backward, 0, first_forward, 1, 0, firstdown.shape[1]))
    up_one = Sums(Factor(first_forward, 0, backward, 1, 0, firstup.shape[1]))
    vectors = jnp.concatenate(
        [
            first_gain,
            attend_gain,
            outer_gain,
            inner_gain,
            second_gain,
            final_gain,
            first_shift,
            attend_shift,
            outer_shift,
            inner_shift,
            second_shift,
            final_shift,
            taps_grad,
        ]
    )
    small_packed = Packed([pack_small(language_hot, low_start, vectors)])
    small = Sums(Factor(small_packed, 0, small_packed, 1, 0, QUARTERS * LANES, relative=False))
    up_two_mine = rounds.step([down_one], [conv], [up_two], margin=16)
    conv_mine = rounds.step([up_one], [attend], [conv])
    order.wait(down_two_mine)
    attend_mine = rounds.step([small], [down_one], [attend])
    order.wait(up_two_mine)
    down_one_mine = rounds.step([], [up_one, small], [down_one])
    order.wait(conv_mine)
    last_mine = rounds.step([], [], [up_one, small])
    ffn_pieces = rounds.share([down_two_mine, up_two_mine])
    order.wait(attend_mine)
    middle_pieces = rounds.share([conv_mine, attend_mine])
    seconddown_grad, secondup_grad = spread(
        order, place, [seconddown.shape[1], secondup.shape[1]], ffn_pieces
    )
    middle = [gating, pointwise, projection, merger]
    gating_grad, pointwise_grad, projection_grad, merger_grad = spread(
        order, place, [w.shape[1] for w in middle], middle_pieces
    )
    last_pieces = rounds.share([down_one_mine, last_mine])
    firstdown_grad, firstup_grad, small = spread(
        order, place, [firstdown.shape[1], firstup.shape[1], QUARTERS * LANES], last_pieces
    )
    counts = [embedding.shape[0], gains.shape[0], shifts.shape[0], kernel.shape[0]]
    table_sum, gain_sum, shift_sum, taps_sum = unpack_small(small, counts)
    return (
        encoded,
        frames_grad,
        table_sum,
        gain_sum,
        shift_sum,
        firstup_grad,
        firstdown_grad,
        projection_grad,
        merger_grad,
        gating_grad,
        taps_sum,
        pointwise_grad,
        secondup_grad,
        seconddown_grad,
    )


def solution(mesh):
    dp_size, fsdp_size = mesh.shape["dp"], mesh.shape["fsdp"]
    layers = fsdp_size // 2
    split = Mesh(mesh.devices.reshape(dp_size, layers, 2), ("dp", "z", "core"))
    return jax.shard_map(
        functools.partial(shards, (dp_size, layers)),
        mesh=split,
        in_specs=(
            P(("dp", "z", "core"), None),
            P(("dp", "z", "core"), None),
            P(("dp", "z", "core"), None),
            P(None, ("z", "core")),
            P(None, ("z", "core")),
            P(None, ("z", "core")),
            P(("z", "core"), None),
            P(("z", "core"), None),
            P(("z", "core"), None),
            P(("z", "core"), None),
            P(("z", "core"), None),
            P(None, ("z", "core")),
            P(("z", "core"), None),
            P(("z", "core"), None),
            P(("z", "core"), None),
            P(("dp", "z", "core"), None),
        ),
        out_specs=(
            P(("dp", "z", "core"), None),
            P(("dp", "z", "core"), None),
            P(None, ("z", "core")),
            P(None, ("z", "core")),
            P(None, ("z", "core")),
            P(("z", "core"), None),
            P(("z", "core"), None),
            P(("z", "core"), None),
            P(("z", "core"), None),
            P(("z", "core"), None),
            P(None, ("z", "core")),
            P(("z", "core"), None),
            P(("z", "core"), None),
            P(("z", "core"), None),
        ),
        check_vma=False,
    )
```

time: 832 us -> 684 us (0.82)
  waiting for transfers between devices: 398 us -> 294 us
  Pallas kernels: 194 us -> 266 us
  local copies, waits for them, and re-layouts: 115 us -> 43.5 us
  starting transfers between devices: 71.8 us -> 34.3 us
    reduce_scatter x6, waiting for transfers between devices: 77.6 us -> 0.05 us  [step(): lax.psum_scatter(outs[slots.index(2)], 'z', scatter_dimension=0, tiled=True)]
    pallas_call x45 -> x42, Pallas kernels: 194 us -> 266 us  [call(): pl.pallas_call(body, out_shape=[*out_shape, *[jax.ShapeDtypeStruct(x.shap...]
    unnamed x628 -> x173, local copies, waits for them, and re-layouts: 95.3 us -> 30.1 us
    ppermute x54 -> x34, starting transfers between devices: 57.5 us -> 26.7 us  [swap_pairs(): return lax.ppermute(value, ('dp', 'core'), pairs)]
    ppermute x54 -> x34, waiting for transfers between devices: 301 us -> 273 us  [swap_pairs(): return lax.ppermute(value, ('dp', 'core'), pairs)]
    all_gather x6 -> x4, waiting for transfers between devices: 12.8 us -> 19 us  [__init__(): self.gathered = lax.all_gather(mine, ('z', 'core'), axis=0, tiled=False)]
  transfers between devices with their start and end apart: 128 -> 72, of which waited for: 32 -> 27; matrix products, arithmetic and copies ran while one was open for 3% -> 4% of each run, Pallas kernels for 22% -> 34%
where the time goes in v3:
time: 684 us; the launch traced here: 680 us
  waiting for transfers between devices  294 us (43%)
  Pallas kernels  266 us (39%)
  local copies, waits for them, and re-layouts  43.5 us (6%)
  starting transfers between devices  34.3 us (5%)
  blocking collectives  18.8 us (3%)
  between operations  15.9 us (2%)
    ppermute x34, waiting for transfers between devices, swap_pairs(): return lax.ppermute(value, ('dp', 'core'), pairs)  273 us
    pallas_call x42, Pallas kernels, call(): pl.pallas_call(body, out_shape=[*out_shape, *[jax.ShapeDtypeStruct(x.shap...  266 us
    unnamed x173, local copies, waits for them, and re-layouts  30.1 us
    ppermute x34, starting transfers between devices, swap_pairs(): return lax.ppermute(value, ('dp', 'core'), pairs)  26.7 us
    all_gather x4, waiting for transfers between devices, __init__(): self.gathered = lax.all_gather(mine, ('z', 'core'), axis=0, tiled=False)  19 us
    all_gather x1, blocking collectives, gather_small(): full = lax.all_gather(packed, ('z', 'core'), axis=0, tiled=False)  18.8 us
  transfers between devices with their start and end apart: 72, of which 27 were waited for; matrix products, arithmetic and copies ran while one was open for 4% of the time, Pallas kernels for 34%

profile of v3, /device:TPU:0, one launch (start us, length us, event | category | flops | bytes accessed | tf_op | source)
XLA Modules:
  0.0 679.6 jit_solution(11268332184973353319)
XLA Ops:
  22.2 18.8 %all-gather = bf16[1024,128]{1,0:T(8,128)(2,1)S(1)} all-gather(bf16[128,128]{1,0:T(8,128)(2,1)S(1)} %fusion.9), channel_id=2, replica_groups=mesh['dp'=4,'z'=4,'core'=2] {'z','core'}, dimensions={0}, use_global_device_ids=true | all-gather | bytes 294912 | tf_op jit(solution)/shard_map/all_gather | solution.py:458
  43.5 18.9 %all-gather.10.cloned.1.call-done = bf16[1024,2048]{1,0:T(8,128)(2,1)} async-done(((bf16[128,2048]{1,0:T(8,128)(2,1)}), bf16[1024,2048]{1,0:T(8,128)(2,1)}) %all-gather.10.cloned.1.call-update) | async-done | bytes 4194320 | tf_op jit(solution)/shard_map/all_gather | solution.py:429
  68.0 18.4 %collective-permute-done.1.refs_1_.refs_7_.refs_9_ = bf16[768,1024]{1,0:T(8,128)(2,1)S(1)} collective-permute-done((bf16[768,1024]{1,0:T(8,128)(2,1)}, bf16[768,1024]{1,0:T(8,128)(2,1)S(1)}, u32[]{:S(2)}, u32[]{:S(2)}) %collective-permute-start.1) | collective-permute-done | bytes 1572896 | tf_op jit(solution)/shard_map/ppermute | solution.py:121
  96.6 19.2 %collective-permute-done.3.refs_3_.refs_9_.refs_11_ = bf16[384,1024]{1,0:T(8,128)(2,1)S(1)} collective-permute-done((bf16[384,1024]{1,0:T(8,128)(2,1)}, bf16[384,1024]{1,0:T(8,128)(2,1)S(1)}, u32[]{:S(2)}, u32[]{:S(2)}) %collective-permute-start.3) | collective-permute-done | bytes 786464 | tf_op jit(solution)/shard_map/ppermute | solution.py:121
  132.1 20.0 %collective-permute-done.7.refs_3_.refs_9_.refs_8_ = bf16[384,1024]{1,0:T(8,128)(2,1)S(1)} collective-permute-done((bf16[384,1024]{1,0:T(8,128)(2,1)S(1)}, bf16[384,1024]{1,0:T(8,128)(2,1)S(1)}, u32[]{:S(2)}, u32[]{:S(2)}) %collective-permute-start.7) | collective-permute-done | bytes 786464 | tf_op jit(solution)/shard_map/ppermute | solution.py:121
  155.8 10.2 %shard_map.271 = (bf16[4,256,1024]{2,1,0:T(8,128)(2,1)}, bf16[5,128,1024]{2,1,0:T(8,128)(2,1)}, bf16[5,128,1024]{2,1,0:T(8,128)(2,1)}, bf16[256,1024]{1,0:T(8,128)(2,1)}) custom-call(s32[3]{0:T(128)} %pad_add_fusion.refs_0_, f32[256,1024]{1,0:T(8,128)} %convolution_add_fusion.refs_1_, ...), custom_call_target="tpu_custom_call", output_to_operand_aliasing={{3}: (11, {})} | custom-call | tf_op jit(solution)/shard_map/pallas_call | solution.py:87
  175.5 12.2 %collective-permute-done.11.refs_3_.refs_13_.refs_8_.refs_11_ = bf16[384,1024]{1,0:T(8,128)(2,1)S(1)} collective-permute-done((bf16[384,1024]{1,0:T(8,128)(2,1)}, bf16[384,1024]{1,0:T(8,128)(2,1)S(1)}, u32[]{:S(2)}, u32[]{:S(2)}) %collective-permute-start.11) | collective-permute-done | bytes 786464 | tf_op jit(solution)/shard_map/ppermute | solution.py:121
  204.9 15.6 %collective-permute-done.15.refs_3_.refs_11_.refs_18_.refs_13_ = bf16[384,768]{1,0:T(8,128)(2,1)S(1)} collective-permute-done((bf16[384,768]{1,0:T(8,128)(2,1)S(1)}, bf16[384,768]{1,0:T(8,128)(2,1)S(1)}, u32[]{:S(2)}, u32[]{:S(2)}) %collective-permute-start.15) | collective-permute-done | bytes 589856 | tf_op jit(solution)/shard_map/ppermute | solution.py:121
  246.8 20.5 %collective-permute-done.19.refs_3_.refs_9_.refs_11_ = bf16[384,1024]{1,0:T(8,128)(2,1)} collective-permute-done((bf16[384,1024]{1,0:T(8,128)(2,1)}, bf16[384,1024]{1,0:T(8,128)(2,1)}, u32[]{:S(2)}, u32[]{:S(2)}) %collective-permute-start.19) | collective-permute-done | bytes 786464 | tf_op jit(solution)/shard_map/ppermute | solution.py:121
  269.8 10.0 %shard_map.281 = (f32[256,1024]{1,0:T(8,128)}, bf16[256,2048]{1,0:T(8,128)(2,1)}, f32[256,1024]{1,0:T(8,128)}, bf16[2,256,1024]{2,1,0:T(8,128)(2,1)}, bf16[256,1024]{1,0:T(8,128)(2,1)}) custom-call(s32[3]{0:T(128)} %pad_add_fusion.refs_0_, f32[256,1024]{1,0:T(8,128)} %get-tuple-element.174.refs_1_, ...), custom_call_target="tpu_custom_call", output_to_operand_aliasing={{4}: (20, {})} | custom-call | tf_op jit(solution)/shard_map/pallas_call | solution.py:87
  284.8 11.6 %collective-permute-done.23.refs_12_.refs_8_ = bf16[384,1024]{1,0:T(8,128)(2,1)S(1)} collective-permute-done((bf16[384,1024]{1,0:T(8,128)(2,1)}, bf16[384,1024]{1,0:T(8,128)(2,1)S(1)}, u32[]{:S(2)}, u32[]{:S(2)}) %collective-permute-start.23) | collective-permute-done | bytes 786464 | tf_op jit(solution)/shard_map/ppermute | solution.py:121
  296.4 10.0 %shard_map.283 = (bf16[4,256,1024]{2,1,0:T(8,128)(2,1)}, bf16[5,128,1024]{2,1,0:T(8,128)(2,1)}, bf16[5,128,1024]{2,1,0:T(8,128)(2,1)}, bf16[256,1024]{1,0:T(8,128)(2,1)}) custom-call(s32[3]{0:T(128)} %pad_add_fusion.refs_0_, f32[256,1024]{1,0:T(8,128)} %get-tuple-element.180.refs_1_, ...), custom_call_target="tpu_custom_call", output_to_operand_aliasing={{3}: (11, {})} | custom-call | tf_op jit(solution)/shard_map/pallas_call | solution.py:87
  311.3 10.0 %shard_map.284 = (bf16[256,1024]{1,0:T(8,128)(2,1)}, f32[256,1024]{1,0:T(8,128)}, bf16[256,1024]{1,0:T(8,128)(2,1)}, f32[1,1024]{1,0:T(1,128)}, f32[1,1024]{1,0:...) custom-call(s32[3]{0:T(128)} %pad_add_fusion.refs_0_, ...), custom_call_target="tpu_custom_call", output_to_operand_aliasing={{5}: (14, {}), {6}: (15, {}), {7}: (16, {}), {8}: (17, {}),... | custom-call | tf_op jit(solution)/shard_map/pallas_call | solution.py:87
  322.0 10.2 %shard_map.285 = (bf16[5,128,1024]{2,1,0:T(8,128)(2,1)}, bf16[5,128,1024]{2,1,0:T(8,128)(2,1)}, bf16[256,1024]{1,0:T(8,128)(2,1)}) custom-call(s32[3]{0:T(128)} %pad_add_fusion.refs_0_, bf16[256,1024]{1,0:T(8,128)(2,1)} %get-tuple-element.192.refs_1_, bf16[4,256,1024]{2,1,0:T(8,128)(2,1)} %get-tuple-element.193.refs_2_, ...), custom_call_target="tpu_custom_call", output_to_operand_aliasing={{2}: (10, {})} | custom-call | tf_op jit(solution)/shard_map/pallas_call | solution.py:87
  333.4 9.9 %shard_map.286 = (f32[256,1024]{1,0:T(8,128)}, bf16[256,1024]{1,0:T(8,128)(2,1)}, f32[1,1024]{1,0:T(1,128)}, f32[1,1024]{1,0:T(1,128)}, bf16[5,128,1024]{2,1,0:T...) custom-call(s32[3]{0:T(128)} %pad_add_fusion.refs_0_, ...), custom_call_target="tpu_custom_call", output_to_operand_aliasing={{4}: (13, {}), {5}: (14, {}), {6}: (15, {})} | custom-call | tf_op jit(solution)/shard_map/pallas_call | solution.py:87
  416.3 11.2 %shard_map.295 = (bf16[544,2048]{1,0:T(8,128)(2,1)}, bf16[512,1024]{1,0:T(8,128)(2,1)}, bf16[512,1024]{1,0:T(8,128)(2,1)}, bf16[256,1024]{1,0:T(8,128)(2,1)}) custom-call(s32[3]{0:T(128)} %pad_add_fusion.refs_0_, bf16[2,256,1024]{2,1,0:T(8,128)(2,1)} %get-tuple-element.207.refs_11_.refs_1_.refs_9_, ...), custom_call_target="tpu_custom_call", output_to_operand_aliasing={{3}: (18, {})} | custom-call | tf_op jit(solution)/shard_map/pallas_call | solution.py:87
  440.9 20.3 %collective-permute-done.44.refs_23_.refs_22_ = bf16[560,1536]{1,0:T(8,128)(2,1)} collective-permute-done((bf16[560,1536]{1,0:T(8,128)(2,1)}, bf16[560,1536]{1,0:T(8,128)(2,1)}, u32[]{:S(2)}, u32[]{:S(2)}) %collective-permute-start.44) | collective-permute-done | bytes 1720352 | tf_op jit(solution)/shard_map/ppermute | solution.py:121
  461.3 10.1 %shard_map.297 = (bf16[528,2048]{1,0:T(8,128)(2,1)}, bf16[512,768]{1,0:T(8,128)(2,1)}, bf16[512,1024]{1,0:T(8,128)(2,1)}, bf16[256,1024]{1,0:T(8,128)(2,1)}) custom-call(s32[3]{0:T(128)} %pad_add_fusion.refs_0_, bf16[5,128,1024]{2,1,0:T(8,128)(2,1)} %get-tuple-element.228.refs_4_.refs_1_.refs_5_.refs_3_, ...), custom_call_target="tpu_custom_call", output_to_operand_aliasing={{3}: (26, {})} | custom-call | tf_op jit(solution)/shard_map/pallas_call | solution.py:87
  473.2 19.2 %collective-permute-done.46.refs_23_ = bf16[512,768]{1,0:T(8,128)(2,1)S(1)} collective-permute-done((bf16[512,768]{1,0:T(8,128)(2,1)}, bf16[512,768]{1,0:T(8,128)(2,1)S(1)}, u32[]{:S(2)}, u32[]{:S(2)}) %collective-permute-start.46) | collective-permute-done | bytes 786464 | tf_op jit(solution)/shard_map/ppermute | solution.py:121
  493.5 11.0 %shard_map.298 = (bf16[512,2048]{1,0:T(8,128)(2,1)}, bf16[512,1024]{1,0:T(8,128)(2,1)}, bf16[512,768]{1,0:T(8,128)(2,1)}, bf16[256,1024]{1,0:T(8,128)(2,1)}) custom-call(s32[3]{0:T(128)} %pad_add_fusion.refs_0_, bf16[5,128,1024]{2,1,0:T(8,128)(2,1)} %get-tuple-element.204.refs_9_.refs_5_.refs_1_.refs_7_, ...), custom_call_target="tpu_custom_call", output_to_operand_aliasing={{3}: (24, {})} | custom-call | tf_op jit(solution)/shard_map/pallas_call | solution.py:87
  508.5 15.7 %collective-permute-done.48.refs_17_.refs_13_ = bf16[528,2048]{1,0:T(8,128)(2,1)} collective-permute-done((bf16[528,2048]{1,0:T(8,128)(2,1)}, bf16[528,2048]{1,0:T(8,128)(2,1)}, u32[]{:S(2)}, u32[]{:S(2)}) %collective-permute-start.48) | collective-permute-done | bytes 2162720 | tf_op jit(solution)/shard_map/ppermute | solution.py:121
  543.7 17.7 %collective-permute-done.50.refs_12_.refs_13_ = bf16[512,256]{1,0:T(8,128)(2,1)S(1)} collective-permute-done((bf16[512,256]{1,0:T(8,128)(2,1)}, bf16[512,256]{1,0:T(8,128)(2,1)S(1)}, u32[]{:S(2)}, u32[]{:S(2)}) %collective-permute-start.50) | collective-permute-done | bytes 262176 | tf_op jit(solution)/shard_map/ppermute | solution.py:121
  573.2 16.1 %collective-permute-done.52.refs_12_ = bf16[512,1152]{1,0:T(8,128)(2,1)S(1)} collective-permute-done((bf16[512,1152]{1,0:T(8,128)(2,1)}, bf16[512,1152]{1,0:T(8,128)(2,1)S(1)}, u32[]{:S(2)}, u32[]{:S(2)}) %collective-permute-start.52) | collective-permute-done | bytes 1179680 | tf_op jit(solution)/shard_map/ppermute | solution.py:121
  640.8 13.8 %collective-permute-done.59.refs_2_ = bf16[128,2176]{1,0:T(8,128)(2,1)S(1)} collective-permute-done((bf16[128,2176]{1,0:T(8,128)(2,1)}, bf16[128,2176]{1,0:T(8,128)(2,1)S(1)}, u32[]{:S(2)}, u32[]{:S(2)}) %collective-permute-start.59) | collective-permute-done | bytes 557088 | tf_op jit(solution)/shard_map/ppermute | solution.py:121
  (413 shorter events, 312.8 us)
Async XLA Ops:
  7.2 55.3 %all-gather.10.cloned.1.call-start = ((), (), s32[]{:S(2)}) async-start(), calls=%async_computation.12 | async-start | bytes 4718592 | tf_op jit(solution)/shard_map/all_gather | solution.py:429
  10.4 116.3 %all-gather.12.cloned.1.call-start = ((), (), s32[]{:S(2)}) async-start(), calls=%async_computation.13 | async-start | bytes 4128768 | tf_op jit(solution)/shard_map/all_gather | solution.py:429
  14.0 186.8 %all-gather.14.cloned.1.call-start = ((), (), s32[]{:S(2)}) async-start(), calls=%async_computation.14 | async-start | bytes 2359296 | tf_op jit(solution)/shard_map/all_gather | solution.py:429
  21.7 46.3 %collective-permute-start = (bf16[128,23552]{1,0:T(8,128)(2,1)}, bf16[128,23552]{1,0:T(8,128)(2,1)}, u32[]{:S(2)}, u32[]{:S(2)}) collective-permute-start(bf16[128,23552]{1,0:T(8,128)(2,1)} %constant_dynamic-update-slice_fusion), channel_id=1, source_target_pairs={{0,1},{1,0},{2,3},{3,2},{4,5},{5,4},{6,7},{7,6},{8,9},{9,8},{10,11... | collective-permute-start | bytes 18087944 | tf_op jit(solution)/shard_map/ppermute | solution.py:112
  67.9 173.3 %all-gather.16.cloned.1.call-start = ((), (), s32[]{:S(2)}) async-start(), calls=%async_computation.15 | async-start | bytes 2359296 | tf_op jit(solution)/shard_map/all_gather | solution.py:429
  122.5 43.6 %collective-permute-start.6 = (bf16[768,1024]{1,0:T(8,128)(2,1)}, bf16[768,1024]{1,0:T(8,128)(2,1)}, u32[]{:S(2)}, u32[]{:S(2)}) collective-permute-start(bf16[768,1024]{1,0:T(8,128)(2,1)} %collective-permute-done.5.refs_1_.refs_7_.refs_6_), channel_id=1, source_target_pairs={{0,1},{1,0},{2,3},{3,2},{4,5},{5,4},{6,7},{7,6},{8,9},{9,8},{10,11... | collective-permute-start | bytes 4718600 | tf_op jit(solution)/shard_map/ppermute | solution.py:112
  130.1 36.0 %collective-permute-start.9 = (bf16[768,1024]{1,0:T(8,128)(2,1)}, bf16[768,1024]{1,0:T(8,128)(2,1)S(1)}, u32[]{:S(2)}, u32[]{:S(2)}) collective-permute-start(bf16[768,1024]{1,0:T(8,128)(2,1)} %get-tuple-element.162), channel_id=1, source_target_pairs={{0,8},{1,17},{8,0},{9,25},{16,24},{17,1},{24,16},{25,9},{2,10},{3,... | collective-permute-start | bytes 4718600 | tf_op jit(solution)/shard_map/ppermute | solution.py:121
  154.0 354.5 %reduce-scatter.7.cloned.1.call-start = ((), (), s32[]{:S(2)}) async-start(), calls=%async_computation.6 | async-start | bytes 1310720 | tf_op jit(solution)/shard_map/reduce_scatter | solution.py:383
  204.2 33.1 %collective-permute-start.17 = (bf16[768,1024]{1,0:T(8,128)(2,1)}, bf16[768,1024]{1,0:T(8,128)(2,1)}, u32[]{:S(2)}, u32[]{:S(2)}) collective-permute-start(bf16[768,1024]{1,0:T(8,128)(2,1)} %get-tuple-element.176), channel_id=1, source_target_pairs={{0,8},{1,17},{8,0},{9,25},{16,24},{17,1},{24,16},{25,9},{2,10},{3,... | collective-permute-start | bytes 4718600 | tf_op jit(solution)/shard_map/ppermute | solution.py:121
  204.4 32.9 %collective-permute-start.14 = (bf16[768,768]{1,0:T(8,128)(2,1)S(1)}, bf16[768,768]{1,0:T(8,128)(2,1)S(1)}, u32[]{:S(2)}, u32[]{:S(2)}) collective-permute-start(bf16[768,768]{1,0:T(8,128)(2,1)S(1)} %copy-done.9), channel_id=1, source_target_pairs={{0,1},{1,0},{2,3},{3,2},{4,5},{5,4},{6,7},{7,6},{8,9},{9,8},{10,11... | collective-permute-start | bytes 3538952 | tf_op jit(solution)/shard_map/ppermute | solution.py:112
  244.5 35.4 %collective-permute-start.21 = (bf16[768,1024]{1,0:T(8,128)(2,1)}, bf16[768,1024]{1,0:T(8,128)(2,1)S(1)}, u32[]{:S(2)}, u32[]{:S(2)}) collective-permute-start(bf16[768,1024]{1,0:T(8,128)(2,1)} %get-tuple-element.182), channel_id=1, source_target_pairs={{0,8},{1,17},{8,0},{9,25},{16,24},{17,1},{24,16},{25,9},{2,10},{3,... | collective-permute-start | bytes 4718600 | tf_op jit(solution)/shard_map/ppermute | solution.py:121
  246.6 33.3 %collective-permute-start.18 = (bf16[768,1024]{1,0:T(8,128)(2,1)}, bf16[768,1024]{1,0:T(8,128)(2,1)S(1)}, u32[]{:S(2)}, u32[]{:S(2)}) collective-permute-start(bf16[768,1024]{1,0:T(8,128)(2,1)} %collective-permute-done.17.refs_1_.refs_7_.refs_9_), channel_id=1, source_target_pairs={{0,1},{1,0},{2,3},{3,2},{4,5},{5,4},{6,7},{7,6},{8,9},{9,8},{10,11... | collective-permute-start | bytes 4718600 | tf_op jit(solution)/shard_map/ppermute | solution.py:112
  349.5 35.5 %collective-permute-start.35 = (bf16[592,2048]{1,0:T(8,128)(2,1)}, bf16[592,2048]{1,0:T(8,128)(2,1)}, u32[]{:S(2)}, u32[]{:S(2)}) collective-permute-start(bf16[592,2048]{1,0:T(8,128)(2,1)} %get-tuple-element.221), channel_id=1, source_target_pairs={{0,8},{1,17},{8,0},{9,25},{16,24},{17,1},{24,16},{25,9},{2,10},{3,... | collective-permute-start | bytes 7274504 | tf_op jit(solution)/shard_map/ppermute | solution.py:121
  355.2 58.2 %collective-permute-start.38 = (bf16[576,2048]{1,0:T(8,128)(2,1)}, bf16[576,2048]{1,0:T(8,128)(2,1)}, u32[]{:S(2)}, u32[]{:S(2)}) collective-permute-start(bf16[576,2048]{1,0:T(8,128)(2,1)} %get-tuple-element.230), channel_id=1, source_target_pairs={{0,8},{1,17},{8,0},{9,25},{16,24},{17,1},{24,16},{25,9},{2,10},{3,... | collective-permute-start | bytes 7077896 | tf_op jit(solution)/shard_map/ppermute | solution.py:121
  427.5 116.1 %reduce-scatter.9.cloned.1.call-start = ((), (), s32[]{:S(2)}) async-start(), calls=%async_computation.7 | async-start | bytes 1310720 | tf_op jit(solution)/shard_map/reduce_scatter | solution.py:383
  427.6 33.6 %collective-permute-start.44 = (bf16[560,1536]{1,0:T(8,128)(2,1)}, bf16[560,1536]{1,0:T(8,128)(2,1)}, u32[]{:S(2)}, u32[]{:S(2)}) collective-permute-start(bf16[560,1536]{1,0:T(8,128)(2,1)} %get-tuple-element.250), channel_id=1, source_target_pairs={{0,8},{1,17},{8,0},{9,25},{16,24},{17,1},{24,16},{25,9},{2,10},{3,... | collective-permute-start | bytes 5160968 | tf_op jit(solution)/shard_map/ppermute | solution.py:121
  428.2 32.9 %collective-permute-start.45 = (bf16[512,1024]{1,0:T(8,128)(2,1)}, bf16[512,1024]{1,0:T(8,128)(2,1)}, u32[]{:S(2)}, u32[]{:S(2)}) collective-permute-start(bf16[512,1024]{1,0:T(8,128)(2,1)} %get-tuple-element.251), channel_id=1, source_target_pairs={{0,16},{1,9},{8,24},{9,1},{16,0},{17,25},{24,8},{25,17},{2,18},{3,... | collective-permute-start | bytes 3145736 | tf_op jit(solution)/shard_map/ppermute | solution.py:121
  430.3 63.2 %collective-permute-start.43 = (bf16[544,2048]{1,0:T(8,128)(2,1)}, bf16[544,2048]{1,0:T(8,128)(2,1)}, u32[]{:S(2)}, u32[]{:S(2)}) collective-permute-start(bf16[544,2048]{1,0:T(8,128)(2,1)} %get-tuple-element.249), channel_id=1, source_target_pairs={{0,8},{1,17},{8,0},{9,25},{16,24},{17,1},{24,16},{25,9},{2,10},{3,... | collective-permute-start | bytes 6684680 | tf_op jit(solution)/shard_map/ppermute | solution.py:121
  471.4 101.8 %reduce-scatter.13.cloned.1.call-start = ((), (), s32[]{:S(2)}) async-start(), calls=%async_computation.9 | async-start | bytes 983040 | tf_op jit(solution)/shard_map/reduce_scatter | solution.py:383
  472.0 52.2 %collective-permute-start.48 = (bf16[528,2048]{1,0:T(8,128)(2,1)}, bf16[528,2048]{1,0:T(8,128)(2,1)}, u32[]{:S(2)}, u32[]{:S(2)}) collective-permute-start(bf16[528,2048]{1,0:T(8,128)(2,1)} %get-tuple-element.256), channel_id=1, source_target_pairs={{0,8},{1,17},{8,0},{9,25},{16,24},{17,1},{24,16},{25,9},{2,10},{3,... | collective-permute-start | bytes 6488072 | tf_op jit(solution)/shard_map/ppermute | solution.py:121
  504.6 93.8 %reduce-scatter.17.cloned.1.call-start = ((), (), s32[]{:S(2)}) async-start(), calls=%async_computation.11 | async-start | bytes 1310720 | tf_op jit(solution)/shard_map/reduce_scatter | solution.py:383
  506.0 57.7 %collective-permute-start.47 = (bf16[512,2048]{1,0:T(8,128)(2,1)}, bf16[512,2048]{1,0:T(8,128)(2,1)}, u32[]{:S(2)}, u32[]{:S(2)}) collective-permute-start(bf16[512,2048]{1,0:T(8,128)(2,1)} %get-tuple-element.255), channel_id=1, source_target_pairs={{0,8},{1,17},{8,0},{9,25},{16,24},{17,1},{24,16},{25,9},{2,10},{3,... | collective-permute-start | bytes 6291464 | tf_op jit(solution)/shard_map/ppermute | solution.py:121
  542.1 95.1 %reduce-scatter.11.cloned.1.call-start = ((), (), s32[]{:S(2)}) async-start(), calls=%async_computation.8 | async-start | bytes 1310720 | tf_op jit(solution)/shard_map/reduce_scatter | solution.py:383
  572.8 64.5 %reduce-scatter.15.cloned.1.call-start = ((), (), s32[]{:S(2)}) async-start(), calls=%async_computation.10 | async-start | bytes 1474560 | tf_op jit(solution)/shard_map/reduce_scatter | solution.py:383
  (128 other events, 1480.3 us)
Sparse Core Ops, SparseCore 0:
  10.5 51.8 all-gather.9
  64.6 41.3 all-gather.11
  108.2 27.9 all-gather.13
  154.1 26.0 all-gather.15
  427.6 23.9 reduce-scatter.6
  471.6 23.9 reduce-scatter.8
  504.7 20.1 reduce-scatter.12
  542.2 23.9 reduce-scatter.16
  572.9 24.4 reduce-scatter.10
  599.5 27.7 reduce-scatter.14

commit v4 on v3

--- a/solution.py
+++ b/solution.py
@@ -136,11 +136,11 @@
         copy.wait()
 
 
-def pick(order, place, layers, gathered, base, width):
+def pick(order, place, layers, gathered, base, width, margin):
     blocks = 2 * (layers - 1)
     return order.call(
         functools.partial(pick_kernel, layers, base),
-        [jax.ShapeDtypeStruct((blocks * gathered.shape[1], width), gathered.dtype)],
+        [jax.ShapeDtypeStruct((blocks * gathered.shape[1] + margin, width), gathered.dtype)],
         [SMEM_SPACE, ANY_SPACE],
         [VMEM_SPACE],
         [pltpu.SemaphoreType.DMA((blocks,))],
@@ -156,10 +156,10 @@
     copy.wait()
 
 
-def half(order, place, piece):
+def half(order, place, piece, rows):
     return order.call(
         half_kernel,
-        [jax.ShapeDtypeStruct((piece.shape[0] // 2, piece.shape[1]), piece.dtype)],
+        [jax.ShapeDtypeStruct((rows // 2, piece.shape[1]), piece.dtype)],
         [SMEM_SPACE, ANY_SPACE],
         [VMEM_SPACE],
         [pltpu.SemaphoreType.DMA((1,))],
@@ -233,15 +233,26 @@
 TILE = 512
 
 
-def own_rows(ref, layers, core):
-    tokens, features = ref.shape
+def left_width(features, layers):
+    return features // 2 if features // (2 * layers) % LANES == 0 else features
+
+
+def left_spans(features, layers, core):
     rows = features // (2 * layers)
-    if rows % LANES == 0:
-        blocks = [
-            ref[:, pl.ds(pl.multiple_of((2 * k + core) * rows, rows), rows)] for k in range(layers)
-        ]
-        return jnp.concatenate(blocks, axis=1).T
-    turned = ref[...].T.reshape(layers, 2, rows, tokens)
+    if rows % LANES:
+        return [(pl.ds(0, features), pl.ds(0, features))]
+    return [
+        (pl.ds(pl.multiple_of((2 * k + core) * rows, rows), rows), pl.ds(k * rows, rows))
+        for k in range(layers)
+    ]
+
+
+def own_rows(values, features, layers, core):
+    tokens, width = values.shape
+    if width < features:
+        return values.T
+    rows = features // (2 * layers)
+    turned = values.T.reshape(layers, 2, rows, tokens)
     return jnp.where(core == 0, turned[:, 0], turned[:, 1]).reshape(layers * rows, tokens)
 
 
@@ -264,8 +275,12 @@
     for i, factor in enumerate(lefts):
         at, copies = 0, []
         for k, (array, index, rows) in enumerate(factor.left):
-            target = left_buffer.at[i, at : at + rows]
-            copies.append(start(ins[tables[id(array)]].at[index], target, left_sems.at[i, k]))
+            source = ins[tables[id(array)]].at[index]
+            spans = left_spans(source.shape[1], layers, core)
+            for number, (columns, there) in enumerate(spans):
+                target = left_buffer.at[i, at : at + rows, there]
+                sem = left_sems.at[i, k * len(spans) + number]
+                copies.append(start(source.at[:, columns], target, sem))
             at += rows
         left_copies.append(copies)
     loads = []
@@ -286,7 +301,7 @@
         for copy in left_copies[i]:
             copy.wait()
         turned[i, :, : factor.tokens] = own_rows(
-            left_buffer.at[i, pl.ds(0, factor.tokens)], layers, core
+            left_buffer[i, : factor.tokens], factor.left[0][0].shape[2], layers, core
         )
     stores = []
     for number, (i, _, _, width, adds, (out, column)) in enumerate(jobs):
@@ -314,7 +329,7 @@
         self.dp_size, self.layers = sizes
 
     def step(self, halves=(), quarters=(), rows=(), margin=0):
-        lefts, jobs, widths = [], [], [0, 0, 0]
+        lefts, jobs, widths = [], [], [0] * (2 + len(rows))
 
         def left(factor):
             if factor not in lefts:
@@ -335,9 +350,9 @@
             sums.own_at = add(sums, "near", 0, [])
         for sums in quarters:
             sums.far_at = add(sums, "far", 1, [(sums.halves, sums.near_at)])
-        for sums in rows:
-            add(sums, "own", 2, [(sums.halves, sums.own_at), (sums.quarters, sums.far_at)])
-        slots = [k for k in range(3) if widths[k]]
+        for number, sums in enumerate(rows):
+            add(sums, "own", 2 + number, [(sums.halves, sums.own_at), (sums.quarters, sums.far_at)])
+        slots = [k for k in range(2 + len(rows)) if widths[k]]
         jobs = [job[:5] + ((slots.index(job[5][0]), job[5][1]),) for job in jobs]
         arrays, tables = [], {}
         used = [a for factor in lefts for a in factor.arrays] + [a for job in jobs for a, _ in job[4]]
@@ -363,12 +378,14 @@
             [SMEM_SPACE] + [ANY_SPACE] * len(arrays),
             [ANY_SPACE] * len(slots),
             [
-                pltpu.VMEM((len(lefts), tokens, features), jnp.bfloat16),
+                pltpu.VMEM(
+                    (len(lefts), tokens, left_width(features, self.layers)), jnp.bfloat16
+                ),
                 pltpu.VMEM((len(lefts), height, tokens), jnp.bfloat16),
                 pltpu.VMEM((len(jobs), tokens, widest), jnp.bfloat16),
                 pltpu.VMEM((len(jobs), depth, height, widest), jnp.bfloat16),
                 pltpu.VMEM((len(jobs), height, widest), jnp.bfloat16),
-                pltpu.SemaphoreType.DMA((len(lefts), pieces)),
+                pltpu.SemaphoreType.DMA((len(lefts), pieces * self.layers)),
                 pltpu.SemaphoreType.DMA((len(jobs), rights + depth)),
                 pltpu.SemaphoreType.DMA((len(jobs),)),
             ],
@@ -379,8 +396,11 @@
             sums.halves = moved[0]
         for sums in quarters:
             sums.quarters = moved[1]
-        if 2 in slots:
-            return lax.psum_scatter(outs[slots.index(2)], "z", scatter_dimension=0, tiled=True)
+        return [
+            lax.psum_scatter(outs[slots.index(k)], "z", scatter_dimension=0, tiled=True)
+            for k in slots
+            if k >= 2
+        ]
 
     def share(self, mine):
         summed = join(self.order, mine)
@@ -435,10 +455,11 @@
         self.dp_size, self.layers = sizes
         self.source, self.base, self.other, self.other_base = source, base, other, other_base
         self.width = sum(w.shape[1] for w in group) // QUARTERS
-
-    def near(self):
+        self.rows = 2 * (self.layers - 1) * group[0].shape[0]
+
+    def near(self, margin):
         piece = pick(
-            self.order, self.place, self.layers, self.source.gathered, self.base, self.width
+            self.order, self.place, self.layers, self.source.gathered, self.base, self.width, margin
         )
         self.piece = swap_pairs(piece, 0, self.dp_size)
         self.other_piece = swap_core(self.piece)
@@ -447,7 +468,7 @@
         return [self.other_piece, self.rest, self.other_rest]
 
     def far(self):
-        self.rest = swap_pairs(half(self.order, self.place, self.piece), 1, self.dp_size)
+        self.rest = swap_pairs(half(self.order, self.place, self.piece, self.rows), 1, self.dp_size)
         self.other_rest = swap_core(self.rest)
 
 
@@ -709,7 +730,7 @@
     encoded[...] = (shape * gain + shifts[row : row + 1]).astype(jnp.bfloat16)
     back, gain_grad, shift_grad = norm_back(total, cotangent[...].astype(jnp.float32), gain)
     grad_out[...] = back
-    low_out[...] = (0.5 * back).astype(jnp.bfloat16)
+    low_out[0] = (0.5 * back).astype(jnp.bfloat16)
     gain_out[...] = gain_grad
     shift_out[...] = shift_grad
 
@@ -718,21 +739,20 @@
     return [jax.ShapeDtypeStruct((1, width), jnp.float32)] * count
 
 
-def last_step(order, place, gather, index, row, values, active, cotangent, gains, shifts, through):
+def last_step(order, place, gather, index, row, values, active, cotangent, gains, shifts):
     pieces = Pieces(gather, index)
     return order.call(
         functools.partial(last_kernel, pieces, row),
         [
             jax.ShapeDtypeStruct(values.shape, jnp.bfloat16),
             jax.ShapeDtypeStruct(values.shape, jnp.float32),
-            jax.ShapeDtypeStruct(values.shape, jnp.bfloat16),
+            jax.ShapeDtypeStruct((1, *values.shape), jnp.bfloat16),
             *vector_shapes(values.shape[1]),
         ],
         [SMEM_SPACE] + [VMEM_SPACE] * (4 + CUTS) + [ANY_SPACE] * len(pieces.operands),
         [VMEM_SPACE] * 5,
         pieces.scratch,
         [place, values, cotangent, gains, shifts, *active, *pieces.operands],
-        through,
         lazy=True,
     )
 
@@ -741,23 +761,23 @@
     weight, outs, (buffer, sems) = refs[: -2 - CUTS], refs[-2 - CUTS : -2], refs[-2:]
     steps = pieces.load(place, weight, buffer, sems)
     ready()
-    store_part(outs, 0, gradient[...])
     for r, (index, copies) in enumerate(steps):
         for copy in copies:
             copy.wait()
-        active_grad = dot_rows(gradient[...], pieces.block(buffer, index))
-        store_part(outs, 1 + r, silu_back(expanded[r].astype(jnp.float32), active_grad).astype(jnp.bfloat16))
-
-
-def down_back_step(order, place, gather, index, gradient, expanded):
+        active_grad = dot_rows(gradient[0], pieces.block(buffer, index))
+        store_part(outs, r, silu_back(expanded[r].astype(jnp.float32), active_grad).astype(jnp.bfloat16))
+
+
+def down_back_step(order, place, gather, index, gradient, expanded, through=()):
     pieces = Pieces(gather, index)
     return order.call(
         functools.partial(down_back_kernel, pieces),
-        packed_shapes(1 + QUARTERS, *gradient.shape),
+        packed_shapes(QUARTERS, gradient.shape[1], pieces.part),
         [SMEM_SPACE] + [VMEM_SPACE] * 2 + [ANY_SPACE] * len(pieces.operands),
         [VMEM_SPACE] * CUTS,
         pieces.scratch,
         [place, gradient, expanded, *pieces.operands],
+        through,
         lazy=True,
     )
 
@@ -769,7 +789,7 @@
     back, gain_grad, shift_grad = norm_back(values[...], hidden_grad, gains[row : row + 1])
     total = residual[...] + back
     grad_out[...] = total
-    low_out[...] = (scale * total).astype(jnp.bfloat16)
+    low_out[0] = (scale * total).astype(jnp.bfloat16)
     gain_out[...] = gain_grad
     shift_out[...] = shift_grad
 
@@ -782,7 +802,7 @@
         functools.partial(into_norm_kernel, pieces, first, row, scale),
         [
             jax.ShapeDtypeStruct(values.shape, jnp.float32),
-            jax.ShapeDtypeStruct(values.shape, jnp.bfloat16),
+            jax.ShapeDtypeStruct((1, *values.shape), jnp.bfloat16),
             *vector_shapes(values.shape[1]),
         ],
         [SMEM_SPACE] + [VMEM_SPACE] * (3 + CUTS) + [ANY_SPACE] * len(pieces.operands),
@@ -878,7 +898,7 @@
     total = None
     for index in range(QUARTERS):
         column = slice(index * pieces.part, (index + 1) * pieces.part)
-        term = dot_cols(gradient[:, column], pieces.block(buffer, index))
+        term = dot_cols(gradient[0, :, column], pieces.block(buffer, index))
         total = term if total is None else total + term
     mixed_grad[...] = total.astype(jnp.bfloat16)
     matching = down[...] == across[...]
@@ -898,21 +918,18 @@
         out[:, head(heads + h)] = turn(key_grad, cosine[...], -sine[...]).astype(jnp.bfloat16)
         out[:, head(2 * heads + h)] = value_grad.astype(jnp.bfloat16)
     to_quarters(place, outs, 0, out)
-    to_quarters(place, outs, out.shape[1] // QUARTERS, gradient)
 
 
 def attend_back_step(order, place, gather, index, gradient, turned, totals, cosine, sine, down, across):
     pieces = Pieces(gather, index)
     return order.call(
         functools.partial(attend_back_kernel, pieces),
-        packed_shapes(
-            QUARTERS, turned.shape[0], (turned.shape[1] + gradient.shape[1]) // QUARTERS
-        ),
+        packed_shapes(QUARTERS, turned.shape[0], turned.shape[1] // QUARTERS),
         [SMEM_SPACE] + [VMEM_SPACE] * 7 + [ANY_SPACE] * len(pieces.operands),
         [VMEM_SPACE] * CUTS,
         [
             pltpu.VMEM(turned.shape, jnp.bfloat16),
-            pltpu.VMEM(gradient.shape, jnp.bfloat16),
+            pltpu.VMEM(gradient.shape[1:], jnp.bfloat16),
             *pieces.scratch,
         ],
         [place, gradient, turned, totals, cosine, sine, down, across, *pieces.operands],
@@ -1014,7 +1031,7 @@
     total = None
     for index in range(QUARTERS):
         column = slice(index * pieces.part, (index + 1) * pieces.part)
-        term = dot_cols(gradient[:, column], pieces.block(buffer, index))
+        term = dot_cols(gradient[0, :, column], pieces.block(buffer, index))
         total = term if total is None else total + term
     gain = gains[row : row + 1]
     shape, _ = standard(filtered[...])
@@ -1035,7 +1052,6 @@
     doubled_grad[:, :half] = (gated_grad * gate).astype(jnp.bfloat16)
     doubled_grad[:, half:] = (gated_grad * gated * (1.0 - gate)).astype(jnp.bfloat16)
     to_quarters(place, outs, 0, doubled_grad)
-    to_quarters(place, outs, doubled_grad.shape[1] // QUARTERS, gradient)
 
 
 def conv_back_step(order, place, gather, index, row, gradient, filtered, doubled, gains, shifts, taps, keep):
@@ -1044,9 +1060,7 @@
     return order.call(
         functools.partial(conv_back_kernel, pieces, row),
         [
-            *packed_shapes(
-                QUARTERS, doubled.shape[0], (doubled.shape[1] + gradient.shape[1]) // QUARTERS
-            ),
+            *packed_shapes(QUARTERS, doubled.shape[0], doubled.shape[1] // QUARTERS),
             *vector_shapes(width),
             jax.ShapeDtypeStruct(taps.shape, jnp.float32),
         ],
@@ -1130,39 +1144,36 @@
         language_hot.astype(jnp.bfloat16), table_full, preferred_element_type=jnp.float32
     )
 
-    gathers[0].near()
+    gathers[0].near(80)
+    gathers[1].near(64)
     order.wait(everything_other)
     gathers[0].far()
-    gathers[1].near()
-    order.wait(*gathers[0].arrived())
+    order.wait(gathers[0].rest)
+    gathers[2].near(48)
     gathers[1].far()
-    gathers[2].near()
+    gathers[3].near(32)
     first_expanded, first_packed = up_step(
         order, place, gathers[0], 0, 0, start_sum, gain_rows, shift_rows
     )
-    order.wait(*gathers[1].arrived())
     gathers[2].far()
-    gathers[3].near()
+    gathers[4].near(16)
     after_first = down_step(order, place, gathers[1], 0, start_sum, first_packed)
-    order.wait(*gathers[2].arrived())
     gathers[3].far()
-    gathers[4].near()
+    gathers[5].near(0)
     turned, totals, attend_packed = attend_step(
         order, place, gathers[2], 0, 1, after_first, gain_rows, shift_rows, cosine, sine, down, across
     )
     after_attention = merge_step(order, place, gathers[2], 1, after_first, attend_packed)
-    order.wait(*gathers[3].arrived())
     gathers[4].far()
-    gathers[5].near()
     after_conv, doubled, filtered, conv_packed = conv_step(
         order, place, gathers[3], 2, after_attention, gain_rows, shift_rows, taps, keep
     )
-    order.wait(*gathers[4].arrived())
     gathers[5].far()
     second_expanded, second_packed = up_step(
         order, place, gathers[4], 0, 4, after_conv, gain_rows, shift_rows
     )
-    encoded, grad_second, low_second, final_gain, final_shift, *held = last_step(
+    second_forward = Packed(second_packed)
+    encoded, grad_second, low_second, final_gain, final_shift = last_step(
         order,
         place,
         gathers[5],
@@ -1173,40 +1184,36 @@
         cotangent,
         gain_rows,
         shift_rows,
-        [*second_packed, conv_packed, attend_packed],
-    )
-    *second_packed, conv_packed, attend_packed = held
-    forward, conv_forward, attend_forward = (
-        Packed(second_packed),
-        Packed([conv_packed]),
-        Packed([attend_packed]),
     )
     rounds = Rounds(place, sizes, order)
-    width = frames.shape[1]
-
-    packed = down_back_step(order, place, gathers[5], 0, low_second, second_expanded)
-    backward = Packed(packed)
-    grad_conv, low_conv, second_gain, second_shift, *first_packed = into_norm_step(
+
+    low = Packed([low_second])
+    down_two = Sums(Factor(low, 0, second_forward, 1, 0, seconddown.shape[1]))
+    rounds.step([down_two], margin=80)
+    *packed, first_packed_a, first_packed_b = down_back_step(
+        order, place, gathers[5], 0, low_second, second_expanded, first_packed
+    )
+    backward, first_forward = Packed(packed), Packed([first_packed_a, first_packed_b])
+    grad_conv, low_conv, second_gain, second_shift, *held = into_norm_step(
         order,
         place,
         gathers[4],
         0,
-        1,
+        0,
         4,
         1.0,
         packed,
         after_conv,
         grad_second,
         gain_rows,
-        first_packed,
-    )
-    first_forward = Packed(first_packed)
-    down_two = Sums(Factor(backward, 0, forward, 1, 0, seconddown.shape[1]))
-    up_two = Sums(Factor(forward, 0, backward, 1, 0, secondup.shape[1]))
-    order.wait(*conv_forward.all, *attend_forward.all)
-    rounds.step([down_two], margin=80)
+        [conv_packed, attend_packed],
+    )
+    conv_forward, attend_forward = Packed(held[:1]), Packed(held[1:])
+    up_two = Sums(Factor(second_forward, 0, backward, 0, 0, secondup.shape[1]))
     order.wait(*first_forward.all)
     rounds.step([up_two], margin=64)
+    low = Packed([low_conv])
+    order.wait(*conv_forward.all, *attend_forward.all)
     *packed, inner_gain, inner_shift, taps_grad = conv_back_step(
         order, place, gathers[3], 1, 3, low_conv, filtered, doubled, gain_rows, shift_rows, taps, keep
     )
@@ -1226,14 +1233,14 @@
     )
     conv = Sums(
         Factor(conv_forward, 0, backward, 0, 0, gating.shape[1]),
-        Factor(conv_forward, 1, backward, 0, gating.shape[1] // QUARTERS, pointwise.shape[1]),
-    )
-    order.wait(*backward.all)
+        Factor(conv_forward, 1, low, 0, 0, pointwise.shape[1], relative=False),
+        Factor(attend_forward, 1, Packed([low_attention]), 0, 0, merger.shape[1], relative=False),
+    )
+    rounds.step([conv], [down_two], margin=48)
     packed = attend_back_step(
         order, place, gathers[2], 1, low_attention, turned, totals, cosine, sine, down, across
     )
     backward = Packed(packed)
-    rounds.step([conv], [down_two], margin=48)
     grad_first, low_first, attend_gain, attend_shift = into_norm_step(
         order,
         place,
@@ -1247,19 +1254,18 @@
         grad_attention,
         gain_rows,
     )
-    attend = Sums(
-        Factor(attend_forward, 0, backward, 0, 0, projection.shape[1]),
-        Factor(attend_forward, 1, backward, 0, projection.shape[1] // QUARTERS, merger.shape[1]),
-    )
+    projection_factor = Factor(attend_forward, 0, backward, 0, 0, projection.shape[1])
     order.wait(*backward.all)
+    low = Packed([low_first])
     packed = down_back_step(order, place, gathers[1], 0, low_first, first_expanded)
     backward = Packed(packed)
-    down_two_mine = rounds.step([attend], [up_two], [down_two], margin=32)
+    down_one = Sums(Factor(low, 0, first_forward, 1, 0, firstdown.shape[1]))
+    (down_two_mine,) = rounds.step([down_one], [up_two], [down_two], margin=32)
     frames_grad, low_start, first_gain, first_shift = into_norm_step(
-        order, place, gathers[0], 0, 1, 0, 1.0, packed, start_sum, grad_first, gain_rows
-    )
-    down_one = Sums(Factor(backward, 0, first_forward, 1, 0, firstdown.shape[1]))
-    up_one = Sums(Factor(first_forward, 0, backward, 1, 0, firstup.shape[1]))
+        order, place, gathers[0], 0, 0, 0, 1.0, packed, start_sum, grad_first, gain_rows
+    )
+    up_one = Sums(Factor(first_forward, 0, backward, 0, 0, firstup.shape[1]))
+    (up_two_mine,) = rounds.step([up_one], [conv], [up_two], margin=16)
     vectors = jnp.concatenate(
         [
             first_gain,
@@ -1277,29 +1283,31 @@
             taps_grad,
         ]
     )
-    small_packed = Packed([pack_small(language_hot, low_start, vectors)])
-    small = Sums(Factor(small_packed, 0, small_packed, 1, 0, QUARTERS * LANES, relative=False))
-    up_two_mine = rounds.step([down_one], [conv], [up_two], margin=16)
-    conv_mine = rounds.step([up_one], [attend], [conv])
+    small_packed = Packed([pack_small(language_hot, low_start[0], vectors)])
+    last = Sums(
+        projection_factor,
+        Factor(small_packed, 0, small_packed, 1, 0, QUARTERS * LANES, relative=False),
+    )
     order.wait(down_two_mine)
-    attend_mine = rounds.step([small], [down_one], [attend])
+    (conv_mine,) = rounds.step([last], [down_one], [conv], margin=80)
     order.wait(up_two_mine)
-    down_one_mine = rounds.step([], [up_one, small], [down_one])
+    (down_one_mine,) = rounds.step([], [up_one], [down_one])
     order.wait(conv_mine)
-    last_mine = rounds.step([], [], [up_one, small])
-    ffn_pieces = rounds.share([down_two_mine, up_two_mine])
-    order.wait(attend_mine)
-    middle_pieces = rounds.share([conv_mine, attend_mine])
+    (up_one_mine,) = rounds.step([], [last], [up_one])
+    pieces = rounds.share([down_two_mine, up_two_mine])
+    order.wait(down_one_mine)
+    (last_mine,) = rounds.step([], [], [last])
+    middle_pieces = rounds.share([conv_mine, down_one_mine])
     seconddown_grad, secondup_grad = spread(
-        order, place, [seconddown.shape[1], secondup.shape[1]], ffn_pieces
-    )
-    middle = [gating, pointwise, projection, merger]
-    gating_grad, pointwise_grad, projection_grad, merger_grad = spread(
+        order, place, [seconddown.shape[1], secondup.shape[1]], pieces
+    )
+    middle = [gating, pointwise, merger, firstdown]
+    gating_grad, pointwise_grad, merger_grad, firstdown_grad = spread(
         order, place, [w.shape[1] for w in middle], middle_pieces
     )
-    last_pieces = rounds.share([down_one_mine, last_mine])
-    firstdown_grad, firstup_grad, small = spread(
-        order, place, [firstdown.shape[1], firstup.shape[1], QUARTERS * LANES], last_pieces
+    pieces = rounds.share([up_one_mine, last_mine])
+    firstup_grad, projection_grad, small = spread(
+        order, place, [firstup.shape[1], projection.shape[1], QUARTERS * LANES], pieces
     )
     counts = [embedding.shape[0], gains.shape[0], shifts.shape[0], kernel.shape[0]]
     table_sum, gain_sum, shift_sum, taps_sum = unpack_small(small, counts)

time: 684 us -> 616 us (0.901)
  waiting for transfers between devices: 294 us -> 224 us
  starting transfers between devices: 34.3 us -> 42 us
    ppermute x34 -> x33, waiting for transfers between devices: 273 us -> 190 us  [swap_pairs(): return lax.ppermute(value, ('dp', 'core'), pairs)]
    all_gather x4, waiting for transfers between devices: 19 us -> 29.3 us  [__init__(): self.gathered = lax.all_gather(mine, ('z', 'core'), axis=0, tiled=False)]
    ppermute x34 -> x33, starting transfers between devices: 26.7 us -> 33.1 us  [swap_pairs(): return lax.ppermute(value, ('dp', 'core'), pairs)]
    unnamed x173 -> x169, local copies, waits for them, and re-layouts: 30.1 us -> 30.3 us
  transfers between devices with their start and end apart: 72 -> 75, of which waited for: 27 -> 22; matrix products, arithmetic and copies ran while one was open for 4% -> 4% of each run, Pallas kernels for 34% -> 39%
where the time goes in v4:
time: 616 us; the launch traced here: 612 us
  Pallas kernels  261 us (42%)
  waiting for transfers between devices  224 us (36%)
  local copies, waits for them, and re-layouts  44.4 us (7%)
  starting transfers between devices  42 us (7%)
  blocking collectives  18 us (3%)
  between operations  15.8 us (3%)
    pallas_call x42, Pallas kernels, call(): pl.pallas_call(body, out_shape=[*out_shape, *[jax.ShapeDtypeStruct(x.shap...  261 us
    ppermute x33, waiting for transfers between devices, swap_pairs(): return lax.ppermute(value, ('dp', 'core'), pairs)  190 us
    ppermute x33, starting transfers between devices, swap_pairs(): return lax.ppermute(value, ('dp', 'core'), pairs)  33.1 us
    unnamed x169, local copies, waits for them, and re-layouts  30.3 us
    all_gather x4, waiting for transfers between devices, __init__(): self.gathered = lax.all_gather(mine, ('z', 'core'), axis=0, tiled=False)  29.3 us
    all_gather x1, blocking collectives, gather_small(): full = lax.all_gather(packed, ('z', 'core'), axis=0, tiled=False)  18 us
  transfers between devices with their start and end apart: 75, of which 22 were waited for; matrix products, arithmetic and copies ran while one was open for 4% of the time, Pallas kernels for 39%

profile of v4, /device:TPU:0, one launch (start us, length us, event | category | flops | bytes accessed | tf_op | source)
XLA Modules:
  0.0 612.3 jit_solution(15837270284872777323)
XLA Ops:
  23.1 18.0 %all-gather = bf16[1024,128]{1,0:T(8,128)(2,1)S(1)} all-gather(bf16[128,128]{1,0:T(8,128)(2,1)S(1)} %fusion.9), channel_id=2, replica_groups=mesh['dp'=4,'z'=4,'core'=2] {'z','core'}, dimensions={0}, use_global_device_ids=true | all-gather | bytes 294912 | tf_op jit(solution)/shard_map/all_gather | solution.py:479
  43.5 18.9 %all-gather.10.cloned.1.call-done = bf16[1024,2048]{1,0:T(8,128)(2,1)} async-done(((bf16[128,2048]{1,0:T(8,128)(2,1)}), bf16[1024,2048]{1,0:T(8,128)(2,1)}) %all-gather.10.cloned.1.call-update) | async-done | bytes 4194320 | tf_op jit(solution)/shard_map/all_gather | solution.py:449
  71.2 17.0 %collective-permute-done.1.refs_1_.refs_7_.refs_9_ = bf16[848,1024]{1,0:T(8,128)(2,1)S(1)} collective-permute-done((bf16[848,1024]{1,0:T(8,128)(2,1)}, bf16[848,1024]{1,0:T(8,128)(2,1)S(1)}, u32[]{:S(2)}, u32[]{:S(2)}) %collective-permute-start.1) | collective-permute-done | bytes 1736736 | tf_op jit(solution)/shard_map/ppermute | solution.py:121
  95.8 10.3 %all-gather.12.cloned.1.call-done = bf16[1024,1792]{1,0:T(8,128)(2,1)} async-done(((bf16[128,1792]{1,0:T(8,128)(2,1)}), bf16[1024,1792]{1,0:T(8,128)(2,1)}) %all-gather.12.cloned.1.call-update) | async-done | bytes 3670032 | tf_op jit(solution)/shard_map/all_gather | solution.py:449
  128.0 9.9 %shard_map.272 = (bf16[4,256,1024]{2,1,0:T(8,128)(2,1)}, bf16[5,128,1024]{2,1,0:T(8,128)(2,1)}, bf16[5,128,1024]{2,1,0:T(8,128)(2,1)}, bf16[256,1024]{1,0:T(8,128)(2,1)}) custom-call(s32[3]{0:T(128)} %pad_add_fusion.refs_0_, f32[256,1024]{1,0:T(8,128)} %convolution_add_fusion.refs_1_, ...), custom_call_target="tpu_custom_call", output_to_operand_aliasing={{3}: (11, {})} | custom-call | tf_op jit(solution)/shard_map/pallas_call | solution.py:87
  158.5 13.6 %collective-permute-done.11.refs_13_.refs_8_.refs_11_ = bf16[384,1024]{1,0:T(8,128)(2,1)} collective-permute-done((bf16[384,1024]{1,0:T(8,128)(2,1)}, bf16[384,1024]{1,0:T(8,128)(2,1)}, u32[]{:S(2)}, u32[]{:S(2)}) %collective-permute-start.11) | collective-permute-done | bytes 786464 | tf_op jit(solution)/shard_map/ppermute | solution.py:121
  193.7 9.7 %shard_map.278 = (bf16[256,3072]{1,0:T(8,128)(2,1)}, f32[256,8]{1,0:T(8,128)}, bf16[2,256,1024]{2,1,0:T(8,128)(2,1)}, bf16[256,1024]{1,0:T(8,128)(2,1)}) custom-call(s32[3]{0:T(128)} %pad_add_fusion.refs_0_, f32[256,1024]{1,0:T(8,128)} %get-tuple-element.164.refs_1_, ...), custom_call_target="tpu_custom_call", output_to_operand_aliasing={{3}: (15, {})} | custom-call | tf_op jit(solution)/shard_map/pallas_call | solution.py:87
  216.3 10.1 %shard_map.281 = (f32[256,1024]{1,0:T(8,128)}, bf16[256,2048]{1,0:T(8,128)(2,1)}, f32[256,1024]{1,0:T(8,128)}, bf16[2,256,1024]{2,1,0:T(8,128)(2,1)}, bf16[256,1024]{1,0:T(8,128)(2,1)}) custom-call(s32[3]{0:T(128)} %pad_add_fusion.refs_0_, f32[256,1024]{1,0:T(8,128)} %get-tuple-element.172.refs_1_, ...), custom_call_target="tpu_custom_call", output_to_operand_aliasing={{4}: (20, {})} | custom-call | tf_op jit(solution)/shard_map/pallas_call | solution.py:87
  230.2 11.2 %collective-permute-done.23.refs_12_.refs_8_ = bf16[384,1024]{1,0:T(8,128)(2,1)} collective-permute-done((bf16[384,1024]{1,0:T(8,128)(2,1)}, bf16[384,1024]{1,0:T(8,128)(2,1)}, u32[]{:S(2)}, u32[]{:S(2)}) %collective-permute-start.23) | collective-permute-done | bytes 786464 | tf_op jit(solution)/shard_map/ppermute | solution.py:121
  242.3 9.9 %shard_map.283 = (bf16[4,256,1024]{2,1,0:T(8,128)(2,1)}, bf16[5,128,1024]{2,1,0:T(8,128)(2,1)}, bf16[5,128,1024]{2,1,0:T(8,128)(2,1)}, bf16[256,1024]{1,0:T(8,128)(2,1)}) custom-call(s32[3]{0:T(128)} %pad_add_fusion.refs_0_, f32[256,1024]{1,0:T(8,128)} %get-tuple-element.177.refs_1_, ...), custom_call_target="tpu_custom_call", output_to_operand_aliasing={{3}: (11, {})} | custom-call | tf_op jit(solution)/shard_map/pallas_call | solution.py:87
  252.9 10.0 %shard_map.284 = (bf16[256,1024]{1,0:T(8,128)(2,1)}, f32[256,1024]{1,0:T(8,128)}, bf16[1,256,1024]{2,1,0:T(8,128)(2,1)}, f32[1,1024]{1,0:T(1,128)}, f32[1,1024]{1,0:T(1,128)}, /*index=5*/bf16[256,1024]{1,0:T(8,128)(2,1)}) custom-call(s32[3]{0:T(128)} %pad_add_fusion.refs_0_, ...), custom_call_target="tpu_custom_call", output_to_operand_aliasing={{5}: (14, {})} | custom-call | tf_op jit(solution)/shard_map/pallas_call | solution.py:87
  272.5 9.5 %shard_map.286 = (bf16[4,128,1024]{2,1,0:T(8,128)(2,1)}, bf16[4,128,1024]{2,1,0:T(8,128)(2,1)}, bf16[5,128,1024]{2,1,0:T(8,128)(2,1)}, bf16[5,128,1024]{2,1,0:T(8,128)(2,1)}, bf16[256,1024]{1,0:T(8,128)(2,1)}) custom-call(s32[3]{0:T(128)} %pad_add_fusion.refs_0_, ...), custom_call_target="tpu_custom_call", output_to_operand_aliasing={{2}: (10, {}), {3}: (11, {}), {4}: (12, {})} | custom-call | tf_op jit(solution)/shard_map/pallas_call | solution.py:87
  283.3 9.7 %shard_map.287 = (f32[256,1024]{1,0:T(8,128)}, bf16[1,256,1024]{2,1,0:T(8,128)(2,1)}, f32[1,1024]{1,0:T(1,128)}, f32[1,1024]{1,0:T(1,128)}, bf16[2,256,1024]{2,1...) custom-call(s32[3]{0:T(128)} %pad_add_fusion.refs_0_, ...), custom_call_target="tpu_custom_call", output_to_operand_aliasing={{4}: (13, {}), {5}: (14, {}), {6}: (15, {})} | custom-call | tf_op jit(solution)/shard_map/pallas_call | solution.py:87
  364.8 9.8 %shard_map.295 = (bf16[544,2048]{1,0:T(8,128)(2,1)}, bf16[512,1024]{1,0:T(8,128)(2,1)}, bf16[512,1024]{1,0:T(8,128)(2,1)}, bf16[256,1024]{1,0:T(8,128)(2,1)}) custom-call(s32[3]{0:T(128)} %pad_add_fusion.refs_0_, bf16[1,256,1024]{2,1,0:T(8,128)(2,1)} %get-tuple-element.220.refs_1_.refs_9_, ...), custom_call_target="tpu_custom_call", output_to_operand_aliasing={{3}: (20, {})} | custom-call | tf_op jit(solution)/shard_map/pallas_call | solution.py:87
  378.7 9.7 %shard_map.296 = (f32[256,1024]{1,0:T(8,128)}, bf16[1,256,1024]{2,1,0:T(8,128)(2,1)}, f32[1,1024]{1,0:T(1,128)}, f32[1,1024]{1,0:T(1,128)}, bf16[256,1024]{1,0:T(8,128)(2,1)}) custom-call(s32[3]{0:T(128)} %pad_add_fusion.refs_0_, f32[256,1024]{1,0:T(8,128)} %convolution_add_fusion.refs_1_, ...), custom_call_target="tpu_custom_call", output_to_operand_aliasing={{4}: (13, {})} | custom-call | tf_op jit(solution)/shard_map/pallas_call | solution.py:87
  388.4 14.2 %collective-permute-done.49.refs_31_ = bf16[512,1024]{1,0:T(8,128)(2,1)} collective-permute-done((bf16[512,1024]{1,0:T(8,128)(2,1)}, bf16[512,1024]{1,0:T(8,128)(2,1)}, u32[]{:S(2)}, u32[]{:S(2)}) %collective-permute-start.49) | collective-permute-done | bytes 1048608 | tf_op jit(solution)/shard_map/ppermute | solution.py:121
  402.7 10.9 %shard_map.297 = (bf16[528,2048]{1,0:T(8,128)(2,1)}, bf16[512,1024]{1,0:T(8,128)(2,1)}, bf16[512,1024]{1,0:T(8,128)(2,1)}, bf16[256,1024]{1,0:T(8,128)(2,1)}) custom-call(s32[3]{0:T(128)} %pad_add_fusion.refs_0_, bf16[5,128,1024]{2,1,0:T(8,128)(2,1)} %get-tuple-element.202.refs_9_.refs_3_.refs_1_.refs_11_, ...), custom_call_target="tpu_custom_call", output_to_operand_aliasing={{3}: (32, {})} | custom-call | tf_op jit(solution)/shard_map/pallas_call | solution.py:87
  417.7 23.4 %collective-permute-done.50.refs_27_ = bf16[512,1024]{1,0:T(8,128)(2,1)S(1)} collective-permute-done((bf16[512,1024]{1,0:T(8,128)(2,1)}, bf16[512,1024]{1,0:T(8,128)(2,1)S(1)}, u32[]{:S(2)}, u32[]{:S(2)}) %collective-permute-start.50) | collective-permute-done | bytes 1048608 | tf_op jit(solution)/shard_map/ppermute | solution.py:121
  442.0 11.6 %shard_map.298 = (bf16[592,1792]{1,0:T(8,128)(2,1)}, bf16[512,1024]{1,0:T(8,128)(2,1)}, bf16[512,1024]{1,0:T(8,128)(2,1)}, bf16[256,1024]{1,0:T(8,128)(2,1)}) custom-call(s32[3]{0:T(128)} %pad_add_fusion.refs_0_, bf16[2,256,1024]{2,1,0:T(8,128)(2,1)} %get-tuple-element.201.refs_17_.refs_9_.refs_1_, ...), custom_call_target="tpu_custom_call", output_to_operand_aliasing={{3}: (29, {})} | custom-call | tf_op jit(solution)/shard_map/pallas_call | solution.py:87
  456.2 24.1 %collective-permute-done.53.refs_13_ = bf16[512,1024]{1,0:T(8,128)(2,1)S(1)} collective-permute-done((bf16[512,1024]{1,0:T(8,128)(2,1)}, bf16[512,1024]{1,0:T(8,128)(2,1)S(1)}, u32[]{:S(2)}, u32[]{:S(2)}) %collective-permute-start.53) | collective-permute-done | bytes 1048608 | tf_op jit(solution)/shard_map/ppermute | solution.py:121
  488.2 15.0 %collective-permute-done.54.refs_19_ = bf16[512,1024]{1,0:T(8,128)(2,1)S(1)} collective-permute-done((bf16[512,1024]{1,0:T(8,128)(2,1)}, bf16[512,1024]{1,0:T(8,128)(2,1)S(1)}, u32[]{:S(2)}, u32[]{:S(2)}) %collective-permute-start.54) | collective-permute-done | bytes 1048608 | tf_op jit(solution)/shard_map/ppermute | solution.py:121
  514.3 11.7 %collective-permute-done.55.refs_10_ = bf16[512,896]{1,0:T(8,128)(2,1)S(1)} collective-permute-done((bf16[512,896]{1,0:T(8,128)(2,1)}, bf16[512,896]{1,0:T(8,128)(2,1)S(1)}, u32[]{:S(2)}, u32[]{:S(2)}) %collective-permute-start.55) | collective-permute-done | bytes 917536 | tf_op jit(solution)/shard_map/ppermute | solution.py:121
  536.9 10.6 %collective-permute-done.59.refs_2_ = bf16[128,2048]{1,0:T(8,128)(2,1)S(1)} collective-permute-done((bf16[128,2048]{1,0:T(8,128)(2,1)S(1)}, bf16[128,2048]{1,0:T(8,128)(2,1)S(1)}, u32[]{:S(2)}, u32[]{:S(2)}) %collective-permute-start.59) | collective-permute-done | bytes 524320 | tf_op jit(solution)/shard_map/ppermute | solution.py:121
  577.2 11.2 %collective-permute-done.62.refs_2_ = bf16[128,1920]{1,0:T(8,128)(2,1)S(1)} collective-permute-done((bf16[128,1920]{1,0:T(8,128)(2,1)}, bf16[128,1920]{1,0:T(8,128)(2,1)S(1)}, u32[]{:S(2)}, u32[]{:S(2)}) %collective-permute-start.62) | collective-permute-done | bytes 491552 | tf_op jit(solution)/shard_map/ppermute | solution.py:121
  (415 shorter events, 286.4 us)
Async XLA Ops:
  7.2 55.3 %all-gather.10.cloned.1.call-start = ((), (), s32[]{:S(2)}) async-start(), calls=%async_computation.12 | async-start | bytes 4718592 | tf_op jit(solution)/shard_map/all_gather | solution.py:449
  10.5 95.6 %all-gather.12.cloned.1.call-start = ((), (), s32[]{:S(2)}) async-start(), calls=%async_computation.13 | async-start | bytes 4128768 | tf_op jit(solution)/shard_map/all_gather | solution.py:449
  14.1 140.0 %all-gather.14.cloned.1.call-start = ((), (), s32[]{:S(2)}) async-start(), calls=%async_computation.14 | async-start | bytes 2359296 | tf_op jit(solution)/shard_map/all_gather | solution.py:449
  21.8 49.4 %collective-permute-start = (bf16[128,23552]{1,0:T(8,128)(2,1)}, bf16[128,23552]{1,0:T(8,128)(2,1)}, u32[]{:S(2)}, u32[]{:S(2)}) collective-permute-start(bf16[128,23552]{1,0:T(8,128)(2,1)} %constant_dynamic-update-slice_fusion), channel_id=1, source_target_pairs={{0,1},{1,0},{2,3},{3,2},{4,5},{5,4},{6,7},{7,6},{8,9},{9,8},{10,11... | collective-permute-start | bytes 18087944 | tf_op jit(solution)/shard_map/ppermute | solution.py:112
  23.0 161.6 %all-gather.16.cloned.1.call-start = ((), (), s32[]{:S(2)}) async-start(), calls=%async_computation.15 | async-start | bytes 2359296 | tf_op jit(solution)/shard_map/all_gather | solution.py:449
  70.6 48.0 %collective-permute-start.5 = (bf16[832,1024]{1,0:T(8,128)(2,1)}, bf16[832,1024]{1,0:T(8,128)(2,1)}, u32[]{:S(2)}, u32[]{:S(2)}) collective-permute-start(bf16[832,1024]{1,0:T(8,128)(2,1)} %get-tuple-element.152), channel_id=1, source_target_pairs={{0,8},{1,17},{8,0},{9,25},{16,24},{17,1},{24,16},{25,9},{2,10},{3,... | collective-permute-start | bytes 5111816 | tf_op jit(solution)/shard_map/ppermute | solution.py:121
  95.3 322.3 %reduce-scatter.7.cloned.1.call-start = ((), (), s32[]{:S(2)}) async-start(), calls=%async_computation.6 | async-start | bytes 1310720 | tf_op jit(solution)/shard_map/reduce_scatter | solution.py:400
  118.6 39.4 %collective-permute-start.6 = (bf16[832,1024]{1,0:T(8,128)(2,1)}, bf16[832,1024]{1,0:T(8,128)(2,1)}, u32[]{:S(2)}, u32[]{:S(2)}) collective-permute-start(bf16[832,1024]{1,0:T(8,128)(2,1)} %collective-permute-done.5.refs_1_.refs_7_.refs_6_), channel_id=1, source_target_pairs={{0,1},{1,0},{2,3},{3,2},{4,5},{5,4},{6,7},{7,6},{8,9},{9,8},{10,11... | collective-permute-start | bytes 5111816 | tf_op jit(solution)/shard_map/ppermute | solution.py:112
  121.8 36.2 %collective-permute-start.7 = (bf16[384,1024]{1,0:T(8,128)(2,1)}, bf16[384,1024]{1,0:T(8,128)(2,1)}, u32[]{:S(2)}, u32[]{:S(2)}) collective-permute-start(bf16[384,1024]{1,0:T(8,128)(2,1)} %get-tuple-element.159), channel_id=1, source_target_pairs={{0,16},{1,9},{8,24},{9,1},{16,0},{17,25},{24,8},{25,17},{2,18},{3,... | collective-permute-start | bytes 2359304 | tf_op jit(solution)/shard_map/ppermute | solution.py:121
  157.3 34.2 %collective-permute-start.17 = (bf16[784,1024]{1,0:T(8,128)(2,1)}, bf16[784,1024]{1,0:T(8,128)(2,1)}, u32[]{:S(2)}, u32[]{:S(2)}) collective-permute-start(bf16[784,1024]{1,0:T(8,128)(2,1)} %get-tuple-element.174), channel_id=1, source_target_pairs={{0,8},{1,17},{8,0},{9,25},{16,24},{17,1},{24,16},{25,9},{2,10},{3,... | collective-permute-start | bytes 4816904 | tf_op jit(solution)/shard_map/ppermute | solution.py:121
  158.0 35.7 %collective-permute-start.10 = (bf16[816,1024]{1,0:T(8,128)(2,1)S(1)}, bf16[816,1024]{1,0:T(8,128)(2,1)}, u32[]{:S(2)}, u32[]{:S(2)}) collective-permute-start(bf16[816,1024]{1,0:T(8,128)(2,1)S(1)} %copy-done.4), channel_id=1, source_target_pairs={{0,1},{1,0},{2,3},{3,2},{4,5},{5,4},{6,7},{7,6},{8,9},{9,8},{10,11... | collective-permute-start | bytes 5013512 | tf_op jit(solution)/shard_map/ppermute | solution.py:112
  188.0 38.4 %collective-permute-start.21 = (bf16[768,1024]{1,0:T(8,128)(2,1)}, bf16[768,1024]{1,0:T(8,128)(2,1)}, u32[]{:S(2)}, u32[]{:S(2)}) collective-permute-start(bf16[768,1024]{1,0:T(8,128)(2,1)} %get-tuple-element.179), channel_id=1, source_target_pairs={{0,8},{1,17},{8,0},{9,25},{16,24},{17,1},{24,16},{25,9},{2,10},{3,... | collective-permute-start | bytes 4718600 | tf_op jit(solution)/shard_map/ppermute | solution.py:121
  191.6 49.8 %collective-permute-start.18 = (bf16[784,1024]{1,0:T(8,128)(2,1)}, bf16[784,1024]{1,0:T(8,128)(2,1)}, u32[]{:S(2)}, u32[]{:S(2)}) collective-permute-start(bf16[784,1024]{1,0:T(8,128)(2,1)} %collective-permute-done.17.refs_1_.refs_7_.refs_9_), channel_id=1, source_target_pairs={{0,1},{1,0},{2,3},{3,2},{4,5},{5,4},{6,7},{7,6},{8,9},{9,8},{10,11... | collective-permute-start | bytes 4816904 | tf_op jit(solution)/shard_map/ppermute | solution.py:112
  283.1 40.6 %collective-permute-start.38 = (bf16[592,2048]{1,0:T(8,128)(2,1)}, bf16[592,2048]{1,0:T(8,128)(2,1)}, u32[]{:S(2)}, u32[]{:S(2)}) collective-permute-start(bf16[592,2048]{1,0:T(8,128)(2,1)} %get-tuple-element.213), channel_id=1, source_target_pairs={{0,8},{1,17},{8,0},{9,25},{16,24},{17,1},{24,16},{25,9},{2,10},{3,... | collective-permute-start | bytes 7274504 | tf_op jit(solution)/shard_map/ppermute | solution.py:121
  301.5 62.4 %collective-permute-start.42 = (bf16[576,2048]{1,0:T(8,128)(2,1)}, bf16[576,2048]{1,0:T(8,128)(2,1)}, u32[]{:S(2)}, u32[]{:S(2)}) collective-permute-start(bf16[576,2048]{1,0:T(8,128)(2,1)} %get-tuple-element.225), channel_id=1, source_target_pairs={{0,8},{1,17},{8,0},{9,25},{16,24},{17,1},{24,16},{25,9},{2,10},{3,... | collective-permute-start | bytes 7077896 | tf_op jit(solution)/shard_map/ppermute | solution.py:121
  351.6 51.0 %collective-permute-start.48 = (bf16[560,2048]{1,0:T(8,128)(2,1)}, bf16[560,2048]{1,0:T(8,128)(2,1)}, u32[]{:S(2)}, u32[]{:S(2)}) collective-permute-start(bf16[560,2048]{1,0:T(8,128)(2,1)} %get-tuple-element.245), channel_id=1, source_target_pairs={{0,8},{1,17},{8,0},{9,25},{16,24},{17,1},{24,16},{25,9},{2,10},{3,... | collective-permute-start | bytes 6881288 | tf_op jit(solution)/shard_map/ppermute | solution.py:121
  374.7 81.5 %reduce-scatter.9.cloned.1.call-start = ((), (), s32[]{:S(2)}) async-start(), calls=%async_computation.7 | async-start | bytes 1310720 | tf_op jit(solution)/shard_map/reduce_scatter | solution.py:400
  376.9 64.2 %collective-permute-start.47 = (bf16[544,2048]{1,0:T(8,128)(2,1)}, bf16[544,2048]{1,0:T(8,128)(2,1)}, u32[]{:S(2)}, u32[]{:S(2)}) collective-permute-start(bf16[544,2048]{1,0:T(8,128)(2,1)} %get-tuple-element.244), channel_id=1, source_target_pairs={{0,8},{1,17},{8,0},{9,25},{16,24},{17,1},{24,16},{25,9},{2,10},{3,... | collective-permute-start | bytes 6684680 | tf_op jit(solution)/shard_map/ppermute | solution.py:121
  413.6 74.6 %reduce-scatter.11.cloned.1.call-start = ((), (), s32[]{:S(2)}) async-start(), calls=%async_computation.8 | async-start | bytes 1310720 | tf_op jit(solution)/shard_map/reduce_scatter | solution.py:400
  415.5 40.6 %collective-permute-start.52 = (bf16[528,2048]{1,0:T(8,128)(2,1)}, bf16[528,2048]{1,0:T(8,128)(2,1)}, u32[]{:S(2)}, u32[]{:S(2)}) collective-permute-start(bf16[528,2048]{1,0:T(8,128)(2,1)} %get-tuple-element.252), channel_id=1, source_target_pairs={{0,8},{1,17},{8,0},{9,25},{16,24},{17,1},{24,16},{25,9},{2,10},{3,... | collective-permute-start | bytes 6488072 | tf_op jit(solution)/shard_map/ppermute | solution.py:121
  453.6 72.4 %reduce-scatter.15.cloned.1.call-start = ((), (), s32[]{:S(2)}) async-start(), calls=%async_computation.10 | async-start | bytes 1310720 | tf_op jit(solution)/shard_map/reduce_scatter | solution.py:400
  454.0 49.2 %collective-permute-start.51 = (bf16[592,1792]{1,0:T(8,128)(2,1)}, bf16[592,1792]{1,0:T(8,128)(2,1)S(1)}, u32[]{:S(2)}, u32[]{:S(2)}) collective-permute-start(bf16[592,1792]{1,0:T(8,128)(2,1)} %get-tuple-element.251), channel_id=1, source_target_pairs={{0,8},{1,17},{8,0},{9,25},{16,24},{17,1},{24,16},{25,9},{2,10},{3,... | collective-permute-start | bytes 6365192 | tf_op jit(solution)/shard_map/ppermute | solution.py:121
  488.1 85.0 %reduce-scatter.13.cloned.1.call-start = ((), (), s32[]{:S(2)}) async-start(), calls=%async_computation.9 | async-start | bytes 1310720 | tf_op jit(solution)/shard_map/reduce_scatter | solution.py:400
  512.4 60.7 %reduce-scatter.17.cloned.1.call-start = ((), (), s32[]{:S(2)}) async-start(), calls=%async_computation.11 | async-start | bytes 1146880 | tf_op jit(solution)/shard_map/reduce_scatter | solution.py:400
  (130 other events, 1498.8 us)
Sparse Core Ops, SparseCore 0:
  10.6 51.8 all-gather.9
  64.7 41.3 all-gather.11
  108.2 27.9 all-gather.13
  138.3 28.5 all-gather.15
  374.8 25.1 reduce-scatter.6
  413.7 25.1 reduce-scatter.8
  453.8 25.1 reduce-scatter.10
  488.2 25.1 reduce-scatter.14
  515.7 25.7 reduce-scatter.12
  543.8 23.7 reduce-scatter.16

commit v5 on v4

--- a/solution.py
+++ b/solution.py
@@ -1144,19 +1144,19 @@
         language_hot.astype(jnp.bfloat16), table_full, preferred_element_type=jnp.float32
     )
 
-    gathers[0].near(80)
-    gathers[1].near(64)
+    gathers[0].near(40)
+    gathers[1].near(32)
     order.wait(everything_other)
     gathers[0].far()
     order.wait(gathers[0].rest)
-    gathers[2].near(48)
+    gathers[2].near(24)
     gathers[1].far()
-    gathers[3].near(32)
+    gathers[3].near(16)
     first_expanded, first_packed = up_step(
         order, place, gathers[0], 0, 0, start_sum, gain_rows, shift_rows
     )
     gathers[2].far()
-    gathers[4].near(16)
+    gathers[4].near(8)
     after_first = down_step(order, place, gathers[1], 0, start_sum, first_packed)
     gathers[3].far()
     gathers[5].near(0)
@@ -1301,13 +1301,15 @@
     seconddown_grad, secondup_grad = spread(
         order, place, [seconddown.shape[1], secondup.shape[1]], pieces
     )
+    up_pieces = rounds.share([up_one_mine])
     middle = [gating, pointwise, merger, firstdown]
     gating_grad, pointwise_grad, merger_grad, firstdown_grad = spread(
         order, place, [w.shape[1] for w in middle], middle_pieces
     )
-    pieces = rounds.share([up_one_mine, last_mine])
-    firstup_grad, projection_grad, small = spread(
-        order, place, [firstup.shape[1], projection.shape[1], QUARTERS * LANES], pieces
+    pieces = rounds.share([last_mine])
+    (firstup_grad,) = spread(order, place, [firstup.shape[1]], up_pieces)
+    projection_grad, small = spread(
+        order, place, [projection.shape[1], QUARTERS * LANES], pieces
     )
     counts = [embedding.shape[0], gains.shape[0], shifts.shape[0], kernel.shape[0]]
     table_sum, gain_sum, shift_sum, taps_sum = unpack_small(small, counts)

time: 616 us -> 607 us (0.985)
  waiting for transfers between devices: 224 us -> 197 us
  starting transfers between devices: 42 us -> 55.1 us
    ppermute x33 -> x36, waiting for transfers between devices: 190 us -> 160 us  [swap_pairs(): return lax.ppermute(value, ('dp', 'core'), pairs)]
    ppermute x33 -> x36, starting transfers between devices: 33.1 us -> 46.6 us  [swap_pairs(): return lax.ppermute(value, ('dp', 'core'), pairs)]
    pallas_call x42 -> x44, Pallas kernels: 261 us -> 265 us  [call(): pl.pallas_call(body, out_shape=[*out_shape, *[jax.ShapeDtypeStruct(x.shap...]
    unnamed x169 -> x177, local copies, waits for them, and re-layouts: 30.3 us -> 31.3 us
  transfers between devices with their start and end apart: 75 -> 78, of which waited for: 22 -> 21; matrix products, arithmetic and copies ran while one was open for 4% -> 4% of each run, Pallas kernels for 39% -> 41%
where the time goes in v5:
time: 607 us; the launch traced here: 603 us
  Pallas kernels  265 us (44%)
  waiting for transfers between devices  197 us (32%)
  starting transfers between devices  55.1 us (9%)
  local copies, waits for them, and re-layouts  45.4 us (7%)
  blocking collectives  18 us (3%)
  between operations  15.8 us (3%)
    pallas_call x44, Pallas kernels, call(): pl.pallas_call(body, out_shape=[*out_shape, *[jax.ShapeDtypeStruct(x.shap...  265 us
    ppermute x36, waiting for transfers between devices, swap_pairs(): return lax.ppermute(value, ('dp', 'core'), pairs)  160 us
    ppermute x36, starting transfers between devices, swap_pairs(): return lax.ppermute(value, ('dp', 'core'), pairs)  46.6 us
    all_gather x4, waiting for transfers between devices, __init__(): self.gathered = lax.all_gather(mine, ('z', 'core'), axis=0, tiled=False)  32.3 us
    unnamed x177, local copies, waits for them, and re-layouts  31.3 us
    all_gather x1, blocking collectives, gather_small(): full = lax.all_gather(packed, ('z', 'core'), axis=0, tiled=False)  18 us
  transfers between devices with their start and end apart: 78, of which 21 were waited for; matrix products, arithmetic and copies ran while one was open for 4% of the time, Pallas kernels for 41%

profile of v5, /device:TPU:0, one launch (start us, length us, event | category | flops | bytes accessed | tf_op | source)
XLA Modules:
  0.0 603.0 jit_solution(6151467471085532447)
XLA Ops:
  23.1 18.0 %all-gather = bf16[1024,128]{1,0:T(8,128)(2,1)S(1)} all-gather(bf16[128,128]{1,0:T(8,128)(2,1)S(1)} %fusion.9), channel_id=2, replica_groups=mesh['dp'=4,'z'=4,'core'=2] {'z','core'}, dimensions={0}, use_global_device_ids=true | all-gather | bytes 294912 | tf_op jit(solution)/shard_map/all_gather | solution.py:479
  43.6 18.9 %all-gather.10.cloned.1.call-done = bf16[1024,2048]{1,0:T(8,128)(2,1)} async-done(((bf16[128,2048]{1,0:T(8,128)(2,1)}), bf16[1024,2048]{1,0:T(8,128)(2,1)}) %all-gather.10.cloned.1.call-update) | async-done | bytes 4194320 | tf_op jit(solution)/shard_map/all_gather | solution.py:449
  73.2 14.1 %collective-permute-done.1.refs_1_.refs_7_.refs_9_ = bf16[808,1024]{1,0:T(8,128)(2,1)S(1)} collective-permute-done((bf16[808,1024]{1,0:T(8,128)(2,1)}, bf16[808,1024]{1,0:T(8,128)(2,1)S(1)}, u32[]{:S(2)}, u32[]{:S(2)}) %collective-permute-start.1) | collective-permute-done | bytes 1654816 | tf_op jit(solution)/shard_map/ppermute | solution.py:121
  92.7 13.3 %all-gather.12.cloned.1.call-done = bf16[1024,1792]{1,0:T(8,128)(2,1)} async-done(((bf16[128,1792]{1,0:T(8,128)(2,1)}), bf16[1024,1792]{1,0:T(8,128)(2,1)}) %all-gather.12.cloned.1.call-update) | async-done | bytes 3670032 | tf_op jit(solution)/shard_map/all_gather | solution.py:449
  127.5 10.0 %shard_map.272 = (bf16[4,256,1024]{2,1,0:T(8,128)(2,1)}, bf16[5,128,1024]{2,1,0:T(8,128)(2,1)}, bf16[5,128,1024]{2,1,0:T(8,128)(2,1)}, bf16[256,1024]{1,0:T(8,128)(2,1)}) custom-call(s32[3]{0:T(128)} %pad_add_fusion.refs_0_, f32[256,1024]{1,0:T(8,128)} %convolution_add_fusion.refs_1_, ...), custom_call_target="tpu_custom_call", output_to_operand_aliasing={{3}: (11, {})} | custom-call | tf_op jit(solution)/shard_map/pallas_call | solution.py:87
  157.2 13.5 %collective-permute-done.11.refs_13_.refs_8_.refs_11_ = bf16[384,1024]{1,0:T(8,128)(2,1)} collective-permute-done((bf16[384,1024]{1,0:T(8,128)(2,1)}, bf16[384,1024]{1,0:T(8,128)(2,1)}, u32[]{:S(2)}, u32[]{:S(2)}) %collective-permute-start.11) | collective-permute-done | bytes 786464 | tf_op jit(solution)/shard_map/ppermute | solution.py:121
  191.8 9.6 %shard_map.278 = (bf16[256,3072]{1,0:T(8,128)(2,1)}, f32[256,8]{1,0:T(8,128)}, bf16[2,256,1024]{2,1,0:T(8,128)(2,1)}, bf16[256,1024]{1,0:T(8,128)(2,1)}) custom-call(s32[3]{0:T(128)} %pad_add_fusion.refs_0_, f32[256,1024]{1,0:T(8,128)} %get-tuple-element.167.refs_1_, ...), custom_call_target="tpu_custom_call", output_to_operand_aliasing={{3}: (15, {})} | custom-call | tf_op jit(solution)/shard_map/pallas_call | solution.py:87
  214.0 10.0 %shard_map.281 = (f32[256,1024]{1,0:T(8,128)}, bf16[256,2048]{1,0:T(8,128)(2,1)}, f32[256,1024]{1,0:T(8,128)}, bf16[2,256,1024]{2,1,0:T(8,128)(2,1)}, bf16[256,1024]{1,0:T(8,128)(2,1)}) custom-call(s32[3]{0:T(128)} %pad_add_fusion.refs_0_, f32[256,1024]{1,0:T(8,128)} %get-tuple-element.175.refs_1_, ...), custom_call_target="tpu_custom_call", output_to_operand_aliasing={{4}: (20, {})} | custom-call | tf_op jit(solution)/shard_map/pallas_call | solution.py:87
  228.6 10.6 %collective-permute-done.23.refs_12_.refs_8_ = bf16[384,1024]{1,0:T(8,128)(2,1)} collective-permute-done((bf16[384,1024]{1,0:T(8,128)(2,1)}, bf16[384,1024]{1,0:T(8,128)(2,1)}, u32[]{:S(2)}, u32[]{:S(2)}) %collective-permute-start.23) | collective-permute-done | bytes 786464 | tf_op jit(solution)/shard_map/ppermute | solution.py:121
  240.1 9.9 %shard_map.283 = (bf16[4,256,1024]{2,1,0:T(8,128)(2,1)}, bf16[5,128,1024]{2,1,0:T(8,128)(2,1)}, bf16[5,128,1024]{2,1,0:T(8,128)(2,1)}, bf16[256,1024]{1,0:T(8,128)(2,1)}) custom-call(s32[3]{0:T(128)} %pad_add_fusion.refs_0_, f32[256,1024]{1,0:T(8,128)} %get-tuple-element.180.refs_1_, ...), custom_call_target="tpu_custom_call", output_to_operand_aliasing={{3}: (11, {})} | custom-call | tf_op jit(solution)/shard_map/pallas_call | solution.py:87
  250.6 10.0 %shard_map.284 = (bf16[256,1024]{1,0:T(8,128)(2,1)}, f32[256,1024]{1,0:T(8,128)}, bf16[1,256,1024]{2,1,0:T(8,128)(2,1)}, f32[1,1024]{1,0:T(1,128)}, f32[1,1024]{1,0:T(1,128)}, /*index=5*/bf16[256,1024]{1,0:T(8,128)(2,1)}) custom-call(s32[3]{0:T(128)} %pad_add_fusion.refs_0_, ...), custom_call_target="tpu_custom_call", output_to_operand_aliasing={{5}: (14, {})} | custom-call | tf_op jit(solution)/shard_map/pallas_call | solution.py:87
  270.1 9.5 %shard_map.286 = (bf16[4,128,1024]{2,1,0:T(8,128)(2,1)}, bf16[4,128,1024]{2,1,0:T(8,128)(2,1)}, bf16[5,128,1024]{2,1,0:T(8,128)(2,1)}, bf16[5,128,1024]{2,1,0:T(8,128)(2,1)}, bf16[256,1024]{1,0:T(8,128)(2,1)}) custom-call(s32[3]{0:T(128)} %pad_add_fusion.refs_0_, ...), custom_call_target="tpu_custom_call", output_to_operand_aliasing={{2}: (10, {}), {3}: (11, {}), {4}: (12, {})} | custom-call | tf_op jit(solution)/shard_map/pallas_call | solution.py:87
  281.7 9.8 %shard_map.287 = (f32[256,1024]{1,0:T(8,128)}, bf16[1,256,1024]{2,1,0:T(8,128)(2,1)}, f32[1,1024]{1,0:T(1,128)}, f32[1,1024]{1,0:T(1,128)}, bf16[2,256,1024]{2,1...) custom-call(s32[3]{0:T(128)} %pad_add_fusion.refs_0_, ...), custom_call_target="tpu_custom_call", output_to_operand_aliasing={{4}: (13, {}), {5}: (14, {}), {6}: (15, {})} | custom-call | tf_op jit(solution)/shard_map/pallas_call | solution.py:87
  352.2 9.5 %shard_map.294 = (bf16[4,128,1024]{2,1,0:T(8,128)(2,1)}, bf16[4,128,1024]{2,1,0:T(8,128)(2,1)}, bf16[256,1024]{1,0:T(8,128)(2,1)}) custom-call(s32[3]{0:T(128)} %pad_add_fusion.refs_0_, bf16[1,256,1024]{2,1,0:T(8,128)(2,1)} %get-tuple-element.223.refs_1_.refs_9_, bf16[4,256,1024]{2,1,0:T(8,128)(2,1)} %get-tuple-element.224.refs_2_, ...), custom_call_target="tpu_custom_call", output_to_operand_aliasing={{2}: (14, {})} | custom-call | tf_op jit(solution)/shard_map/pallas_call | solution.py:87
  362.6 9.8 %shard_map.295 = (bf16[544,2048]{1,0:T(8,128)(2,1)}, bf16[512,1024]{1,0:T(8,128)(2,1)}, bf16[512,1024]{1,0:T(8,128)(2,1)}, bf16[256,1024]{1,0:T(8,128)(2,1)}) custom-call(s32[3]{0:T(128)} %pad_add_fusion.refs_0_, bf16[1,256,1024]{2,1,0:T(8,128)(2,1)} %get-tuple-element.223.refs_1_.refs_9_, ...), custom_call_target="tpu_custom_call", output_to_operand_aliasing={{3}: (20, {})} | custom-call | tf_op jit(solution)/shard_map/pallas_call | solution.py:87
  376.4 9.7 %shard_map.296 = (f32[256,1024]{1,0:T(8,128)}, bf16[1,256,1024]{2,1,0:T(8,128)(2,1)}, f32[1,1024]{1,0:T(1,128)}, f32[1,1024]{1,0:T(1,128)}, bf16[256,1024]{1,0:T(8,128)(2,1)}) custom-call(s32[3]{0:T(128)} %pad_add_fusion.refs_0_, f32[256,1024]{1,0:T(8,128)} %convolution_add_fusion.refs_1_, ...), custom_call_target="tpu_custom_call", output_to_operand_aliasing={{4}: (13, {})} | custom-call | tf_op jit(solution)/shard_map/pallas_call | solution.py:87
  386.2 14.2 %collective-permute-done.49.refs_31_ = bf16[512,1024]{1,0:T(8,128)(2,1)} collective-permute-done((bf16[512,1024]{1,0:T(8,128)(2,1)}, bf16[512,1024]{1,0:T(8,128)(2,1)}, u32[]{:S(2)}, u32[]{:S(2)}) %collective-permute-start.49) | collective-permute-done | bytes 1048608 | tf_op jit(solution)/shard_map/ppermute | solution.py:121
  400.4 10.8 %shard_map.297 = (bf16[528,2048]{1,0:T(8,128)(2,1)}, bf16[512,1024]{1,0:T(8,128)(2,1)}, bf16[512,1024]{1,0:T(8,128)(2,1)}, bf16[256,1024]{1,0:T(8,128)(2,1)}) custom-call(s32[3]{0:T(128)} %pad_add_fusion.refs_0_, bf16[5,128,1024]{2,1,0:T(8,128)(2,1)} %get-tuple-element.205.refs_9_.refs_3_.refs_1_.refs_11_, ...), custom_call_target="tpu_custom_call", output_to_operand_aliasing={{3}: (32, {})} | custom-call | tf_op jit(solution)/shard_map/pallas_call | solution.py:87
  415.4 22.9 %collective-permute-done.50.refs_27_ = bf16[512,1024]{1,0:T(8,128)(2,1)S(1)} collective-permute-done((bf16[512,1024]{1,0:T(8,128)(2,1)}, bf16[512,1024]{1,0:T(8,128)(2,1)S(1)}, u32[]{:S(2)}, u32[]{:S(2)}) %collective-permute-start.50) | collective-permute-done | bytes 1048608 | tf_op jit(solution)/shard_map/ppermute | solution.py:121
  439.3 11.6 %shard_map.298 = (bf16[592,1792]{1,0:T(8,128)(2,1)}, bf16[512,1024]{1,0:T(8,128)(2,1)}, bf16[512,1024]{1,0:T(8,128)(2,1)}, bf16[256,1024]{1,0:T(8,128)(2,1)}) custom-call(s32[3]{0:T(128)} %pad_add_fusion.refs_0_, bf16[2,256,1024]{2,1,0:T(8,128)(2,1)} %get-tuple-element.204.refs_17_.refs_9_.refs_1_, ...), custom_call_target="tpu_custom_call", output_to_operand_aliasing={{3}: (29, {})} | custom-call | tf_op jit(solution)/shard_map/pallas_call | solution.py:87
  453.6 23.9 %collective-permute-done.53.refs_13_ = bf16[512,1024]{1,0:T(8,128)(2,1)S(1)} collective-permute-done((bf16[512,1024]{1,0:T(8,128)(2,1)}, bf16[512,1024]{1,0:T(8,128)(2,1)S(1)}, u32[]{:S(2)}, u32[]{:S(2)}) %collective-permute-start.53) | collective-permute-done | bytes 1048608 | tf_op jit(solution)/shard_map/ppermute | solution.py:121
  487.2 13.1 %collective-permute-done.54.refs_19_ = bf16[512,1024]{1,0:T(8,128)(2,1)S(1)} collective-permute-done((bf16[512,1024]{1,0:T(8,128)(2,1)}, bf16[512,1024]{1,0:T(8,128)(2,1)S(1)}, u32[]{:S(2)}, u32[]{:S(2)}) %collective-permute-start.54) | collective-permute-done | bytes 1048608 | tf_op jit(solution)/shard_map/ppermute | solution.py:121
  513.3 9.9 %collective-permute-done.55.refs_10_ = bf16[512,896]{1,0:T(8,128)(2,1)S(1)} collective-permute-done((bf16[512,896]{1,0:T(8,128)(2,1)}, bf16[512,896]{1,0:T(8,128)(2,1)S(1)}, u32[]{:S(2)}, u32[]{:S(2)}) %collective-permute-start.55) | collective-permute-done | bytes 917536 | tf_op jit(solution)/shard_map/ppermute | solution.py:121
  546.6 9.2 %collective-permute-done.56.refs_2_ = bf16[128,2048]{1,0:T(8,128)(2,1)S(1)} collective-permute-done((bf16[128,2048]{1,0:T(8,128)(2,1)}, bf16[128,2048]{1,0:T(8,128)(2,1)S(1)}, u32[]{:S(2)}, u32[]{:S(2)}) %collective-permute-start.56) | collective-permute-done | bytes 524320 | tf_op jit(solution)/shard_map/ppermute | solution.py:121
  (431 shorter events, 285.5 us)
Async XLA Ops:
  7.2 55.3 %all-gather.10.cloned.1.call-start = ((), (), s32[]{:S(2)}) async-start(), calls=%async_computation.12 | async-start | bytes 4718592 | tf_op jit(solution)/shard_map/all_gather | solution.py:449
  10.5 95.6 %all-gather.12.cloned.1.call-start = ((), (), s32[]{:S(2)}) async-start(), calls=%async_computation.13 | async-start | bytes 4128768 | tf_op jit(solution)/shard_map/all_gather | solution.py:449
  14.1 138.7 %all-gather.14.cloned.1.call-start = ((), (), s32[]{:S(2)}) async-start(), calls=%async_computation.14 | async-start | bytes 2359296 | tf_op jit(solution)/shard_map/all_gather | solution.py:449
  21.8 51.4 %collective-permute-start = (bf16[128,23552]{1,0:T(8,128)(2,1)}, bf16[128,23552]{1,0:T(8,128)(2,1)}, u32[]{:S(2)}, u32[]{:S(2)}) collective-permute-start(bf16[128,23552]{1,0:T(8,128)(2,1)} %constant_dynamic-update-slice_fusion), channel_id=1, source_target_pairs={{0,1},{1,0},{2,3},{3,2},{4,5},{5,4},{6,7},{7,6},{8,9},{9,8},{10,11... | collective-permute-start | bytes 18087944 | tf_op jit(solution)/shard_map/ppermute | solution.py:112
  23.0 160.1 %all-gather.16.cloned.1.call-start = ((), (), s32[]{:S(2)}) async-start(), calls=%async_computation.15 | async-start | bytes 2359296 | tf_op jit(solution)/shard_map/all_gather | solution.py:449
  70.5 47.2 %collective-permute-start.5 = (bf16[800,1024]{1,0:T(8,128)(2,1)}, bf16[800,1024]{1,0:T(8,128)(2,1)}, u32[]{:S(2)}, u32[]{:S(2)}) collective-permute-start(bf16[800,1024]{1,0:T(8,128)(2,1)} %get-tuple-element.155), channel_id=1, source_target_pairs={{0,8},{1,17},{8,0},{9,25},{16,24},{17,1},{24,16},{25,9},{2,10},{3,... | collective-permute-start | bytes 4915208 | tf_op jit(solution)/shard_map/ppermute | solution.py:121
  72.9 342.5 %reduce-scatter.7.cloned.1.call-start = ((), (), s32[]{:S(2)}) async-start(), calls=%async_computation.6 | async-start | bytes 1310720 | tf_op jit(solution)/shard_map/reduce_scatter | solution.py:400
  117.8 38.9 %collective-permute-start.6 = (bf16[800,1024]{1,0:T(8,128)(2,1)}, bf16[800,1024]{1,0:T(8,128)(2,1)}, u32[]{:S(2)}, u32[]{:S(2)}) collective-permute-start(bf16[800,1024]{1,0:T(8,128)(2,1)} %collective-permute-done.5.refs_1_.refs_7_.refs_6_), channel_id=1, source_target_pairs={{0,1},{1,0},{2,3},{3,2},{4,5},{5,4},{6,7},{7,6},{8,9},{9,8},{10,11... | collective-permute-start | bytes 4915208 | tf_op jit(solution)/shard_map/ppermute | solution.py:112
  121.0 35.7 %collective-permute-start.7 = (bf16[384,1024]{1,0:T(8,128)(2,1)}, bf16[384,1024]{1,0:T(8,128)(2,1)}, u32[]{:S(2)}, u32[]{:S(2)}) collective-permute-start(bf16[384,1024]{1,0:T(8,128)(2,1)} %get-tuple-element.162), channel_id=1, source_target_pairs={{0,16},{1,9},{8,24},{9,1},{16,0},{17,25},{24,8},{25,17},{2,18},{3,... | collective-permute-start | bytes 2359304 | tf_op jit(solution)/shard_map/ppermute | solution.py:121
  156.0 34.1 %collective-permute-start.17 = (bf16[776,1024]{1,0:T(8,128)(2,1)}, bf16[776,1024]{1,0:T(8,128)(2,1)}, u32[]{:S(2)}, u32[]{:S(2)}) collective-permute-start(bf16[776,1024]{1,0:T(8,128)(2,1)} %get-tuple-element.177), channel_id=1, source_target_pairs={{0,8},{1,17},{8,0},{9,25},{16,24},{17,1},{24,16},{25,9},{2,10},{3,... | collective-permute-start | bytes 4767752 | tf_op jit(solution)/shard_map/ppermute | solution.py:121
  156.7 35.2 %collective-permute-start.10 = (bf16[792,1024]{1,0:T(8,128)(2,1)S(1)}, bf16[792,1024]{1,0:T(8,128)(2,1)}, u32[]{:S(2)}, u32[]{:S(2)}) collective-permute-start(bf16[792,1024]{1,0:T(8,128)(2,1)S(1)} %copy-done.4), channel_id=1, source_target_pairs={{0,1},{1,0},{2,3},{3,2},{4,5},{5,4},{6,7},{7,6},{8,9},{9,8},{10,11... | collective-permute-start | bytes 4866056 | tf_op jit(solution)/shard_map/ppermute | solution.py:112
  186.5 37.6 %collective-permute-start.21 = (bf16[768,1024]{1,0:T(8,128)(2,1)}, bf16[768,1024]{1,0:T(8,128)(2,1)}, u32[]{:S(2)}, u32[]{:S(2)}) collective-permute-start(bf16[768,1024]{1,0:T(8,128)(2,1)} %get-tuple-element.182), channel_id=1, source_target_pairs={{0,8},{1,17},{8,0},{9,25},{16,24},{17,1},{24,16},{25,9},{2,10},{3,... | collective-permute-start | bytes 4718600 | tf_op jit(solution)/shard_map/ppermute | solution.py:121
  190.1 49.0 %collective-permute-start.18 = (bf16[776,1024]{1,0:T(8,128)(2,1)}, bf16[776,1024]{1,0:T(8,128)(2,1)}, u32[]{:S(2)}, u32[]{:S(2)}) collective-permute-start(bf16[776,1024]{1,0:T(8,128)(2,1)} %collective-permute-done.17.refs_1_.refs_7_.refs_9_), channel_id=1, source_target_pairs={{0,1},{1,0},{2,3},{3,2},{4,5},{5,4},{6,7},{7,6},{8,9},{9,8},{10,11... | collective-permute-start | bytes 4767752 | tf_op jit(solution)/shard_map/ppermute | solution.py:112
  280.7 40.6 %collective-permute-start.38 = (bf16[592,2048]{1,0:T(8,128)(2,1)}, bf16[592,2048]{1,0:T(8,128)(2,1)}, u32[]{:S(2)}, u32[]{:S(2)}) collective-permute-start(bf16[592,2048]{1,0:T(8,128)(2,1)} %get-tuple-element.216), channel_id=1, source_target_pairs={{0,8},{1,17},{8,0},{9,25},{16,24},{17,1},{24,16},{25,9},{2,10},{3,... | collective-permute-start | bytes 7274504 | tf_op jit(solution)/shard_map/ppermute | solution.py:121
  300.0 61.8 %collective-permute-start.42 = (bf16[576,2048]{1,0:T(8,128)(2,1)}, bf16[576,2048]{1,0:T(8,128)(2,1)}, u32[]{:S(2)}, u32[]{:S(2)}) collective-permute-start(bf16[576,2048]{1,0:T(8,128)(2,1)} %get-tuple-element.228), channel_id=1, source_target_pairs={{0,8},{1,17},{8,0},{9,25},{16,24},{17,1},{24,16},{25,9},{2,10},{3,... | collective-permute-start | bytes 7077896 | tf_op jit(solution)/shard_map/ppermute | solution.py:121
  350.1 50.3 %collective-permute-start.46 = (bf16[560,2048]{1,0:T(8,128)(2,1)}, bf16[560,2048]{1,0:T(8,128)(2,1)}, u32[]{:S(2)}, u32[]{:S(2)}) collective-permute-start(bf16[560,2048]{1,0:T(8,128)(2,1)} %get-tuple-element.248), channel_id=1, source_target_pairs={{0,8},{1,17},{8,0},{9,25},{16,24},{17,1},{24,16},{25,9},{2,10},{3,... | collective-permute-start | bytes 6881288 | tf_op jit(solution)/shard_map/ppermute | solution.py:121
  372.5 81.1 %reduce-scatter.9.cloned.1.call-start = ((), (), s32[]{:S(2)}) async-start(), calls=%async_computation.7 | async-start | bytes 1310720 | tf_op jit(solution)/shard_map/reduce_scatter | solution.py:400
  375.4 63.0 %collective-permute-start.45 = (bf16[544,2048]{1,0:T(8,128)(2,1)}, bf16[544,2048]{1,0:T(8,128)(2,1)}, u32[]{:S(2)}, u32[]{:S(2)}) collective-permute-start(bf16[544,2048]{1,0:T(8,128)(2,1)} %get-tuple-element.247), channel_id=1, source_target_pairs={{0,8},{1,17},{8,0},{9,25},{16,24},{17,1},{24,16},{25,9},{2,10},{3,... | collective-permute-start | bytes 6684680 | tf_op jit(solution)/shard_map/ppermute | solution.py:121
  411.3 75.9 %reduce-scatter.11.cloned.1.call-start = ((), (), s32[]{:S(2)}) async-start(), calls=%async_computation.8 | async-start | bytes 1310720 | tf_op jit(solution)/shard_map/reduce_scatter | solution.py:400
  413.9 39.7 %collective-permute-start.52 = (bf16[528,2048]{1,0:T(8,128)(2,1)}, bf16[528,2048]{1,0:T(8,128)(2,1)}, u32[]{:S(2)}, u32[]{:S(2)}) collective-permute-start(bf16[528,2048]{1,0:T(8,128)(2,1)} %get-tuple-element.255), channel_id=1, source_target_pairs={{0,8},{1,17},{8,0},{9,25},{16,24},{17,1},{24,16},{25,9},{2,10},{3,... | collective-permute-start | bytes 6488072 | tf_op jit(solution)/shard_map/ppermute | solution.py:121
  450.9 72.3 %reduce-scatter.13.cloned.1.call-start = ((), (), s32[]{:S(2)}) async-start(), calls=%async_computation.9 | async-start | bytes 1310720 | tf_op jit(solution)/shard_map/reduce_scatter | solution.py:400
  453.0 47.3 %collective-permute-start.51 = (bf16[592,1792]{1,0:T(8,128)(2,1)}, bf16[592,1792]{1,0:T(8,128)(2,1)S(1)}, u32[]{:S(2)}, u32[]{:S(2)}) collective-permute-start(bf16[592,1792]{1,0:T(8,128)(2,1)} %get-tuple-element.254), channel_id=1, source_target_pairs={{0,8},{1,17},{8,0},{9,25},{16,24},{17,1},{24,16},{25,9},{2,10},{3,... | collective-permute-start | bytes 6365192 | tf_op jit(solution)/shard_map/ppermute | solution.py:121
  485.2 78.0 %reduce-scatter.17.cloned.1.call-start = ((), (), s32[]{:S(2)}) async-start(), calls=%async_computation.11 | async-start | bytes 1310720 | tf_op jit(solution)/shard_map/reduce_scatter | solution.py:400
  509.5 61.4 %reduce-scatter.15.cloned.1.call-start = ((), (), s32[]{:S(2)}) async-start(), calls=%async_computation.10 | async-start | bytes 1146880 | tf_op jit(solution)/shard_map/reduce_scatter | solution.py:400
  (137 other events, 1528.5 us)
Sparse Core Ops, SparseCore 0:
  10.6 51.8 all-gather.9
  64.7 41.3 all-gather.11
  108.2 27.9 all-gather.13
  138.3 28.5 all-gather.15
  372.6 25.1 reduce-scatter.6
  411.4 25.1 reduce-scatter.8
  451.0 25.5 reduce-scatter.10
  485.3 25.6 reduce-scatter.12
  513.3 25.7 reduce-scatter.16
  541.4 23.7 reduce-scatter.14

commit v6 on v5

--- a/solution.py
+++ b/solution.py
@@ -98,7 +98,7 @@
         return result[:-1]
 
 
-VMEM_LIMIT = 60 * 1024 * 1024
+VMEM_LIMIT = 52 * 1024 * 1024
 QUARTERS = 4
 LANES = 128
 BITS = (0, 1)

time: 607 us -> 600 us (0.988)
  Pallas kernels: 265 us -> 235 us
  waiting for transfers between devices: 197 us -> 217 us
  local copies, waits for them, and re-layouts: 45.4 us -> 55.3 us
  starting transfers between devices: 55.1 us -> 46.9 us
    pallas_call x44, Pallas kernels: 265 us -> 235 us  [call(): pl.pallas_call(body, out_shape=[*out_shape, *[jax.ShapeDtypeStruct(x.shap...]
    ppermute x36, waiting for transfers between devices: 160 us -> 178 us  [swap_pairs(): return lax.ppermute(value, ('dp', 'core'), pairs)]
    ppermute x36, starting transfers between devices: 46.6 us -> 37.7 us  [swap_pairs(): return lax.ppermute(value, ('dp', 'core'), pairs)]
    unnamed x177 -> x179, local copies, waits for them, and re-layouts: 31.3 us -> 37.5 us
  transfers between devices with their start and end apart: 78 -> 78, of which waited for: 21 -> 24; matrix products, arithmetic and copies ran while one was open for 4% -> 4% of each run, Pallas kernels for 41% -> 37%
where the time goes in v6:
time: 600 us; the launch traced here: 596 us
  Pallas kernels  235 us (39%)
  waiting for transfers between devices  217 us (36%)
  local copies, waits for them, and re-layouts  55.3 us (9%)
  starting transfers between devices  46.9 us (8%)
  blocking collectives  20.1 us (3%)
  between operations  15.9 us (3%)
    pallas_call x44, Pallas kernels, call(): pl.pallas_call(body, out_shape=[*out_shape, *[jax.ShapeDtypeStruct(x.shap...  235 us
    ppermute x36, waiting for transfers between devices, swap_pairs(): return lax.ppermute(value, ('dp', 'core'), pairs)  178 us
    ppermute x36, starting transfers between devices, swap_pairs(): return lax.ppermute(value, ('dp', 'core'), pairs)  37.7 us
    unnamed x179, local copies, waits for them, and re-layouts  37.5 us
    all_gather x4, waiting for transfers between devices, __init__(): self.gathered = lax.all_gather(mine, ('z', 'core'), axis=0, tiled=False)  33.5 us
    all_gather x1, blocking collectives, gather_small(): full = lax.all_gather(packed, ('z', 'core'), axis=0, tiled=False)  20.1 us
  transfers between devices with their start and end apart: 78, of which 24 were waited for; matrix products, arithmetic and copies ran while one was open for 4% of the time, Pallas kernels for 37%

profile of v6, /device:TPU:0, one launch (start us, length us, event | category | flops | bytes accessed | tf_op | source)
XLA Modules:
  0.0 595.5 jit_solution(17339670633887455446)
XLA Ops:
  21.6 20.1 %all-gather = bf16[1024,128]{1,0:T(8,128)(2,1)S(1)} all-gather(bf16[128,128]{1,0:T(8,128)(2,1)S(1)} %fusion.9), channel_id=2, replica_groups=mesh['dp'=4,'z'=4,'core'=2] {'z','core'}, dimensions={0}, use_global_device_ids=true | all-gather | bytes 294912 | tf_op jit(solution)/shard_map/all_gather | solution.py:479
  43.7 18.8 %all-gather.10.cloned.1.call-done = bf16[1024,2048]{1,0:T(8,128)(2,1)} async-done(((bf16[128,2048]{1,0:T(8,128)(2,1)}), bf16[1024,2048]{1,0:T(8,128)(2,1)}) %all-gather.10.cloned.1.call-update) | async-done | bytes 4194320 | tf_op jit(solution)/shard_map/all_gather | solution.py:449
  73.1 14.1 %collective-permute-done.1.refs_1_.refs_7_.refs_9_ = bf16[808,1024]{1,0:T(8,128)(2,1)} collective-permute-done((bf16[808,1024]{1,0:T(8,128)(2,1)}, bf16[808,1024]{1,0:T(8,128)(2,1)}, u32[]{:S(2)}, u32[]{:S(2)}) %collective-permute-start.1) | collective-permute-done | bytes 1654816 | tf_op jit(solution)/shard_map/ppermute | solution.py:121
  91.3 14.7 %all-gather.12.cloned.1.call-done = bf16[1024,1792]{1,0:T(8,128)(2,1)} async-done(((bf16[128,1792]{1,0:T(8,128)(2,1)}), bf16[1024,1792]{1,0:T(8,128)(2,1)}) %all-gather.12.cloned.1.call-update) | async-done | bytes 3670032 | tf_op jit(solution)/shard_map/all_gather | solution.py:449
  132.4 11.0 %collective-permute-done.9.refs_1_.refs_11_.refs_6_.refs_9_ = bf16[792,1024]{1,0:T(8,128)(2,1)} collective-permute-done((bf16[792,1024]{1,0:T(8,128)(2,1)}, bf16[792,1024]{1,0:T(8,128)(2,1)}, u32[]{:S(2)}, u32[]{:S(2)}) %collective-permute-start.9) | collective-permute-done | bytes 1622048 | tf_op jit(solution)/shard_map/ppermute | solution.py:121
  153.3 13.5 %collective-permute-done.11.refs_13_.refs_8_.refs_11_ = bf16[384,1024]{1,0:T(8,128)(2,1)S(1)} collective-permute-done((bf16[384,1024]{1,0:T(8,128)(2,1)}, bf16[384,1024]{1,0:T(8,128)(2,1)S(1)}, u32[]{:S(2)}, u32[]{:S(2)}) %collective-permute-start.11) | collective-permute-done | bytes 786464 | tf_op jit(solution)/shard_map/ppermute | solution.py:121
  208.8 9.1 %shard_map.281 = (f32[256,1024]{1,0:T(8,128)}, bf16[256,2048]{1,0:T(8,128)(2,1)}, f32[256,1024]{1,0:T(8,128)}, bf16[2,256,1024]{2,1,0:T(8,128)(2,1)}, bf16[256,1024]{1,0:T(8,128)(2,1)S(1)}) custom-call(s32[3]{0:T(128)S(1)} %pad_add_fusion.refs_0_, f32[256,1024]{1,0:T(8,128)} %get-tuple-element.175.refs_1_, ...), custom_call_target="tpu_custom_call", output_to_operand_aliasing={{4}: (20, {})} | custom-call | tf_op jit(solution)/shard_map/pallas_call | solution.py:87
  220.9 10.9 %collective-permute-done.23.refs_12_.refs_8_ = bf16[384,1024]{1,0:T(8,128)(2,1)S(1)} collective-permute-done((bf16[384,1024]{1,0:T(8,128)(2,1)S(1)}, bf16[384,1024]{1,0:T(8,128)(2,1)S(1)}, u32[]{:S(2)}, u32[]{:S(2)}) %collective-permute-start.23) | collective-permute-done | bytes 786464 | tf_op jit(solution)/shard_map/ppermute | solution.py:121
  243.3 9.7 %shard_map.284 = (bf16[256,1024]{1,0:T(8,128)(2,1)}, f32[256,1024]{1,0:T(8,128)}, bf16[1,256,1024]{2,1,0:T(8,128)(2,1)S(1)}, f32[1,1024]{1,0:T(1,128)S(1)}, f32[...) custom-call(s32[3]{0:T(128)S(1)} %pad_add_fusion.refs_0_, ...), custom_call_target="tpu_custom_call", output_to_operand_aliasing={{5}: (14, {})} | custom-call | tf_op jit(solution)/shard_map/pallas_call | solution.py:87
  261.4 8.8 %shard_map.286 = (bf16[4,128,1024]{2,1,0:T(8,128)(2,1)}, bf16[4,128,1024]{2,1,0:T(8,128)(2,1)}, bf16[5,128,1024]{2,1,0:T(8,128)(2,1)}, bf16[5,128,1024]{2,1,0:T(8,128)(2,1)}, bf16[256,1024]{1,0:T(8,128)(2,1)S(1)}) custom-call(s32[3]{0:T(128)S(1)} %pad_add_fusion.refs_0_, ...), custom_call_target="tpu_custom_call", output_to_operand_aliasing={{2}: (10, {}), {3}: (11, {}), {4}: (12, {})} | custom-call | tf_op jit(solution)/shard_map/pallas_call | solution.py:87
  271.5 9.2 %shard_map.287 = (f32[256,1024]{1,0:T(8,128)}, bf16[1,256,1024]{2,1,0:T(8,128)(2,1)S(1)}, f32[1,1024]{1,0:T(1,128)S(1)}, f32[1,1024]{1,0:T(1,128)S(1)}, bf16[2,2...) custom-call(s32[3]{0:T(128)S(1)} %pad_add_fusion.refs_0_, ...), custom_call_target="tpu_custom_call", output_to_operand_aliasing={{4}: (13, {}), {5}: (14, {}), {6}: (15, {})} | custom-call | tf_op jit(solution)/shard_map/pallas_call | solution.py:87
  321.1 8.8 %shard_map.292 = (bf16[4,128,768]{2,1,0:T(8,128)(2,1)}, bf16[4,128,768]{2,1,0:T(8,128)(2,1)}, bf16[256,1024]{1,0:T(8,128)(2,1)S(1)}) custom-call(s32[3]{0:T(128)S(1)} %pad_add_fusion.refs_0_, bf16[1,256,1024]{2,1,0:T(8,128)(2,1)S(1)} %copy-done.13, bf16[256,3072]{1,0:T(8,128)(2,1)} %get-tuple-element.214.refs_2_, ...), custom_call_target="tpu_custom_call", output_to_operand_aliasing={{2}: (15, {})} | custom-call | tf_op jit(solution)/shard_map/pallas_call | solution.py:87
  347.4 9.2 %shard_map.294 = (bf16[4,128,1024]{2,1,0:T(8,128)(2,1)}, bf16[4,128,1024]{2,1,0:T(8,128)(2,1)}, bf16[256,1024]{1,0:T(8,128)(2,1)S(1)}) custom-call(s32[3]{0:T(128)S(1)} %pad_add_fusion.refs_0_, bf16[1,256,1024]{2,1,0:T(8,128)(2,1)S(1)} %get-tuple-element.223.refs_1_.refs_9_, ...), custom_call_target="tpu_custom_call", output_to_operand_aliasing={{2}: (14, {})} | custom-call | tf_op jit(solution)/shard_map/pallas_call | solution.py:87
  356.6 9.6 %shard_map.295 = (bf16[544,2048]{1,0:T(8,128)(2,1)}, bf16[512,1024]{1,0:T(8,128)(2,1)}, bf16[512,1024]{1,0:T(8,128)(2,1)}, bf16[256,1024]{1,0:T(8,128)(2,1)S(1)}) custom-call(s32[3]{0:T(128)S(1)} %pad_add_fusion.refs_0_, bf16[1,256,1024]{2,1,0:T(8,128)(2,1)S(1)} %get-tuple-element.223.refs_1_.refs_9_, ...), custom_call_target="tpu_custom_call", output_to_operand_aliasing={{3}: (20, {})} | custom-call | tf_op jit(solution)/shard_map/pallas_call | solution.py:87
  371.2 9.2 %shard_map.296 = (f32[256,1024]{1,0:T(8,128)}, bf16[1,256,1024]{2,1,0:T(8,128)(2,1)S(1)}, f32[1,1024]{1,0:T(1,128)S(1)}, f32[1,1024]{1,0:T(1,128)S(1)}, bf16[256,1024]{1,0:T(8,128)(2,1)S(1)}) custom-call(s32[3]{0:T(128)S(1)} %pad_add_fusion.refs_0_, f32[256,1024]{1,0:T(8,128)} %convolution_add_fusion.refs_1_, ...), custom_call_target="tpu_custom_call", output_to_operand_aliasing={{4}: (13, {})} | custom-call | tf_op jit(solution)/shard_map/pallas_call | solution.py:87
  380.4 14.6 %collective-permute-done.49.refs_31_ = bf16[512,1024]{1,0:T(8,128)(2,1)S(1)} collective-permute-done((bf16[512,1024]{1,0:T(8,128)(2,1)}, bf16[512,1024]{1,0:T(8,128)(2,1)S(1)}, u32[]{:S(2)}, u32[]{:S(2)}) %collective-permute-start.49) | collective-permute-done | bytes 1048608 | tf_op jit(solution)/shard_map/ppermute | solution.py:121
  396.0 9.2 %shard_map.297 = (bf16[528,2048]{1,0:T(8,128)(2,1)}, bf16[512,1024]{1,0:T(8,128)(2,1)}, bf16[512,1024]{1,0:T(8,128)(2,1)}, bf16[256,1024]{1,0:T(8,128)(2,1)S(1)}) custom-call(s32[3]{0:T(128)S(1)} %pad_add_fusion.refs_0_, bf16[5,128,1024]{2,1,0:T(8,128)(2,1)} %get-tuple-element.205.refs_9_.refs_3_.refs_1_.refs_11_, ...), custom_call_target="tpu_custom_call", output_to_operand_aliasing={{3}: (32, {})} | custom-call | tf_op jit(solution)/shard_map/pallas_call | solution.py:87
  411.8 23.3 %collective-permute-done.50.refs_27_ = bf16[512,1024]{1,0:T(8,128)(2,1)S(1)} collective-permute-done((bf16[512,1024]{1,0:T(8,128)(2,1)}, bf16[512,1024]{1,0:T(8,128)(2,1)S(1)}, u32[]{:S(2)}, u32[]{:S(2)}) %collective-permute-start.50) | collective-permute-done | bytes 1048608 | tf_op jit(solution)/shard_map/ppermute | solution.py:121
  436.9 11.3 %shard_map.298 = (bf16[592,1792]{1,0:T(8,128)(2,1)}, bf16[512,1024]{1,0:T(8,128)(2,1)}, bf16[512,1024]{1,0:T(8,128)(2,1)}, bf16[256,1024]{1,0:T(8,128)(2,1)S(1)}) custom-call(s32[3]{0:T(128)S(1)} %pad_add_fusion.refs_0_, bf16[2,256,1024]{2,1,0:T(8,128)(2,1)} %get-tuple-element.204.refs_17_.refs_9_.refs_1_, ...), custom_call_target="tpu_custom_call", output_to_operand_aliasing={{3}: (29, {})} | custom-call | tf_op jit(solution)/shard_map/pallas_call | solution.py:87
  450.8 24.2 %collective-permute-done.53.refs_13_ = bf16[512,1024]{1,0:T(8,128)(2,1)S(1)} collective-permute-done((bf16[512,1024]{1,0:T(8,128)(2,1)}, bf16[512,1024]{1,0:T(8,128)(2,1)S(1)}, u32[]{:S(2)}, u32[]{:S(2)}) %collective-permute-start.53) | collective-permute-done | bytes 1048608 | tf_op jit(solution)/shard_map/ppermute | solution.py:121
  482.3 15.0 %collective-permute-done.54.refs_19_ = bf16[512,1024]{1,0:T(8,128)(2,1)S(1)} collective-permute-done((bf16[512,1024]{1,0:T(8,128)(2,1)}, bf16[512,1024]{1,0:T(8,128)(2,1)S(1)}, u32[]{:S(2)}, u32[]{:S(2)}) %collective-permute-start.54) | collective-permute-done | bytes 1048608 | tf_op jit(solution)/shard_map/ppermute | solution.py:121
  506.0 13.3 %collective-permute-done.55.refs_10_ = bf16[512,896]{1,0:T(8,128)(2,1)} collective-permute-done((bf16[512,896]{1,0:T(8,128)(2,1)}, bf16[512,896]{1,0:T(8,128)(2,1)}, u32[]{:S(2)}, u32[]{:S(2)}) %collective-permute-start.55) | collective-permute-done | bytes 917536 | tf_op jit(solution)/shard_map/ppermute | solution.py:121
  527.6 12.4 %collective-permute-done.59.refs_2_ = bf16[128,2048]{1,0:T(8,128)(2,1)S(1)} collective-permute-done((bf16[128,2048]{1,0:T(8,128)(2,1)S(1)}, bf16[128,2048]{1,0:T(8,128)(2,1)S(1)}, u32[]{:S(2)}, u32[]{:S(2)}) %collective-permute-start.59) | collective-permute-done | bytes 524320 | tf_op jit(solution)/shard_map/ppermute | solution.py:121
  542.0 9.2 %collective-permute-done.56.refs_2_ = bf16[128,2048]{1,0:T(8,128)(2,1)S(1)} collective-permute-done((bf16[128,2048]{1,0:T(8,128)(2,1)S(1)}, bf16[128,2048]{1,0:T(8,128)(2,1)S(1)}, u32[]{:S(2)}, u32[]{:S(2)}) %collective-permute-start.56) | collective-permute-done | bytes 524320 | tf_op jit(solution)/shard_map/ppermute | solution.py:121
  (433 shorter events, 270.7 us)
Async XLA Ops:
  7.2 55.2 %all-gather.10.cloned.1.call-start = ((), (), s32[]{:S(2)}) async-start(), calls=%async_computation.12 | async-start | bytes 4718592 | tf_op jit(solution)/shard_map/all_gather | solution.py:449
  10.4 95.7 %all-gather.12.cloned.1.call-start = ((), (), s32[]{:S(2)}) async-start(), calls=%async_computation.13 | async-start | bytes 4128768 | tf_op jit(solution)/shard_map/all_gather | solution.py:449
  11.4 137.6 %all-gather.14.cloned.1.call-start = ((), (), s32[]{:S(2)}) async-start(), calls=%async_computation.14 | async-start | bytes 2359296 | tf_op jit(solution)/shard_map/all_gather | solution.py:449
  20.3 52.8 %collective-permute-start = (bf16[128,23552]{1,0:T(8,128)(2,1)}, bf16[128,23552]{1,0:T(8,128)(2,1)}, u32[]{:S(2)}, u32[]{:S(2)}) collective-permute-start(bf16[128,23552]{1,0:T(8,128)(2,1)} %constant_dynamic-update-slice_fusion), channel_id=1, source_target_pairs={{0,1},{1,0},{2,3},{3,2},{4,5},{5,4},{6,7},{7,6},{8,9},{9,8},{10,11... | collective-permute-start | bytes 18087944 | tf_op jit(solution)/shard_map/ppermute | solution.py:112
  21.5 157.4 %all-gather.16.cloned.1.call-start = ((), (), s32[]{:S(2)}) async-start(), calls=%async_computation.15 | async-start | bytes 2359296 | tf_op jit(solution)/shard_map/all_gather | solution.py:449
  70.2 45.0 %collective-permute-start.5 = (bf16[800,1024]{1,0:T(8,128)(2,1)}, bf16[800,1024]{1,0:T(8,128)(2,1)}, u32[]{:S(2)}, u32[]{:S(2)}) collective-permute-start(bf16[800,1024]{1,0:T(8,128)(2,1)} %get-tuple-element.155), channel_id=1, source_target_pairs={{0,8},{1,17},{8,0},{9,25},{16,24},{17,1},{24,16},{25,9},{2,10},{3,... | collective-permute-start | bytes 4915208 | tf_op jit(solution)/shard_map/ppermute | solution.py:121
  72.5 339.2 %reduce-scatter.7.cloned.1.call-start = ((), (), s32[]{:S(2)}) async-start(), calls=%async_computation.6 | async-start | bytes 1310720 | tf_op jit(solution)/shard_map/reduce_scatter | solution.py:400
  115.2 37.6 %collective-permute-start.6 = (bf16[800,1024]{1,0:T(8,128)(2,1)}, bf16[800,1024]{1,0:T(8,128)(2,1)}, u32[]{:S(2)}, u32[]{:S(2)}) collective-permute-start(bf16[800,1024]{1,0:T(8,128)(2,1)} %collective-permute-done.5.refs_1_.refs_7_.refs_6_), channel_id=1, source_target_pairs={{0,1},{1,0},{2,3},{3,2},{4,5},{5,4},{6,7},{7,6},{8,9},{9,8},{10,11... | collective-permute-start | bytes 4915208 | tf_op jit(solution)/shard_map/ppermute | solution.py:112
  118.3 34.5 %collective-permute-start.7 = (bf16[384,1024]{1,0:T(8,128)(2,1)}, bf16[384,1024]{1,0:T(8,128)(2,1)}, u32[]{:S(2)}, u32[]{:S(2)}) collective-permute-start(bf16[384,1024]{1,0:T(8,128)(2,1)} %get-tuple-element.162), channel_id=1, source_target_pairs={{0,16},{1,9},{8,24},{9,1},{16,0},{17,25},{24,8},{25,17},{2,18},{3,... | collective-permute-start | bytes 2359304 | tf_op jit(solution)/shard_map/ppermute | solution.py:121
  152.8 34.6 %collective-permute-start.10 = (bf16[792,1024]{1,0:T(8,128)(2,1)}, bf16[792,1024]{1,0:T(8,128)(2,1)}, u32[]{:S(2)}, u32[]{:S(2)}) collective-permute-start(bf16[792,1024]{1,0:T(8,128)(2,1)} %collective-permute-done.9.refs_1_.refs_11_.refs_6_.refs_9_), channel_id=1, source_target_pairs={{0,1},{1,0},{2,3},{3,2},{4,5},{5,4},{6,7},{7,6},{8,9},{9,8},{10,11... | collective-permute-start | bytes 4866056 | tf_op jit(solution)/shard_map/ppermute | solution.py:112
  182.1 35.9 %collective-permute-start.21 = (bf16[768,1024]{1,0:T(8,128)(2,1)}, bf16[768,1024]{1,0:T(8,128)(2,1)}, u32[]{:S(2)}, u32[]{:S(2)}) collective-permute-start(bf16[768,1024]{1,0:T(8,128)(2,1)} %get-tuple-element.182), channel_id=1, source_target_pairs={{0,8},{1,17},{8,0},{9,25},{16,24},{17,1},{24,16},{25,9},{2,10},{3,... | collective-permute-start | bytes 4718600 | tf_op jit(solution)/shard_map/ppermute | solution.py:121
  185.7 46.1 %collective-permute-start.18 = (bf16[776,1024]{1,0:T(8,128)(2,1)}, bf16[776,1024]{1,0:T(8,128)(2,1)}, u32[]{:S(2)}, u32[]{:S(2)}) collective-permute-start(bf16[776,1024]{1,0:T(8,128)(2,1)} %collective-permute-done.17.refs_1_.refs_7_.refs_9_), channel_id=1, source_target_pairs={{0,1},{1,0},{2,3},{3,2},{4,5},{5,4},{6,7},{7,6},{8,9},{9,8},{10,11... | collective-permute-start | bytes 4767752 | tf_op jit(solution)/shard_map/ppermute | solution.py:112
  271.2 39.9 %collective-permute-start.38 = (bf16[592,2048]{1,0:T(8,128)(2,1)}, bf16[592,2048]{1,0:T(8,128)(2,1)}, u32[]{:S(2)}, u32[]{:S(2)}) collective-permute-start(bf16[592,2048]{1,0:T(8,128)(2,1)} %get-tuple-element.216), channel_id=1, source_target_pairs={{0,8},{1,17},{8,0},{9,25},{16,24},{17,1},{24,16},{25,9},{2,10},{3,... | collective-permute-start | bytes 7274504 | tf_op jit(solution)/shard_map/ppermute | solution.py:121
  288.7 67.9 %collective-permute-start.42 = (bf16[576,2048]{1,0:T(8,128)(2,1)}, bf16[576,2048]{1,0:T(8,128)(2,1)}, u32[]{:S(2)}, u32[]{:S(2)}) collective-permute-start(bf16[576,2048]{1,0:T(8,128)(2,1)} %get-tuple-element.228), channel_id=1, source_target_pairs={{0,8},{1,17},{8,0},{9,25},{16,24},{17,1},{24,16},{25,9},{2,10},{3,... | collective-permute-start | bytes 7077896 | tf_op jit(solution)/shard_map/ppermute | solution.py:121
  319.4 37.2 %collective-permute-start.43 = (bf16[512,1024]{1,0:T(8,128)(2,1)}, bf16[512,1024]{1,0:T(8,128)(2,1)}, u32[]{:S(2)}, u32[]{:S(2)}) collective-permute-start(bf16[512,1024]{1,0:T(8,128)(2,1)} %get-tuple-element.229), channel_id=1, source_target_pairs={{0,16},{1,9},{8,24},{9,1},{16,0},{17,25},{24,8},{25,17},{2,18},{3,... | collective-permute-start | bytes 3145736 | tf_op jit(solution)/shard_map/ppermute | solution.py:121
  340.3 54.7 %collective-permute-start.46 = (bf16[560,2048]{1,0:T(8,128)(2,1)}, bf16[560,2048]{1,0:T(8,128)(2,1)}, u32[]{:S(2)}, u32[]{:S(2)}) collective-permute-start(bf16[560,2048]{1,0:T(8,128)(2,1)} %get-tuple-element.248), channel_id=1, source_target_pairs={{0,8},{1,17},{8,0},{9,25},{16,24},{17,1},{24,16},{25,9},{2,10},{3,... | collective-permute-start | bytes 6881288 | tf_op jit(solution)/shard_map/ppermute | solution.py:121
  366.2 84.5 %reduce-scatter.9.cloned.1.call-start = ((), (), s32[]{:S(2)}) async-start(), calls=%async_computation.7 | async-start | bytes 1310720 | tf_op jit(solution)/shard_map/reduce_scatter | solution.py:400
  369.4 65.6 %collective-permute-start.45 = (bf16[544,2048]{1,0:T(8,128)(2,1)}, bf16[544,2048]{1,0:T(8,128)(2,1)}, u32[]{:S(2)}, u32[]{:S(2)}) collective-permute-start(bf16[544,2048]{1,0:T(8,128)(2,1)} %get-tuple-element.247), channel_id=1, source_target_pairs={{0,8},{1,17},{8,0},{9,25},{16,24},{17,1},{24,16},{25,9},{2,10},{3,... | collective-permute-start | bytes 6684680 | tf_op jit(solution)/shard_map/ppermute | solution.py:121
  405.2 77.2 %reduce-scatter.11.cloned.1.call-start = ((), (), s32[]{:S(2)}) async-start(), calls=%async_computation.8 | async-start | bytes 1310720 | tf_op jit(solution)/shard_map/reduce_scatter | solution.py:400
  408.8 41.9 %collective-permute-start.52 = (bf16[528,2048]{1,0:T(8,128)(2,1)}, bf16[528,2048]{1,0:T(8,128)(2,1)}, u32[]{:S(2)}, u32[]{:S(2)}) collective-permute-start(bf16[528,2048]{1,0:T(8,128)(2,1)} %get-tuple-element.255), channel_id=1, source_target_pairs={{0,8},{1,17},{8,0},{9,25},{16,24},{17,1},{24,16},{25,9},{2,10},{3,... | collective-permute-start | bytes 6488072 | tf_op jit(solution)/shard_map/ppermute | solution.py:121
  448.3 71.1 %reduce-scatter.13.cloned.1.call-start = ((), (), s32[]{:S(2)}) async-start(), calls=%async_computation.9 | async-start | bytes 1310720 | tf_op jit(solution)/shard_map/reduce_scatter | solution.py:400
  448.6 48.7 %collective-permute-start.51 = (bf16[592,1792]{1,0:T(8,128)(2,1)}, bf16[592,1792]{1,0:T(8,128)(2,1)}, u32[]{:S(2)}, u32[]{:S(2)}) collective-permute-start(bf16[592,1792]{1,0:T(8,128)(2,1)} %get-tuple-element.254), channel_id=1, source_target_pairs={{0,8},{1,17},{8,0},{9,25},{16,24},{17,1},{24,16},{25,9},{2,10},{3,... | collective-permute-start | bytes 6365192 | tf_op jit(solution)/shard_map/ppermute | solution.py:121
  482.2 74.3 %reduce-scatter.17.cloned.1.call-start = ((), (), s32[]{:S(2)}) async-start(), calls=%async_computation.11 | async-start | bytes 1310720 | tf_op jit(solution)/shard_map/reduce_scatter | solution.py:400
  505.5 61.8 %reduce-scatter.15.cloned.1.call-start = ((), (), s32[]{:S(2)}) async-start(), calls=%async_computation.10 | async-start | bytes 1146880 | tf_op jit(solution)/shard_map/reduce_scatter | solution.py:400
  (138 other events, 1402.8 us)
Sparse Core Ops, SparseCore 0:
  10.5 51.8 all-gather.9
  64.6 41.3 all-gather.11
  108.2 27.9 all-gather.13
  138.2 28.5 all-gather.15
  366.4 25.1 reduce-scatter.6
  405.3 25.1 reduce-scatter.8
  448.4 25.1 reduce-scatter.10
  482.3 25.1 reduce-scatter.12
  509.8 25.7 reduce-scatter.16
  538.4 23.7 reduce-scatter.14

commit v7 on v6

--- a/solution.py
+++ b/solution.py
@@ -1189,7 +1189,7 @@
 
     low = Packed([low_second])
     down_two = Sums(Factor(low, 0, second_forward, 1, 0, seconddown.shape[1]))
-    rounds.step([down_two], margin=80)
+    rounds.step([down_two], margin=40)
     *packed, first_packed_a, first_packed_b = down_back_step(
         order, place, gathers[5], 0, low_second, second_expanded, first_packed
     )
@@ -1211,7 +1211,7 @@
     conv_forward, attend_forward = Packed(held[:1]), Packed(held[1:])
     up_two = Sums(Factor(second_forward, 0, backward, 0, 0, secondup.shape[1]))
     order.wait(*first_forward.all)
-    rounds.step([up_two], margin=64)
+    rounds.step([up_two], margin=32)
     low = Packed([low_conv])
     order.wait(*conv_forward.all, *attend_forward.all)
     *packed, inner_gain, inner_shift, taps_grad = conv_back_step(
@@ -1236,7 +1236,7 @@
         Factor(conv_forward, 1, low, 0, 0, pointwise.shape[1], relative=False),
         Factor(attend_forward, 1, Packed([low_attention]), 0, 0, merger.shape[1], relative=False),
     )
-    rounds.step([conv], [down_two], margin=48)
+    rounds.step([conv], [down_two], margin=24)
     packed = attend_back_step(
         order, place, gathers[2], 1, low_attention, turned, totals, cosine, sine, down, across
     )
@@ -1260,12 +1260,12 @@
     packed = down_back_step(order, place, gathers[1], 0, low_first, first_expanded)
     backward = Packed(packed)
     down_one = Sums(Factor(low, 0, first_forward, 1, 0, firstdown.shape[1]))
-    (down_two_mine,) = rounds.step([down_one], [up_two], [down_two], margin=32)
+    (down_two_mine,) = rounds.step([down_one], [up_two], [down_two], margin=16)
     frames_grad, low_start, first_gain, first_shift = into_norm_step(
         order, place, gathers[0], 0, 0, 0, 1.0, packed, start_sum, grad_first, gain_rows
     )
     up_one = Sums(Factor(first_forward, 0, backward, 0, 0, firstup.shape[1]))
-    (up_two_mine,) = rounds.step([up_one], [conv], [up_two], margin=16)
+    (up_two_mine,) = rounds.step([up_one], [conv], [up_two], margin=8)
     vectors = jnp.concatenate(
         [
             first_gain,

time: 600 us -> 596 us (level)
    unnamed x179 -> x193, local copies, waits for them, and re-layouts: 37.5 us -> 39.2 us
where the time goes in v7:
time: 596 us; the launch traced here: 592 us
  Pallas kernels  235 us (39%)
  waiting for transfers between devices  217 us (36%)
  local copies, waits for them, and re-layouts  52.3 us (9%)
  starting transfers between devices  46.6 us (8%)
  blocking collectives  20.1 us (3%)
  between operations  16.1 us (3%)
    pallas_call x44, Pallas kernels, call(): pl.pallas_call(body, out_shape=[*out_shape, *[jax.ShapeDtypeStruct(x.shap...  235 us
    ppermute x36, waiting for transfers between devices, swap_pairs(): return lax.ppermute(value, ('dp', 'core'), pairs)  178 us
    unnamed x193, local copies, waits for them, and re-layouts  39.2 us
    ppermute x36, starting transfers between devices, swap_pairs(): return lax.ppermute(value, ('dp', 'core'), pairs)  37.9 us
    all_gather x4, waiting for transfers between devices, __init__(): self.gathered = lax.all_gather(mine, ('z', 'core'), axis=0, tiled=False)  33.5 us
    all_gather x1, blocking collectives, gather_small(): full = lax.all_gather(packed, ('z', 'core'), axis=0, tiled=False)  20.1 us
  transfers between devices with their start and end apart: 78, of which 24 were waited for; matrix products, arithmetic and copies ran while one was open for 4% of the time, Pallas kernels for 37%

profile of v7, /device:TPU:0, one launch (start us, length us, event | category | flops | bytes accessed | tf_op | source)
XLA Modules:
  0.0 591.7 jit_solution(3880737194524541214)
XLA Ops:
  21.6 20.1 %all-gather = bf16[1024,128]{1,0:T(8,128)(2,1)S(1)} all-gather(bf16[128,128]{1,0:T(8,128)(2,1)S(1)} %fusion.9), channel_id=2, replica_groups=mesh['dp'=4,'z'=4,'core'=2] {'z','core'}, dimensions={0}, use_global_device_ids=true | all-gather | bytes 294912 | tf_op jit(solution)/shard_map/all_gather | solution.py:479
  43.7 18.8 %all-gather.10.cloned.1.call-done = bf16[1024,2048]{1,0:T(8,128)(2,1)} async-done(((bf16[128,2048]{1,0:T(8,128)(2,1)}), bf16[1024,2048]{1,0:T(8,128)(2,1)}) %all-gather.10.cloned.1.call-update) | async-done | bytes 4194320 | tf_op jit(solution)/shard_map/all_gather | solution.py:449
  72.6 14.6 %collective-permute-done.1.refs_1_.refs_7_.refs_9_ = bf16[808,1024]{1,0:T(8,128)(2,1)} collective-permute-done((bf16[808,1024]{1,0:T(8,128)(2,1)}, bf16[808,1024]{1,0:T(8,128)(2,1)}, u32[]{:S(2)}, u32[]{:S(2)}) %collective-permute-start.1) | collective-permute-done | bytes 1654816 | tf_op jit(solution)/shard_map/ppermute | solution.py:121
  91.3 14.7 %all-gather.12.cloned.1.call-done = bf16[1024,1792]{1,0:T(8,128)(2,1)} async-done(((bf16[128,1792]{1,0:T(8,128)(2,1)}), bf16[1024,1792]{1,0:T(8,128)(2,1)}) %all-gather.12.cloned.1.call-update) | async-done | bytes 3670032 | tf_op jit(solution)/shard_map/all_gather | solution.py:449
  123.8 8.9 %shard_map.272 = (bf16[4,256,1024]{2,1,0:T(8,128)(2,1)}, bf16[5,128,1024]{2,1,0:T(8,128)(2,1)}, bf16[5,128,1024]{2,1,0:T(8,128)(2,1)}, bf16[256,1024]{1,0:T(8,128)(2,1)S(1)}) custom-call(s32[3]{0:T(128)S(1)} %pad_add_fusion.refs_0_, f32[256,1024]{1,0:T(8,128)} %convolution_add_fusion.refs_1_, ...), custom_call_target="tpu_custom_call", output_to_operand_aliasing={{3}: (11, {})} | custom-call | tf_op jit(solution)/shard_map/pallas_call | solution.py:87
  132.7 10.8 %collective-permute-done.9.refs_1_.refs_11_.refs_6_.refs_9_ = bf16[792,1024]{1,0:T(8,128)(2,1)} collective-permute-done((bf16[792,1024]{1,0:T(8,128)(2,1)}, bf16[792,1024]{1,0:T(8,128)(2,1)}, u32[]{:S(2)}, u32[]{:S(2)}) %collective-permute-start.9) | collective-permute-done | bytes 1622048 | tf_op jit(solution)/shard_map/ppermute | solution.py:121
  153.3 13.5 %collective-permute-done.11.refs_13_.refs_8_.refs_11_ = bf16[384,1024]{1,0:T(8,128)(2,1)S(1)} collective-permute-done((bf16[384,1024]{1,0:T(8,128)(2,1)}, bf16[384,1024]{1,0:T(8,128)(2,1)S(1)}, u32[]{:S(2)}, u32[]{:S(2)}) %collective-permute-start.11) | collective-permute-done | bytes 786464 | tf_op jit(solution)/shard_map/ppermute | solution.py:121
  207.4 9.0 %shard_map.281 = (f32[256,1024]{1,0:T(8,128)}, bf16[256,2048]{1,0:T(8,128)(2,1)}, f32[256,1024]{1,0:T(8,128)}, bf16[2,256,1024]{2,1,0:T(8,128)(2,1)}, bf16[256,1024]{1,0:T(8,128)(2,1)S(1)}) custom-call(s32[3]{0:T(128)S(1)} %pad_add_fusion.refs_0_, f32[256,1024]{1,0:T(8,128)} %get-tuple-element.175.refs_1_, ...), custom_call_target="tpu_custom_call", output_to_operand_aliasing={{4}: (20, {})} | custom-call | tf_op jit(solution)/shard_map/pallas_call | solution.py:87
  219.4 10.9 %collective-permute-done.23.refs_12_.refs_8_ = bf16[384,1024]{1,0:T(8,128)(2,1)S(1)} collective-permute-done((bf16[384,1024]{1,0:T(8,128)(2,1)S(1)}, bf16[384,1024]{1,0:T(8,128)(2,1)S(1)}, u32[]{:S(2)}, u32[]{:S(2)}) %collective-permute-start.23) | collective-permute-done | bytes 786464 | tf_op jit(solution)/shard_map/ppermute | solution.py:121
  241.9 9.7 %shard_map.284 = (bf16[256,1024]{1,0:T(8,128)(2,1)}, f32[256,1024]{1,0:T(8,128)}, bf16[1,256,1024]{2,1,0:T(8,128)(2,1)S(1)}, f32[1,1024]{1,0:T(1,128)S(1)}, f32[...) custom-call(s32[3]{0:T(128)S(1)} %pad_add_fusion.refs_0_, ...), custom_call_target="tpu_custom_call", output_to_operand_aliasing={{5}: (14, {})} | custom-call | tf_op jit(solution)/shard_map/pallas_call | solution.py:87
  259.9 8.9 %shard_map.286 = (bf16[4,128,1024]{2,1,0:T(8,128)(2,1)}, bf16[4,128,1024]{2,1,0:T(8,128)(2,1)}, bf16[5,128,1024]{2,1,0:T(8,128)(2,1)}, bf16[5,128,1024]{2,1,0:T(8,128)(2,1)}, bf16[256,1024]{1,0:T(8,128)(2,1)S(1)}) custom-call(s32[3]{0:T(128)S(1)} %pad_add_fusion.refs_0_, ...), custom_call_target="tpu_custom_call", output_to_operand_aliasing={{2}: (10, {}), {3}: (11, {}), {4}: (12, {})} | custom-call | tf_op jit(solution)/shard_map/pallas_call | solution.py:87
  270.1 9.2 %shard_map.287 = (f32[256,1024]{1,0:T(8,128)}, bf16[1,256,1024]{2,1,0:T(8,128)(2,1)S(1)}, f32[1,1024]{1,0:T(1,128)S(1)}, f32[1,1024]{1,0:T(1,128)S(1)}, bf16[2,2...) custom-call(s32[3]{0:T(128)S(1)} %pad_add_fusion.refs_0_, ...), custom_call_target="tpu_custom_call", output_to_operand_aliasing={{4}: (13, {}), {5}: (14, {}), {6}: (15, {})} | custom-call | tf_op jit(solution)/shard_map/pallas_call | solution.py:87
  341.0 9.1 %shard_map.294 = (bf16[4,128,1024]{2,1,0:T(8,128)(2,1)}, bf16[4,128,1024]{2,1,0:T(8,128)(2,1)}, bf16[256,1024]{1,0:T(8,128)(2,1)S(1)}) custom-call(s32[3]{0:T(128)S(1)} %pad_add_fusion.refs_0_, bf16[1,256,1024]{2,1,0:T(8,128)(2,1)S(1)} %get-tuple-element.223.refs_1_.refs_9_, ...), custom_call_target="tpu_custom_call", output_to_operand_aliasing={{2}: (14, {})} | custom-call | tf_op jit(solution)/shard_map/pallas_call | solution.py:87
  350.2 9.6 %shard_map.295 = (bf16[528,2048]{1,0:T(8,128)(2,1)}, bf16[512,1024]{1,0:T(8,128)(2,1)}, bf16[512,1024]{1,0:T(8,128)(2,1)}, bf16[256,1024]{1,0:T(8,128)(2,1)S(1)}) custom-call(s32[3]{0:T(128)S(1)} %pad_add_fusion.refs_0_, bf16[1,256,1024]{2,1,0:T(8,128)(2,1)S(1)} %get-tuple-element.223.refs_1_.refs_9_, ...), custom_call_target="tpu_custom_call", output_to_operand_aliasing={{3}: (20, {})} | custom-call | tf_op jit(solution)/shard_map/pallas_call | solution.py:87
  365.5 9.2 %shard_map.296 = (f32[256,1024]{1,0:T(8,128)}, bf16[1,256,1024]{2,1,0:T(8,128)(2,1)S(1)}, f32[1,1024]{1,0:T(1,128)S(1)}, f32[1,1024]{1,0:T(1,128)S(1)}, bf16[256,1024]{1,0:T(8,128)(2,1)S(1)}) custom-call(s32[3]{0:T(128)S(1)} %pad_add_fusion.refs_0_, f32[256,1024]{1,0:T(8,128)} %convolution_add_fusion.refs_1_, ...), custom_call_target="tpu_custom_call", output_to_operand_aliasing={{4}: (13, {})} | custom-call | tf_op jit(solution)/shard_map/pallas_call | solution.py:87
  374.7 14.6 %collective-permute-done.49.refs_31_ = bf16[512,1024]{1,0:T(8,128)(2,1)S(1)} collective-permute-done((bf16[512,1024]{1,0:T(8,128)(2,1)}, bf16[512,1024]{1,0:T(8,128)(2,1)S(1)}, u32[]{:S(2)}, u32[]{:S(2)}) %collective-permute-start.49) | collective-permute-done | bytes 1048608 | tf_op jit(solution)/shard_map/ppermute | solution.py:121
  390.3 9.2 %shard_map.297 = (bf16[520,2048]{1,0:T(8,128)(2,1)}, bf16[512,1024]{1,0:T(8,128)(2,1)}, bf16[512,1024]{1,0:T(8,128)(2,1)}, bf16[256,1024]{1,0:T(8,128)(2,1)S(1)}) custom-call(s32[3]{0:T(128)S(1)} %pad_add_fusion.refs_0_, bf16[5,128,1024]{2,1,0:T(8,128)(2,1)} %get-tuple-element.205.refs_9_.refs_3_.refs_1_.refs_11_, ...), custom_call_target="tpu_custom_call", output_to_operand_aliasing={{3}: (32, {})} | custom-call | tf_op jit(solution)/shard_map/pallas_call | solution.py:87
  406.2 23.3 %collective-permute-done.50.refs_27_ = bf16[512,1024]{1,0:T(8,128)(2,1)S(1)} collective-permute-done((bf16[512,1024]{1,0:T(8,128)(2,1)}, bf16[512,1024]{1,0:T(8,128)(2,1)S(1)}, u32[]{:S(2)}, u32[]{:S(2)}) %collective-permute-start.50) | collective-permute-done | bytes 1048608 | tf_op jit(solution)/shard_map/ppermute | solution.py:121
  431.4 11.3 %shard_map.298 = (bf16[592,1792]{1,0:T(8,128)(2,1)}, bf16[512,1024]{1,0:T(8,128)(2,1)}, bf16[512,1024]{1,0:T(8,128)(2,1)}, bf16[256,1024]{1,0:T(8,128)(2,1)S(1)}) custom-call(s32[3]{0:T(128)S(1)} %pad_add_fusion.refs_0_, bf16[2,256,1024]{2,1,0:T(8,128)(2,1)} %get-tuple-element.204.refs_17_.refs_9_.refs_1_, ...), custom_call_target="tpu_custom_call", output_to_operand_aliasing={{3}: (29, {})} | custom-call | tf_op jit(solution)/shard_map/pallas_call | solution.py:87
  445.2 24.2 %collective-permute-done.53.refs_13_ = bf16[512,1024]{1,0:T(8,128)(2,1)S(1)} collective-permute-done((bf16[512,1024]{1,0:T(8,128)(2,1)}, bf16[512,1024]{1,0:T(8,128)(2,1)S(1)}, u32[]{:S(2)}, u32[]{:S(2)}) %collective-permute-start.53) | collective-permute-done | bytes 1048608 | tf_op jit(solution)/shard_map/ppermute | solution.py:121
  476.7 15.0 %collective-permute-done.54.refs_19_ = bf16[512,1024]{1,0:T(8,128)(2,1)S(1)} collective-permute-done((bf16[512,1024]{1,0:T(8,128)(2,1)}, bf16[512,1024]{1,0:T(8,128)(2,1)S(1)}, u32[]{:S(2)}, u32[]{:S(2)}) %collective-permute-start.54) | collective-permute-done | bytes 1048608 | tf_op jit(solution)/shard_map/ppermute | solution.py:121
  500.6 13.1 %collective-permute-done.55.refs_10_ = bf16[512,896]{1,0:T(8,128)(2,1)S(1)} collective-permute-done((bf16[512,896]{1,0:T(8,128)(2,1)}, bf16[512,896]{1,0:T(8,128)(2,1)S(1)}, u32[]{:S(2)}, u32[]{:S(2)}) %collective-permute-start.55) | collective-permute-done | bytes 917536 | tf_op jit(solution)/shard_map/ppermute | solution.py:121
  523.0 12.2 %collective-permute-done.59.refs_2_ = bf16[128,2048]{1,0:T(8,128)(2,1)S(1)} collective-permute-done((bf16[128,2048]{1,0:T(8,128)(2,1)S(1)}, bf16[128,2048]{1,0:T(8,128)(2,1)S(1)}, u32[]{:S(2)}, u32[]{:S(2)}) %collective-permute-start.59) | collective-permute-done | bytes 524320 | tf_op jit(solution)/shard_map/ppermute | solution.py:121
  537.2 9.2 %collective-permute-done.56.refs_2_ = bf16[128,2048]{1,0:T(8,128)(2,1)S(1)} collective-permute-done((bf16[128,2048]{1,0:T(8,128)(2,1)S(1)}, bf16[128,2048]{1,0:T(8,128)(2,1)S(1)}, u32[]{:S(2)}, u32[]{:S(2)}) %collective-permute-start.56) | collective-permute-done | bytes 524320 | tf_op jit(solution)/shard_map/ppermute | solution.py:121
  (447 shorter events, 266.6 us)
Async XLA Ops:
  7.2 55.2 %all-gather.10.cloned.1.call-start = ((), (), s32[]{:S(2)}) async-start(), calls=%async_computation.12 | async-start | bytes 4718592 | tf_op jit(solution)/shard_map/all_gather | solution.py:449
  10.4 95.7 %all-gather.12.cloned.1.call-start = ((), (), s32[]{:S(2)}) async-start(), calls=%async_computation.13 | async-start | bytes 4128768 | tf_op jit(solution)/shard_map/all_gather | solution.py:449
  11.4 137.6 %all-gather.14.cloned.1.call-start = ((), (), s32[]{:S(2)}) async-start(), calls=%async_computation.14 | async-start | bytes 2359296 | tf_op jit(solution)/shard_map/all_gather | solution.py:449
  20.3 52.2 %collective-permute-start = (bf16[128,23552]{1,0:T(8,128)(2,1)}, bf16[128,23552]{1,0:T(8,128)(2,1)}, u32[]{:S(2)}, u32[]{:S(2)}) collective-permute-start(bf16[128,23552]{1,0:T(8,128)(2,1)} %constant_dynamic-update-slice_fusion), channel_id=1, source_target_pairs={{0,1},{1,0},{2,3},{3,2},{4,5},{5,4},{6,7},{7,6},{8,9},{9,8},{10,11... | collective-permute-start | bytes 18087944 | tf_op jit(solution)/shard_map/ppermute | solution.py:112
  21.5 157.4 %all-gather.16.cloned.1.call-start = ((), (), s32[]{:S(2)}) async-start(), calls=%async_computation.15 | async-start | bytes 2359296 | tf_op jit(solution)/shard_map/all_gather | solution.py:449
  70.2 45.0 %collective-permute-start.5 = (bf16[800,1024]{1,0:T(8,128)(2,1)}, bf16[800,1024]{1,0:T(8,128)(2,1)}, u32[]{:S(2)}, u32[]{:S(2)}) collective-permute-start(bf16[800,1024]{1,0:T(8,128)(2,1)} %get-tuple-element.155), channel_id=1, source_target_pairs={{0,8},{1,17},{8,0},{9,25},{16,24},{17,1},{24,16},{25,9},{2,10},{3,... | collective-permute-start | bytes 4915208 | tf_op jit(solution)/shard_map/ppermute | solution.py:121
  72.5 333.7 %reduce-scatter.7.cloned.1.call-start = ((), (), s32[]{:S(2)}) async-start(), calls=%async_computation.6 | async-start | bytes 1310720 | tf_op jit(solution)/shard_map/reduce_scatter | solution.py:400
  115.2 37.6 %collective-permute-start.6 = (bf16[800,1024]{1,0:T(8,128)(2,1)}, bf16[800,1024]{1,0:T(8,128)(2,1)}, u32[]{:S(2)}, u32[]{:S(2)}) collective-permute-start(bf16[800,1024]{1,0:T(8,128)(2,1)} %collective-permute-done.5.refs_1_.refs_7_.refs_6_), channel_id=1, source_target_pairs={{0,1},{1,0},{2,3},{3,2},{4,5},{5,4},{6,7},{7,6},{8,9},{9,8},{10,11... | collective-permute-start | bytes 4915208 | tf_op jit(solution)/shard_map/ppermute | solution.py:112
  118.3 34.5 %collective-permute-start.7 = (bf16[384,1024]{1,0:T(8,128)(2,1)}, bf16[384,1024]{1,0:T(8,128)(2,1)}, u32[]{:S(2)}, u32[]{:S(2)}) collective-permute-start(bf16[384,1024]{1,0:T(8,128)(2,1)} %get-tuple-element.162), channel_id=1, source_target_pairs={{0,16},{1,9},{8,24},{9,1},{16,0},{17,25},{24,8},{25,17},{2,18},{3,... | collective-permute-start | bytes 2359304 | tf_op jit(solution)/shard_map/ppermute | solution.py:121
  152.1 33.5 %collective-permute-start.17 = (bf16[776,1024]{1,0:T(8,128)(2,1)}, bf16[776,1024]{1,0:T(8,128)(2,1)}, u32[]{:S(2)}, u32[]{:S(2)}) collective-permute-start(bf16[776,1024]{1,0:T(8,128)(2,1)} %get-tuple-element.177), channel_id=1, source_target_pairs={{0,8},{1,17},{8,0},{9,25},{16,24},{17,1},{24,16},{25,9},{2,10},{3,... | collective-permute-start | bytes 4767752 | tf_op jit(solution)/shard_map/ppermute | solution.py:121
  152.8 34.6 %collective-permute-start.10 = (bf16[792,1024]{1,0:T(8,128)(2,1)}, bf16[792,1024]{1,0:T(8,128)(2,1)}, u32[]{:S(2)}, u32[]{:S(2)}) collective-permute-start(bf16[792,1024]{1,0:T(8,128)(2,1)} %collective-permute-done.9.refs_1_.refs_11_.refs_6_.refs_9_), channel_id=1, source_target_pairs={{0,1},{1,0},{2,3},{3,2},{4,5},{5,4},{6,7},{7,6},{8,9},{9,8},{10,11... | collective-permute-start | bytes 4866056 | tf_op jit(solution)/shard_map/ppermute | solution.py:112
  182.0 34.5 %collective-permute-start.21 = (bf16[768,1024]{1,0:T(8,128)(2,1)}, bf16[768,1024]{1,0:T(8,128)(2,1)}, u32[]{:S(2)}, u32[]{:S(2)}) collective-permute-start(bf16[768,1024]{1,0:T(8,128)(2,1)} %get-tuple-element.182), channel_id=1, source_target_pairs={{0,8},{1,17},{8,0},{9,25},{16,24},{17,1},{24,16},{25,9},{2,10},{3,... | collective-permute-start | bytes 4718600 | tf_op jit(solution)/shard_map/ppermute | solution.py:121
  185.7 44.7 %collective-permute-start.18 = (bf16[776,1024]{1,0:T(8,128)(2,1)}, bf16[776,1024]{1,0:T(8,128)(2,1)}, u32[]{:S(2)}, u32[]{:S(2)}) collective-permute-start(bf16[776,1024]{1,0:T(8,128)(2,1)} %collective-permute-done.17.refs_1_.refs_7_.refs_9_), channel_id=1, source_target_pairs={{0,1},{1,0},{2,3},{3,2},{4,5},{5,4},{6,7},{7,6},{8,9},{9,8},{10,11... | collective-permute-start | bytes 4767752 | tf_op jit(solution)/shard_map/ppermute | solution.py:112
  269.8 39.7 %collective-permute-start.38 = (bf16[552,2048]{1,0:T(8,128)(2,1)}, bf16[552,2048]{1,0:T(8,128)(2,1)}, u32[]{:S(2)}, u32[]{:S(2)}) collective-permute-start(bf16[552,2048]{1,0:T(8,128)(2,1)} %get-tuple-element.216), channel_id=1, source_target_pairs={{0,8},{1,17},{8,0},{9,25},{16,24},{17,1},{24,16},{25,9},{2,10},{3,... | collective-permute-start | bytes 6782984 | tf_op jit(solution)/shard_map/ppermute | solution.py:121
  287.2 63.0 %collective-permute-start.42 = (bf16[544,2048]{1,0:T(8,128)(2,1)}, bf16[544,2048]{1,0:T(8,128)(2,1)}, u32[]{:S(2)}, u32[]{:S(2)}) collective-permute-start(bf16[544,2048]{1,0:T(8,128)(2,1)} %get-tuple-element.228), channel_id=1, source_target_pairs={{0,8},{1,17},{8,0},{9,25},{16,24},{17,1},{24,16},{25,9},{2,10},{3,... | collective-permute-start | bytes 6684680 | tf_op jit(solution)/shard_map/ppermute | solution.py:121
  338.6 36.1 %collective-permute-start.46 = (bf16[536,2048]{1,0:T(8,128)(2,1)}, bf16[536,2048]{1,0:T(8,128)(2,1)}, u32[]{:S(2)}, u32[]{:S(2)}) collective-permute-start(bf16[536,2048]{1,0:T(8,128)(2,1)} %get-tuple-element.248), channel_id=1, source_target_pairs={{0,8},{1,17},{8,0},{9,25},{16,24},{17,1},{24,16},{25,9},{2,10},{3,... | collective-permute-start | bytes 6586376 | tf_op jit(solution)/shard_map/ppermute | solution.py:121
  360.6 84.6 %reduce-scatter.9.cloned.1.call-start = ((), (), s32[]{:S(2)}) async-start(), calls=%async_computation.7 | async-start | bytes 1310720 | tf_op jit(solution)/shard_map/reduce_scatter | solution.py:400
  363.8 65.7 %collective-permute-start.45 = (bf16[528,2048]{1,0:T(8,128)(2,1)}, bf16[528,2048]{1,0:T(8,128)(2,1)}, u32[]{:S(2)}, u32[]{:S(2)}) collective-permute-start(bf16[528,2048]{1,0:T(8,128)(2,1)} %get-tuple-element.247), channel_id=1, source_target_pairs={{0,8},{1,17},{8,0},{9,25},{16,24},{17,1},{24,16},{25,9},{2,10},{3,... | collective-permute-start | bytes 6488072 | tf_op jit(solution)/shard_map/ppermute | solution.py:121
  399.5 77.2 %reduce-scatter.11.cloned.1.call-start = ((), (), s32[]{:S(2)}) async-start(), calls=%async_computation.8 | async-start | bytes 1310720 | tf_op jit(solution)/shard_map/reduce_scatter | solution.py:400
  403.3 41.9 %collective-permute-start.52 = (bf16[520,2048]{1,0:T(8,128)(2,1)}, bf16[520,2048]{1,0:T(8,128)(2,1)}, u32[]{:S(2)}, u32[]{:S(2)}) collective-permute-start(bf16[520,2048]{1,0:T(8,128)(2,1)} %get-tuple-element.255), channel_id=1, source_target_pairs={{0,8},{1,17},{8,0},{9,25},{16,24},{17,1},{24,16},{25,9},{2,10},{3,... | collective-permute-start | bytes 6389768 | tf_op jit(solution)/shard_map/ppermute | solution.py:121
  442.7 71.0 %reduce-scatter.13.cloned.1.call-start = ((), (), s32[]{:S(2)}) async-start(), calls=%async_computation.9 | async-start | bytes 1310720 | tf_op jit(solution)/shard_map/reduce_scatter | solution.py:400
  443.1 48.6 %collective-permute-start.51 = (bf16[592,1792]{1,0:T(8,128)(2,1)}, bf16[592,1792]{1,0:T(8,128)(2,1)}, u32[]{:S(2)}, u32[]{:S(2)}) collective-permute-start(bf16[592,1792]{1,0:T(8,128)(2,1)} %get-tuple-element.254), channel_id=1, source_target_pairs={{0,8},{1,17},{8,0},{9,25},{16,24},{17,1},{24,16},{25,9},{2,10},{3,... | collective-permute-start | bytes 6365192 | tf_op jit(solution)/shard_map/ppermute | solution.py:121
  476.6 75.3 %reduce-scatter.17.cloned.1.call-start = ((), (), s32[]{:S(2)}) async-start(), calls=%async_computation.11 | async-start | bytes 1310720 | tf_op jit(solution)/shard_map/reduce_scatter | solution.py:400
  500.0 63.2 %reduce-scatter.15.cloned.1.call-start = ((), (), s32[]{:S(2)}) async-start(), calls=%async_computation.10 | async-start | bytes 1146880 | tf_op jit(solution)/shard_map/reduce_scatter | solution.py:400
  (145 other events, 1438.4 us)
Sparse Core Ops, SparseCore 0:
  10.5 51.8 all-gather.9
  64.6 41.3 all-gather.11
  108.2 27.9 all-gather.13
  138.2 28.5 all-gather.15
  360.7 25.1 reduce-scatter.6
  399.6 25.1 reduce-scatter.8
  442.8 25.0 reduce-scatter.10
  476.7 25.0 reduce-scatter.12
  504.1 25.7 reduce-scatter.16
  532.8 23.7 reduce-scatter.14
